TPU v7x, 128 devices: a whole 4x4x4 slice. The times are simulated.
128 devices in a mesh: dp: 4 (over x), fsdp: 32 (over z, y, core).
Axes of the slice: x: 4, y: 4, z: 4, core: 2. Of those that a mesh axis runs over, the one named last changes fastest.
Arguments:
- grad_parts: bfloat16 [4, 6144, 4096], P('dp', 'fsdp'), may hold values from -6 to 6
- weights: float32 [6144, 4096], P('fsdp', 'dp'), may hold values from -6 to 6
- moment_one: float32 [6144, 4096], P('fsdp', 'dp'), may hold values from -0.75 to 0.75
- moment_two: float32 [6144, 4096], P('fsdp', 'dp'), may hold values from 0.002 to 0.2
- left_basis: bfloat16 [6144, 6144], P('fsdp'), may hold values from -0.078125 to 0.078125
- right_basis: bfloat16 [4096, 4096], P(('dp', 'fsdp')), may hold values from -0.09375 to 0.09375
Outputs:
- new_weights: float32 [6144, 4096], P('fsdp', 'dp')
- new_one: float32 [6144, 4096], P('fsdp', 'dp')
- new_two: float32 [6144, 4096], P('fsdp', 'dp')
- update: float32 [6144, 4096], P('fsdp', 'dp')
All inputs are finite; a program needn't handle non-finite values.
Results may differ from a plain program's by a relative error of at most 0.034.
Values may be sent and summed in bfloat16 or wider, within the bound.
No kernel may reach another device: no remote copies, remote signals or barrier semaphores. Data moves between devices by JAX's collectives and lax.ppermute only.
A program may use at most 128 MiB of HBM per device.

v0:
```python
import jax
import jax.numpy as jnp
from jax import lax
from jax.sharding import PartitionSpec as P

beta_first = 0.95
beta_second = 0.95
bias_first = 1.0 - 0.95**10
bias_second = 1.0 - 0.95**10
epsilon = 1e-08
learn_rate = 0.02
weight_decay = 0.1


def per_device(grad_parts, weights, moment_one, moment_two, left_basis, right_basis):
    replica_part = grad_parts[0].astype(jnp.float32)
    gradient = lax.psum_scatter(
        replica_part.astype(jnp.bfloat16), "dp", scatter_dimension=1, tiled=True
    )
    whole_term = lax.dot_general(
        left_basis, gradient, (((0,), (0,)), ((), ())), preferred_element_type=jnp.float32
    )
    rotated_left = lax.psum_scatter(
        whole_term.astype(jnp.bfloat16), "fsdp", scatter_dimension=0, tiled=True
    )
    basis_block = lax.all_gather(right_basis, "fsdp", axis=0, tiled=True)
    partial_sum = jnp.dot(rotated_left, basis_block, preferred_element_type=jnp.float32)
    rotated = lax.psum_scatter(
        partial_sum.astype(jnp.bfloat16), "dp", scatter_dimension=1, tiled=True
    ).astype(jnp.float32)
    new_one = beta_first * moment_one + (1.0 - beta_first) * rotated
    new_two = beta_second * moment_two + (1.0 - beta_second) * rotated * rotated
    normed = (new_one / bias_first / (jnp.sqrt(new_two / bias_second) + epsilon)).astype(
        jnp.bfloat16
    )
    back_left = jnp.dot(
        left_basis,
        lax.all_gather(normed, "fsdp", axis=0, tiled=True),
        preferred_element_type=jnp.float32,
    ).astype(jnp.bfloat16)
    full_rows = lax.all_gather(back_left, "dp", axis=1, tiled=True)
    update = lax.dot_general(
        full_rows, basis_block, (((1,), (1,)), ((), ())), preferred_element_type=jnp.float32
    )
    new_weights = weights - learn_rate * (update + weight_decay * weights)
    return (new_weights, new_one, new_two, update)


def solution(mesh):
    return jax.shard_map(
        per_device,
        mesh=mesh,
        in_specs=(
            P("dp", "fsdp", None),
            P("fsdp", "dp"),
            P("fsdp", "dp"),
            P("fsdp", "dp"),
            P("fsdp", None),
            P(("dp", "fsdp"), None),
        ),
        out_specs=(P("fsdp", "dp"), P("fsdp", "dp"), P("fsdp", "dp"), P("fsdp", "dp")),
        check_vma=False,
    )
```

profile of v0, /device:TPU:1, one launch (start us, length us, event | category | flops | bytes accessed | tf_op | source)
XLA Modules:
  0.0 325.7 jit_solution(2236229464674896910)
XLA Ops:
  8.0 0.0 copy-start
  8.0 0.0 reduce-scatter.4.cloned.1.call-start
  8.1 0.7 reduce-scatter.4.cloned.1.call-update
  8.7 0.0 all-gather.4.cloned.1.call-start
  8.8 0.5 all-gather.4.cloned.1.call-update
  9.3 0.0 reduce-scatter.6.cloned.1.call-start
  9.4 29.8 %reduce-scatter.4.cloned.1.call-done = bf16[192,1024]{1,0:T(8,128)(2,1)} async-done(((bf16[192,4096]{1,0:T(8,128)(2,1)}), bf16[192,1024]{1,0:T(8,128)(2,1)}) %reduce-scatter.4.cloned.1.call-update) | async-done | bytes 393232 | tf_op jit(solution)/shard_map/reduce_scatter | solution.py:17
  39.2 0.0 copy-done
  39.2 7.6 %convolution_convert_fusion = bf16[6144,1024]{1,0:T(8,128)(2,1)} fusion(bf16[192,6144]{1,0:T(8,128)(2,1)S(1)} %copy-done, bf16[192,1024]{1,0:T(8,128)(2,1)} %reduce-scatter.4.cloned.1.call-done), kind=kOutput, calls=%fused_computation | convolution fusion | flops 2422210560 | bytes 15335424 | tf_op jit(solution)/shard_map/dot_general | solution.py:20
  46.7 0.0 reduce-scatter.6.cloned.1.call-update
  46.8 0.0 copy-start.2
  46.8 0.0 reduce-scatter.8.cloned.1.call-start
  46.8 21.3 %all-gather.4.cloned.1.call-done = bf16[1024,4096]{1,0:T(8,128)(2,1)} async-done(((bf16[32,4096]{1,0:T(8,128)(2,1)}), bf16[1024,4096]{1,0:T(8,128)(2,1)}) %all-gather.4.cloned.1.call-update) | async-done | bytes 8388624 | tf_op jit(solution)/shard_map/all_gather | solution.py:26
  68.1 105.8 %reduce-scatter.6.cloned.1.call-done = bf16[192,1024]{1,0:T(8,128)(2,1)} async-done(((bf16[6144,1024]{1,0:T(8,128)(2,1)}), bf16[192,1024]{1,0:T(8,128)(2,1)}) %reduce-scatter.6.cloned.1.call-update) | async-done | bytes 393232 | tf_op jit(solution)/shard_map/reduce_scatter | solution.py:23
  173.8 6.5 %convolution_convert_fusion.1 = bf16[192,4096]{1,0:T(8,128)(2,1)} fusion(bf16[192,1024]{1,0:T(8,128)(2,1)} %reduce-scatter.6.cloned.1.call-done, bf16[1024,4096]{1,0:T(8,128)(2,1)} %all-gather.4.cloned.1.call-done), kind=kOutput, calls=%fused_computation.1 | convolution fusion | flops 1611399168 | bytes 10354688 | tf_op jit(solution)/shard_map/dot_general | solution.py:27
  180.3 0.0 reduce-scatter.8.cloned.1.call-update
  180.4 0.0 all-gather.6.cloned.1.call-start
  180.4 25.3 %reduce-scatter.8.cloned.1.call-done = bf16[192,1024]{1,0:T(8,128)(2,1)} async-done(((bf16[192,4096]{1,0:T(8,128)(2,1)}), bf16[192,1024]{1,0:T(8,128)(2,1)}) %reduce-scatter.8.cloned.1.call-update) | async-done | bytes 393232 | tf_op jit(solution)/shard_map/reduce_scatter | solution.py:28
  205.7 0.0 copy-done.2
  205.7 2.8 divide_convert_fusion
  208.6 0.0 all-gather.6.cloned.1.call-update
  208.6 0.0 copy-start.1
  208.6 0.0 all-gather.8.cloned.1.call-start
  208.7 64.3 %all-gather.6.cloned.1.call-done = bf16[6144,1024]{1,0:T(8,128)(2,1)} async-done(((bf16[192,1024]{1,0:T(8,128)(2,1)}), bf16[6144,1024]{1,0:T(8,128)(2,1)}) %all-gather.6.cloned.1.call-update) | async-done | bytes 12582928 | tf_op jit(solution)/shard_map/all_gather | solution.py:38
  272.9 7.3 %fusion = bf16[192,1024]{0,1:T(8,128)(2,1)} fusion(bf16[6144,1024]{1,0:T(8,128)(2,1)} %all-gather.6.cloned.1.call-done, bf16[192,6144]{1,0:T(8,128)(2,1)S(1)} %copy-done), kind=kOutput, calls=%fused_computation.3 | convolution fusion | flops 2416115712 | bytes 15335424 | tf_op jit(solution)/shard_map/dot_general | solution.py:36
  280.2 0.0 all-gather.8.cloned.1.call-update
  280.2 30.0 %all-gather.8.cloned.1.call-done = bf16[192,4096]{0,1:T(8,128)(2,1)} async-done(((bf16[192,1024]{0,1:T(8,128)(2,1)}), bf16[192,4096]{0,1:T(8,128)(2,1)}) %all-gather.8.cloned.1.call-update) | async-done | bytes 1572880 | tf_op jit(solution)/shard_map/all_gather | solution.py:41
  310.2 0.0 copy-done.1
  310.2 8.1 %multiply_subtract_fusion = (f32[192,1024]{1,0:T(8,128)}, f32[192,1024]{1,0:T(8,128)}) fusion(f32[192,1024]{1,0:T(8,128)S(1)} %copy-done.1, bf16[192,4096]{0,1:T(8,128)(2,1)} %all-gather.8.cloned.1.call-done, bf16[1024,4096]{1,0:T(8,128)(2,1)} %all-gather.4.cloned.1.call-done), kind=kOutput, calls=%fused_computation.7 | convolution fusion | flops 1611399168 | bytes 12320768 | tf_op jit(solution)/shard_map/dot_general | solution.py:42
Async XLA Ops:
  8.0 31.2 %copy-start = (bf16[192,6144]{1,0:T(8,128)(2,1)S(1)}, bf16[192,6144]{1,0:T(8,128)(2,1)}, u32[]{:S(2)}) copy-start(bf16[192,6144]{1,0:T(8,128)(2,1)} %param.10) | copy-start | bytes 7077892
  8.0 31.1 %reduce-scatter.4.cloned.1.call-start = ((), (), s32[]{:S(2)}) async-start(), calls=%async_computation.3 | async-start | bytes 1966080 | tf_op jit(solution)/shard_map/reduce_scatter | solution.py:17
  8.7 59.3 %all-gather.4.cloned.1.call-start = ((), (), s32[]{:S(2)}) async-start(), calls=%async_computation.5 | async-start | bytes 8650752 | tf_op jit(solution)/shard_map/all_gather | solution.py:26
  9.3 164.5 %reduce-scatter.6.cloned.1.call-start = ((), (), s32[]{:S(2)}) async-start(), calls=%async_computation.4 | async-start | bytes 12976128 | tf_op jit(solution)/shard_map/reduce_scatter | solution.py:23
  46.8 159.0 %copy-start.2 = (f32[192,1024]{1,0:T(8,128)S(1)}, f32[192,1024]{1,0:T(8,128)}, u32[]{:S(2)}) copy-start(f32[192,1024]{1,0:T(8,128)} %param.8) | copy-start | bytes 2359300
  46.8 158.9 %reduce-scatter.8.cloned.1.call-start = ((), (), s32[]{:S(2)}) async-start(), calls=%async_computation.6 | async-start | bytes 1966080 | tf_op jit(solution)/shard_map/reduce_scatter | solution.py:28
  180.4 92.6 %all-gather.6.cloned.1.call-start = ((), (), s32[]{:S(2)}) async-start(), calls=%async_computation.7 | async-start | bytes 12976128 | tf_op jit(solution)/shard_map/all_gather | solution.py:38
  208.6 101.6 %copy-start.1 = (f32[192,1024]{1,0:T(8,128)S(1)}, f32[192,1024]{1,0:T(8,128)}, u32[]{:S(2)}) copy-start(f32[192,1024]{1,0:T(8,128)} %param.7) | copy-start | bytes 2359300
  208.6 101.6 %all-gather.8.cloned.1.call-start = ((), (), s32[]{:S(2)}) async-start(), calls=%async_computation.8 | async-start | bytes 2621440 | tf_op jit(solution)/shard_map/all_gather | solution.py:41
Sparse Core Ops, SparseCore 0:
  11.3 27.8 reduce-scatter.3
  180.5 25.1 reduce-scatter.7
  280.3 29.8 all-gather.7
Sparse Core Ops, SparseCore 1:
  11.5 56.5 all-gather.3
  71.8 102.0 reduce-scatter.5
  208.7 64.2 all-gather.5
where the time goes:
time: 326 us
  waiting for transfers between devices  278 us (85%)
  matrix products  29.5 us (9%)
  between operations  15.5 us (5%)
    reduce_scatter x1, waiting for transfers between devices, per_device(): lax.psum_scatter(whole_term.astype(jnp.bfloat16), 'fsdp', scatter_dimensi...  106 us
    all_gather x1, waiting for transfers between devices, per_device(): lax.all_gather(normed, 'fsdp', axis=0, tiled=True)  64.3 us
    all_gather x1, waiting for transfers between devices, per_device(): full_rows = lax.all_gather(back_left, 'dp', axis=1, tiled=True)  30 us
    reduce_scatter x1, waiting for transfers between devices, per_device(): lax.psum_scatter(replica_part.astype(jnp.bfloat16), 'dp', scatter_dimensi...  29.8 us
    reduce_scatter x1, waiting for transfers between devices, per_device(): lax.psum_scatter(partial_sum.astype(jnp.bfloat16), 'dp', scatter_dimensio...  25.3 us
    all_gather x1, waiting for transfers between devices, per_device(): basis_block = lax.all_gather(right_basis, 'fsdp', axis=0, tiled=True)  21.3 us
    dot_general x1, matrix products, per_device(): lax.dot_general(full_rows, basis_block, (((1,), (1,)), ((), ())), preferr...  8.12 us
    dot_general x1, matrix products, per_device(): lax.dot_general(left_basis, gradient, (((0,), (0,)), ((), ())), preferred...  7.57 us
  transfers between devices with their start and end apart: 6, of which 6 were waited for; matrix products, arithmetic and copies ran while one was open for 2% of the time, Pallas kernels for 0%

commit v1 on v0

v1 whole, which is shorter than its diff:
```python
import jax
import jax.numpy as jnp
from jax import lax
from jax.sharding import Mesh, PartitionSpec as P

beta_first = 0.95
beta_second = 0.95
bias_first = 1.0 - 0.95**10
bias_second = 1.0 - 0.95**10
epsilon = 1e-08
learn_rate = 0.02
weight_decay = 0.1

RING = 4
bf16 = jnp.bfloat16
f32 = jnp.float32


def shift(value, axis, distance):
    return lax.ppermute(value, axis, [(i, (i + distance) % RING) for i in range(RING)])


def swap(value):
    return lax.ppermute(value, "core", [(0, 1), (1, 0)])


def dot(a, b, contract):
    return lax.dot_general(a, b, ((contract[:1], contract[1:]), ((), ())), preferred_element_type=f32)


def total(pieces):
    return sum(piece.astype(f32) for piece in pieces)


def per_device(grad_parts, weights, moment_one, moment_two, left_basis, right_basis):
    x, z, y, core = (lax.axis_index(name) for name in ("x", "z", "y", "core"))
    first = core == 0
    rows, features = left_basis.shape
    columns = weights.shape[1]
    half = columns // 2
    quarter = half // 2
    spread = features // RING
    chunk = 2 * rows

    def block(value, index, width):
        return lax.dynamic_slice_in_dim(value, (index % RING) * width, width, 1)

    whole = grad_parts[0]
    arrived = [shift(block(whole, x + d, columns), "x", d) for d in (1, 2, 3)]
    gradient = total([block(whole, x, columns), *arrived]).astype(bf16)
    both = jnp.concatenate([gradient, swap(gradient)], axis=0)

    by_core = right_basis.reshape(-1, RING, 2, half)
    mine = lax.dynamic_index_in_dim(by_core, core, 2, keepdims=False).reshape(-1, RING * half)
    others = lax.dynamic_index_in_dim(by_core, 1 - core, 2, keepdims=False).reshape(-1, RING * half)
    others = swap(others)
    pair = jnp.where(first, jnp.concatenate([mine, others]), jnp.concatenate([others, mine]))
    basis = lax.all_gather(pair, ("z", "y"), axis=0, tiled=True)

    by_y = left_basis.reshape(rows, RING, RING, chunk)

    def for_y(d):
        return lax.dynamic_index_in_dim(by_y, (y + d) % RING, 2, keepdims=False).reshape(rows, spread)

    left_y = jnp.concatenate([for_y(0)] + [shift(for_y(d), "y", d) for d in (1, 2, 3)])
    left_z = jnp.concatenate(
        [block(left_basis, z, spread)] + [shift(block(left_basis, z + d, spread), "z", d) for d in (1, 2, 3)]
    )
    left_y_other, left_z_other = swap(left_y), swap(left_z)

    parts = [dot(both, block(basis, x + d, half), (1, 0)).astype(bf16) for d in range(RING)]
    right = total([parts[0]] + [shift(parts[d], "x", d) for d in (1, 2, 3)]).astype(bf16)

    def rotate(value, left, left_other, axis, across, at):
        pieces = [value] + [shift(value, axis, d) for d in (1, 2, 3)]
        own = jnp.concatenate([p[:rows] for p in pieces])
        other = jnp.concatenate([p[rows:] for p in pieces])
        out = (dot(left, own, (0, 0)) + dot(left_other, other, (0, 0))).astype(bf16)

        def part(d):
            return lax.dynamic_slice_in_dim(out, ((at + d) % RING) * chunk, chunk, 0)

        return total([part(0)] + [shift(part(d), across, d) for d in (1, 2, 3)]).astype(bf16)

    turned = jnp.concatenate(
        [
            rotate(right[:, :quarter], left_y, left_y_other, "y", "z", z),
            rotate(right[:, quarter:], left_z, left_z_other, "z", "y", y),
        ],
        axis=1,
    )
    own = lax.dynamic_slice_in_dim(turned, core * rows, rows, 0)
    other = swap(lax.dynamic_slice_in_dim(turned, (1 - core) * rows, rows, 0))
    rotated = jnp.where(
        first, jnp.concatenate([own, other], axis=1), jnp.concatenate([other, own], axis=1)
    ).astype(f32)

    new_one = beta_first * moment_one + (1.0 - beta_first) * rotated
    new_two = beta_second * moment_two + (1.0 - beta_second) * rotated * rotated
    normed = (new_one / bias_first / (jnp.sqrt(new_two / bias_second) + epsilon)).astype(bf16)

    mine = lax.dynamic_slice_in_dim(normed, core * half, half, 1)
    others = swap(lax.dynamic_slice_in_dim(normed, (1 - core) * half, half, 1))
    normed = jnp.where(first, jnp.concatenate([mine, others]), jnp.concatenate([others, mine]))

    def back(value, left, left_other, axis, across, at):
        gathered = jnp.zeros((spread, quarter), bf16)
        for d in range(RING):
            piece = value if d == 0 else shift(value, across, d)
            gathered = lax.dynamic_update_slice_in_dim(gathered, piece, ((at - d) % RING) * chunk, 0)
        own = dot(left, gathered, (1, 0)).astype(bf16).reshape(RING, rows, quarter)
        other = dot(left_other, gathered, (1, 0)).astype(bf16).reshape(RING, rows, quarter)
        pieces = [jnp.concatenate([own[d], other[d]]) for d in range(RING)]
        return total([pieces[0]] + [shift(pieces[d], axis, -d) for d in (1, 2, 3)]).astype(bf16)

    back_left = jnp.concatenate(
        [
            back(normed[:, :quarter], left_y, left_y_other, "y", "z", z),
            back(normed[:, quarter:], left_z, left_z_other, "z", "y", y),
        ],
        axis=1,
    )

    update = dot(back_left, block(basis, x, half), (1, 1))
    for d in (1, 2, 3):
        update = update + dot(shift(back_left, "x", d), block(basis, x - d, half), (1, 1))
    update = update[:rows] + swap(update[rows:])
    new_weights = weights - learn_rate * (update + weight_decay * weights)
    return (new_weights, new_one, new_two, update)


def solution(mesh):
    grid = Mesh(mesh.devices.reshape(RING, RING, RING, 2), ("x", "z", "y", "core"))
    fsdp = ("z", "y", "core")
    placed = P(fsdp, "x")
    return jax.shard_map(
        per_device,
        mesh=grid,
        in_specs=(
            P("x", fsdp, None),
            placed,
            placed,
            placed,
            P(fsdp, None),
            P(("x", *fsdp), None),
        ),
        out_specs=(placed, placed, placed, placed),
        check_vma=False,
    )
```

time: 326 us -> 254 us (0.78); the launches traced: 326 us -> 250 us
  waiting for transfers between devices: 278 us -> 91.6 us
  starting transfers between devices: 0.25 us -> 64.6 us
  local copies, waits for them, and re-layouts: 0.02 us -> 41.4 us
  other arithmetic: 2.84 us -> 11.7 us
  matrix products: 29.5 us -> 25.6 us
    reduce_scatter x3 -> x0, waiting for transfers between devices: 161 us -> none  [the longest x1 106 us: per_device(): lax.psum_scatter(whole_term.astype(jnp.bfloat16), 'fsdp', scatter_dimensi...]
    all_gather x3 -> x1, waiting for transfers between devices: 116 us -> 33.3 us  [per_device(): basis = lax.all_gather(pair, ('z', 'y'), axis=0, tiled=True)]
    ppermute x0 -> x46, starting transfers between devices: none -> 64.6 us  [the longest x39 51.6 us: shift(): lax.ppermute(value, axis, [(i, (i + distance) % RING) for i in range(RING)])]
    ppermute x0 -> x46, waiting for transfers between devices: none -> 58.3 us  [the longest x39 56 us: shift(): lax.ppermute(value, axis, [(i, (i + distance) % RING) for i in range(RING)])]
    dynamic_slice x0 -> x7, local copies, waits for them, and re-layouts: none -> 20.6 us  [the longest x1 15.2 us: for_y(): lax.dynamic_index_in_dim(by_y, (y + d) % RING, 2, keepdims=False)]
    unnamed x6 -> x37, local copies, waits for them, and re-layouts: 0.02 us -> 13.5 us
    reshape x0 -> x2, local copies, waits for them, and re-layouts: none -> 4.62 us  [the longest x1 3.47 us: per_device(): by_y = left_basis.reshape(rows, RING, RING, chunk)]
    dot_general x4 -> x16, matrix products: 29.5 us -> 25.6 us  [dot(): lax.dot_general(a, b, ((contract[:1], contract[1:]), ((), ())), preferred...]
  transfers between devices with their start and end apart: 6 -> 47, of which waited for: 6 -> 17; matrix products, arithmetic and copies ran while one was open for 2% -> 26% of each run, Pallas kernels for 0% -> 0%
where the time goes in v1:
time: 254 us; the launch traced here: 250 us
  waiting for transfers between devices  91.6 us (36%)
  starting transfers between devices  64.6 us (25%)
  local copies, waits for them, and re-layouts  41.4 us (16%)
  matrix products  25.6 us (10%)
  between operations  15.5 us (6%)
  other arithmetic  11.7 us (5%)
    ppermute x39, waiting for transfers between devices, shift(): lax.ppermute(value, axis, [(i, (i + distance) % RING) for i in range(RING)])  56 us
    ppermute x39, starting transfers between devices, shift(): lax.ppermute(value, axis, [(i, (i + distance) % RING) for i in range(RING)])  51.6 us
    all_gather x1, waiting for transfers between devices, per_device(): basis = lax.all_gather(pair, ('z', 'y'), axis=0, tiled=True)  33.3 us
    dot_general x16, matrix products, dot(): lax.dot_general(a, b, ((contract[:1], contract[1:]), ((), ())), preferred...  25.6 us
    dynamic_slice x1, local copies, waits for them, and re-layouts, for_y(): lax.dynamic_index_in_dim(by_y, (y + d) % RING, 2, keepdims=False)  15.2 us
    unnamed x37, local copies, waits for them, and re-layouts  13.5 us
    ppermute x7, starting transfers between devices, swap(): return lax.ppermute(value, 'core', [(0, 1), (1, 0)])  13 us
  transfers between devices with their start and end apart: 47, of which 17 were waited for; matrix products, arithmetic and copies ran while one was open for 26% of the time, Pallas kernels for 0%

profile of v1, /device:TPU:1, one launch (start us, length us, event | category | flops | bytes accessed | tf_op | source)
XLA Modules:
  0.0 250.3 jit_solution(3422146636239419548)
XLA Ops:
  8.4 1.6 dynamic-slice_reduce_fusion.5
  13.4 2.3 dynamic-slice_bitcast_fusion.2
  17.0 2.5 collective-permute-start.4
  21.8 1.6 collective-permute-start.18
  23.5 3.3 %collective-permute-start.19 = (bf16[192,1536]{1,0:T(8,128)(2,1)}, bf16[192,1536]{1,0:T(8,128)(2,1)}, u32[]{:S(2)}, u32[]{:S(2)}) collective-permute-start(bf16[192,1536]{1,0:T(8,128)(2,1)} %get-tuple-element.26), channel_id=1, source_target_pairs={{0,16},{8,24},{16,0},{24,8},{1,17},{9,25},{17,1},{25,9},{2,18},{10... | collective-permute-start | bytes 1769480 | tf_op jit(solution)/shard_map/ppermute | solution.py:20
  26.8 3.5 %reshape.80 = bf16[192,4,4,384]{3,2,1,0:T(4,128)(2,1)S(1)} reshape(bf16[192,6144]{1,0:T(8,128)(2,1)} %param.10) | data formatting | bytes 4718592 | tf_op jit(solution)/shard_map/reshape | solution.py:60
  31.5 15.2 %dynamic-slice_reduce_fusion = (bf16[192,4,384]{2,1,0:T(4,128)(2,1)S(1)}, bf16[192,4,384]{2,1,0:T(4,128)(2,1)}, bf16[192,4,384]{2,1,0:T(4,128)(2,1)S(1)}, bf16[192,4,384]{2,1,0:T(4,128)(2,1)S(1)}) fusion(bf16[192,4,4,384]{3,2,1,0:T(4,128)(2,1)S(1)} %reshape.80, s32[]{:T(128)S(6)} %select_n.270, s32[]{:T(128)S(6)} %select_n.268, s32[]{:T(128)S(6)} %select_n.266, ...), kind=kLoop, calls=%fused_computation.21 | loop fusion | bytes 4718608 | tf_op jit(solution)/shard_map/jit(dynamic_index_in_dim)/dynamic_slice | solution.py:63
  50.9 2.6 %collective-permute-start.1 = (bf16[192,1536]{1,0:T(8,128)(2,1)}, bf16[192,1536]{1,0:T(8,128)(2,1)}, u32[]{:S(2)}, u32[]{:S(2)}) collective-permute-start(bf16[192,1536]{1,0:T(8,128)(2,1)} %bitcast.10), channel_id=1, source_target_pairs={{0,4},{2,6},{4,0},{6,2},{1,5},{3,7},{5,1},{7,3},{8,12},{10,14},{12... | collective-permute-start | bytes 1769480 | tf_op jit(solution)/shard_map/ppermute | solution.py:20
  53.6 1.6 fusion.24
  56.3 2.6 %collective-permute-start.6 = (bf16[192,1024]{1,0:T(8,128)(2,1)S(1)}, bf16[192,1024]{1,0:T(8,128)(2,1)}, u32[]{:S(2)}, u32[]{:S(2)}) collective-permute-start(bf16[192,1024]{1,0:T(8,128)(2,1)S(1)} %fusion.24), channel_id=1, source_target_pairs={{0,1},{1,0},{2,3},{3,2},{4,5},{5,4},{6,7},{7,6},{8,9},{9,8},{10,11... | collective-permute-start | bytes 1179656 | tf_op jit(solution)/shard_map/ppermute | solution.py:24
  61.5 2.0 constant_dynamic-update-slice_fusion.10
  63.4 33.3 %all-gather.2.cloned.1.call-done = bf16[1024,2048]{1,0:T(8,128)(2,1)} async-done(((bf16[64,2048]{1,0:T(8,128)(2,1)}), bf16[1024,2048]{1,0:T(8,128)(2,1)}) %all-gather.2.cloned.1.call-update) | async-done | bytes 4194320 | tf_op jit(solution)/shard_map/all_gather | solution.py:58
  96.7 2.2 convolution_convert_fusion.4
  98.9 1.8 collective-permute-start.10
  100.7 1.9 convolution_convert_fusion.6
  102.7 1.6 convolution_convert_fusion.5
  104.3 1.8 collective-permute-start.9
  106.2 1.9 constant_dynamic-update-slice_fusion.9
  108.1 1.9 constant_dynamic-update-slice_fusion.8
  111.3 3.4 %collective-permute-done.8 = bf16[384,512]{1,0:T(8,128)(2,1)S(1)} collective-permute-done((bf16[384,512]{1,0:T(8,128)(2,1)S(1)}, bf16[384,512]{1,0:T(8,128)(2,1)S(1)}, u32[]{:S(2)}, u32[]{:S(2)}) %collective-permute-start.8) | collective-permute-done | bytes 393248 | tf_op jit(solution)/shard_map/ppermute | solution.py:20
  114.7 6.6 %collective-permute-done.9 = bf16[384,512]{1,0:T(8,128)(2,1)S(1)} collective-permute-done((bf16[384,512]{1,0:T(8,128)(2,1)S(1)}, bf16[384,512]{1,0:T(8,128)(2,1)S(1)}, u32[]{:S(2)}, u32[]{:S(2)}) %collective-permute-start.9) | collective-permute-done | bytes 393248 | tf_op jit(solution)/shard_map/ppermute | solution.py:20
  121.3 1.6 fusion.6
  125.8 8.3 %collective-permute-done.21 = bf16[384,256]{1,0:T(8,128)(2,1)S(1)} collective-permute-done((bf16[384,256]{1,0:T(8,128)(2,1)S(1)}, bf16[384,256]{1,0:T(8,128)(2,1)S(1)}, u32[]{:S(2)}, u32[]{:S(2)}) %collective-permute-start.21) | collective-permute-done | bytes 196640 | tf_op jit(solution)/shard_map/ppermute | solution.py:20
  137.0 2.5 fusion.47
  141.1 2.2 collective-permute-done.11
  143.3 1.7 collective-permute-start.27
  146.5 2.5 fusion
  149.2 2.7 %collective-permute-start.16 = (bf16[384,256]{0,1:T(8,128)(2,1)S(1)}, bf16[384,256]{0,1:T(8,128)(2,1)S(1)}, u32[]{:S(2)}, u32[]{:S(2)}) collective-permute-start(bf16[384,256]{0,1:T(8,128)(2,1)S(1)} %get-tuple-element.35), channel_id=1, source_target_pairs={{0,16},{8,24},{16,0},{24,8},{1,17},{9,25},{17,1},{25,9},{2,18},{10... | collective-permute-start | bytes 589832 | tf_op jit(solution)/shard_map/ppermute | solution.py:20
  152.9 2.0 collective-permute-done.15
  154.9 3.1 %collective-permute-done.16 = bf16[384,256]{0,1:T(8,128)(2,1)S(1)} collective-permute-done((bf16[384,256]{0,1:T(8,128)(2,1)S(1)}, bf16[384,256]{0,1:T(8,128)(2,1)S(1)}, u32[]{:S(2)}, u32[]{:S(2)}) %collective-permute-start.16) | collective-permute-done | bytes 196640 | tf_op jit(solution)/shard_map/ppermute | solution.py:20
  159.3 5.9 %collective-permute-start.28 = (bf16[192,512]{0,1:T(8,128)(2,1)}, bf16[192,512]{0,1:T(8,128)(2,1)S(1)}, u32[]{:S(2)}, u32[]{:S(2)}) collective-permute-start(bf16[192,512]{0,1:T(8,128)(2,1)} %get-tuple-element.57), channel_id=1, source_target_pairs={{0,1},{1,0},{2,3},{3,2},{4,5},{5,4},{6,7},{7,6},{8,9},{9,8},{10,11... | collective-permute-start | bytes 589832 | tf_op jit(solution)/shard_map/ppermute | solution.py:24
  167.8 2.8 %divide_convert_fusion = (bf16[192,1024]{0,1:T(8,128)(2,1)S(1)}, f32[192,1024]{0,1:T(8,128)}, f32[192,1024]{0,1:T(8,128)S(1)}) fusion(bf16[192,512]{0,1:T(8,128)(2,1)S(1)} %get-tuple-element.58, bf16[192,512]{0,1:T(8,128)(2,1)} %copy-done.9, pred[]{:T(512)S(6)} %eq.40, f32[192,1024]{0,1:T(8,128)S(1)} %copy.18, f32[192,1024]{0,1:T(8,128)S(1)} %copy.21), kind=kLoop, calls=%fused_computation.32 | loop fusion | flops 4128768 | bytes 3932161 | tf_op jit(solution)/shard_map/convert_element_type | solution.py:100
  172.8 3.2 %collective-permute-start.31 = (bf16[384,256]{0,1:T(8,128)(2,1)S(1)}, bf16[384,256]{0,1:T(8,128)(2,1)S(1)}, u32[]{:S(2)}, u32[]{:S(2)}) collective-permute-start(bf16[384,256]{0,1:T(8,128)(2,1)S(1)} %get-tuple-element.46), channel_id=1, source_target_pairs={{0,16},{8,24},{16,0},{24,8},{1,17},{9,25},{17,1},{25,9},{2,18},{10... | collective-permute-start | bytes 589832 | tf_op jit(solution)/shard_map/ppermute | solution.py:20
  176.2 4.3 %collective-permute-start.37 = (bf16[384,256]{0,1:T(8,128)(2,1)S(1)}, bf16[384,256]{0,1:T(8,128)(2,1)S(1)}, u32[]{:S(2)}, u32[]{:S(2)}) collective-permute-start(bf16[384,256]{0,1:T(8,128)(2,1)S(1)} %get-tuple-element.48), channel_id=1, source_target_pairs={{0,4},{2,6},{4,0},{6,2},{1,5},{3,7},{5,1},{7,3},{8,12},{10,14},{12... | collective-permute-start | bytes 589832 | tf_op jit(solution)/shard_map/ppermute | solution.py:20
  180.6 3.0 %collective-permute-start.38 = (bf16[384,256]{0,1:T(8,128)(2,1)S(1)}, bf16[384,256]{0,1:T(8,128)(2,1)S(1)}, u32[]{:S(2)}, u32[]{:S(2)}) collective-permute-start(bf16[384,256]{0,1:T(8,128)(2,1)S(1)} %get-tuple-element.48), channel_id=1, source_target_pairs={{0,6},{2,0},{4,2},{6,4},{1,7},{3,1},{5,3},{7,5},{8,14},{10,8},{12,... | collective-permute-start | bytes 589832 | tf_op jit(solution)/shard_map/ppermute | solution.py:20
  185.2 2.6 %convolution_convert_fusion.3 = bf16[768,256]{1,0:T(8,128)(2,1)S(1)} fusion(bf16[768,1536]{1,0:T(8,128)(2,1)} %constant_dynamic-update-slice_fusion.8, bf16[1536,256]{0,1:T(8,128)(2,1)S(1)} %constant_dynamic-update-slice_fusion.4), kind=kOutput, calls=%fused_computation.11 | convolution fusion | flops 604176384 | bytes 3538944 | tf_op jit(solution)/shard_map/dot_general | solution.py:28
  188.8 3.3 %collective-permute-start.33 = (bf16[384,256]{1,0:T(8,128)(2,1)S(1)}, bf16[384,256]{1,0:T(8,128)(2,1)S(1)}, u32[]{:S(2)}, u32[]{:S(2)}) collective-permute-start(bf16[384,256]{1,0:T(8,128)(2,1)S(1)} %pad_maximum_fusion.3), channel_id=1, source_target_pairs={{0,6},{2,0},{4,2},{6,4},{1,7},{3,1},{5,3},{7,5},{8,14},{10,8},{12,... | collective-permute-start | bytes 589832 | tf_op jit(solution)/shard_map/ppermute | solution.py:20
  193.9 2.5 convolution_convert_fusion
  196.4 2.9 %collective-permute-start.39 = (bf16[384,256]{1,0:T(8,128)(2,1)S(1)}, bf16[384,256]{1,0:T(8,128)(2,1)S(1)}, u32[]{:S(2)}, u32[]{:S(2)}) collective-permute-start(bf16[384,256]{1,0:T(8,128)(2,1)S(1)} %pad_maximum_fusion.6), channel_id=1, source_target_pairs={{0,24},{8,0},{16,8},{24,16},{1,25},{9,1},{17,9},{25,17},{2,26},{10... | collective-permute-start | bytes 589832 | tf_op jit(solution)/shard_map/ppermute | solution.py:20
  200.4 4.0 %collective-permute-done.35 = bf16[384,256]{1,0:T(8,128)(2,1)S(1)} collective-permute-done((bf16[384,256]{1,0:T(8,128)(2,1)S(1)}, bf16[384,256]{1,0:T(8,128)(2,1)S(1)}, u32[]{:S(2)}, u32[]{:S(2)}) %collective-permute-start.35) | collective-permute-done | bytes 196640 | tf_op jit(solution)/shard_map/ppermute | solution.py:20
  204.5 2.5 %collective-permute-done.39 = bf16[384,256]{1,0:T(8,128)(2,1)S(1)} collective-permute-done((bf16[384,256]{1,0:T(8,128)(2,1)S(1)}, bf16[384,256]{1,0:T(8,128)(2,1)S(1)}, u32[]{:S(2)}, u32[]{:S(2)}) %collective-permute-start.39) | collective-permute-done | bytes 196640 | tf_op jit(solution)/shard_map/ppermute | solution.py:20
  207.0 4.9 %collective-permute-done.41 = bf16[384,256]{1,0:T(8,128)(2,1)S(1)} collective-permute-done((bf16[384,256]{1,0:T(8,128)(2,1)S(1)}, bf16[384,256]{1,0:T(8,128)(2,1)S(1)}, u32[]{:S(2)}, u32[]{:S(2)}) %collective-permute-start.41) | collective-permute-done | bytes 196640 | tf_op jit(solution)/shard_map/ppermute | solution.py:20
  212.4 2.5 collective-permute-start.44
  214.8 1.8 fusion.19
  216.7 15.3 %collective-permute-done.42 = bf16[384,512]{1,0:T(8,128)(2,1)S(1)} collective-permute-done((bf16[384,512]{1,0:T(8,128)(2,1)S(1)}, bf16[384,512]{1,0:T(8,128)(2,1)S(1)}, u32[]{:S(2)}, u32[]{:S(2)}) %collective-permute-start.42) | collective-permute-done | bytes 393248 | tf_op jit(solution)/shard_map/ppermute | solution.py:20
  232.0 1.8 fusion.14
  236.6 2.4 copy.22
  240.3 2.8 %multiply_subtract_fusion = (f32[192,1024]{1,0:T(8,128)}, f32[192,1024]{1,0:T(8,128)}) fusion(f32[192,1024]{1,0:T(8,128)} %param.7, f32[192,1024]{1,0:T(8,128)} %collective-permute-done.45, f32[384,1024]{1,0:T(8,128)S(1)} %add_add_fusion), kind=kLoop, calls=%fused_computation.45 | loop fusion | flops 983040 | bytes 3932160 | tf_op jit(solution)/shard_map/sub | solution.py:128
  (149 shorter events, 44.3 us)
Async XLA Ops:
  7.2 89.5 %all-gather.2.cloned.1.call-start = ((), (), s32[]{:S(2)}) async-start(), calls=%async_computation | async-start | bytes 4456448 | tf_op jit(solution)/shard_map/all_gather | solution.py:58
  10.0 2.5 collective-permute-start.7
  15.7 14.6 %collective-permute-start.3 = (bf16[192,1024]{1,0:T(8,128)(2,1)}, bf16[192,1024]{1,0:T(8,128)(2,1)}, u32[]{:S(2)}, u32[]{:S(2)}) collective-permute-start(bf16[192,1024]{1,0:T(8,128)(2,1)} %get-tuple-element.27), channel_id=1, source_target_pairs={{0,32},{32,64},{64,96},{96,0},{1,33},{33,65},{65,97},{97,1},{2,34}... | collective-permute-start | bytes 1179656 | tf_op jit(solution)/shard_map/ppermute | solution.py:20
  17.0 29.9 %collective-permute-start.4 = (bf16[192,1024]{1,0:T(8,128)(2,1)}, bf16[192,1024]{1,0:T(8,128)(2,1)}, u32[]{:S(2)}, u32[]{:S(2)}) collective-permute-start(bf16[192,1024]{1,0:T(8,128)(2,1)} %get-tuple-element.29), channel_id=1, source_target_pairs={{0,64},{32,96},{64,0},{96,32},{1,65},{33,97},{65,1},{97,33},{2,66}... | collective-permute-start | bytes 1179656 | tf_op jit(solution)/shard_map/ppermute | solution.py:20
  19.4 31.5 %collective-permute-start.5 = (bf16[192,1024]{1,0:T(8,128)(2,1)}, bf16[192,1024]{1,0:T(8,128)(2,1)}, u32[]{:S(2)}, u32[]{:S(2)}) collective-permute-start(bf16[192,1024]{1,0:T(8,128)(2,1)} %get-tuple-element.28), channel_id=1, source_target_pairs={{0,96},{32,0},{64,32},{96,64},{1,97},{33,1},{65,33},{97,65},{2,98}... | collective-permute-start | bytes 1179656 | tf_op jit(solution)/shard_map/ppermute | solution.py:20
  21.8 33.3 %collective-permute-start.18 = (bf16[192,1536]{1,0:T(8,128)(2,1)}, bf16[192,1536]{1,0:T(8,128)(2,1)}, u32[]{:S(2)}, u32[]{:S(2)}) collective-permute-start(bf16[192,1536]{1,0:T(8,128)(2,1)} %get-tuple-element.24), channel_id=1, source_target_pairs={{0,8},{8,16},{16,24},{24,0},{1,9},{9,17},{17,25},{25,1},{2,10},{10... | collective-permute-start | bytes 1769480 | tf_op jit(solution)/shard_map/ppermute | solution.py:20
  23.5 32.9 %collective-permute-start.19 = (bf16[192,1536]{1,0:T(8,128)(2,1)}, bf16[192,1536]{1,0:T(8,128)(2,1)}, u32[]{:S(2)}, u32[]{:S(2)}) collective-permute-start(bf16[192,1536]{1,0:T(8,128)(2,1)} %get-tuple-element.26), channel_id=1, source_target_pairs={{0,16},{8,24},{16,0},{24,8},{1,17},{9,25},{17,1},{25,9},{2,18},{10... | collective-permute-start | bytes 1769480 | tf_op jit(solution)/shard_map/ppermute | solution.py:20
  30.3 28.7 %collective-permute-start.20 = (bf16[192,1536]{1,0:T(8,128)(2,1)}, bf16[192,1536]{1,0:T(8,128)(2,1)}, u32[]{:S(2)}, u32[]{:S(2)}) collective-permute-start(bf16[192,1536]{1,0:T(8,128)(2,1)} %get-tuple-element.25), channel_id=1, source_target_pairs={{0,24},{8,0},{16,8},{24,16},{1,25},{9,1},{17,9},{25,17},{2,26},{10... | collective-permute-start | bytes 1769480 | tf_op jit(solution)/shard_map/ppermute | solution.py:20
  46.9 14.5 %collective-permute-start = (bf16[192,1536]{1,0:T(8,128)(2,1)S(1)}, bf16[192,1536]{1,0:T(8,128)(2,1)}, u32[]{:S(2)}, u32[]{:S(2)}) collective-permute-start(bf16[192,1536]{1,0:T(8,128)(2,1)S(1)} %bitcast.41), channel_id=1, source_target_pairs={{0,2},{2,4},{4,6},{6,0},{1,3},{3,5},{5,7},{7,1},{8,10},{10,12},{12... | collective-permute-start | bytes 1769480 | tf_op jit(solution)/shard_map/ppermute | solution.py:20
  50.9 53.4 %collective-permute-start.1 = (bf16[192,1536]{1,0:T(8,128)(2,1)}, bf16[192,1536]{1,0:T(8,128)(2,1)}, u32[]{:S(2)}, u32[]{:S(2)}) collective-permute-start(bf16[192,1536]{1,0:T(8,128)(2,1)} %bitcast.10), channel_id=1, source_target_pairs={{0,4},{2,6},{4,0},{6,2},{1,5},{3,7},{5,1},{7,3},{8,12},{10,14},{12... | collective-permute-start | bytes 1769480 | tf_op jit(solution)/shard_map/ppermute | solution.py:20
  55.2 52.9 %collective-permute-start.2 = (bf16[192,1536]{1,0:T(8,128)(2,1)}, bf16[192,1536]{1,0:T(8,128)(2,1)}, u32[]{:S(2)}, u32[]{:S(2)}) collective-permute-start(bf16[192,1536]{1,0:T(8,128)(2,1)} %bitcast.12), channel_id=1, source_target_pairs={{0,6},{2,0},{4,2},{6,4},{1,7},{3,1},{5,3},{7,5},{8,14},{10,8},{12,... | collective-permute-start | bytes 1769480 | tf_op jit(solution)/shard_map/ppermute | solution.py:20
  56.3 7.1 %collective-permute-start.6 = (bf16[192,1024]{1,0:T(8,128)(2,1)S(1)}, bf16[192,1024]{1,0:T(8,128)(2,1)}, u32[]{:S(2)}, u32[]{:S(2)}) collective-permute-start(bf16[192,1024]{1,0:T(8,128)(2,1)S(1)} %fusion.24), channel_id=1, source_target_pairs={{0,1},{1,0},{2,3},{3,2},{4,5},{5,4},{6,7},{7,6},{8,9},{9,8},{10,11... | collective-permute-start | bytes 1179656 | tf_op jit(solution)/shard_map/ppermute | solution.py:24
  60.6 78.9 %copy-start.3 = (bf16[768,1536]{1,0:T(8,128)(2,1)}, bf16[768,1536]{1,0:T(8,128)(2,1)S(1)}, u32[]{:S(2)}) copy-start(bf16[768,1536]{1,0:T(8,128)(2,1)S(1)} %pad_maximum_fusion) | copy-start | bytes 7077892
  60.6 76.4 %collective-permute-start.24 = (bf16[768,1536]{1,0:T(8,128)(2,1)S(1)}, bf16[768,1536]{1,0:T(8,128)(2,1)}, u32[]{:S(2)}, u32[]{:S(2)}) collective-permute-start(bf16[768,1536]{1,0:T(8,128)(2,1)S(1)} %pad_maximum_fusion), channel_id=1, source_target_pairs={{0,1},{1,0},{2,3},{3,2},{4,5},{5,4},{6,7},{7,6},{8,9},{9,8},{10,11... | collective-permute-start | bytes 7077896 | tf_op jit(solution)/shard_map/ppermute | solution.py:24
  98.9 12.4 %collective-permute-start.10 = (bf16[384,512]{1,0:T(8,128)(2,1)S(1)}, bf16[384,512]{1,0:T(8,128)(2,1)S(1)}, u32[]{:S(2)}, u32[]{:S(2)}) collective-permute-start(bf16[384,512]{1,0:T(8,128)(2,1)S(1)} %convolution_convert_fusion.4), channel_id=1, source_target_pairs={{0,96},{32,0},{64,32},{96,64},{1,97},{33,1},{65,33},{97,65},{2,98}... | collective-permute-start | bytes 1179656 | tf_op jit(solution)/shard_map/ppermute | solution.py:20
  102.6 12.1 %collective-permute-start.8 = (bf16[384,512]{1,0:T(8,128)(2,1)S(1)}, bf16[384,512]{1,0:T(8,128)(2,1)S(1)}, u32[]{:S(2)}, u32[]{:S(2)}) collective-permute-start(bf16[384,512]{1,0:T(8,128)(2,1)S(1)} %convolution_convert_fusion.6), channel_id=1, source_target_pairs={{0,32},{32,64},{64,96},{96,0},{1,33},{33,65},{65,97},{97,1},{2,34}... | collective-permute-start | bytes 1179656 | tf_op jit(solution)/shard_map/ppermute | solution.py:20
  104.3 17.0 %collective-permute-start.9 = (bf16[384,512]{1,0:T(8,128)(2,1)S(1)}, bf16[384,512]{1,0:T(8,128)(2,1)S(1)}, u32[]{:S(2)}, u32[]{:S(2)}) collective-permute-start(bf16[384,512]{1,0:T(8,128)(2,1)S(1)} %convolution_convert_fusion.5), channel_id=1, source_target_pairs={{0,64},{32,96},{64,0},{96,32},{1,65},{33,97},{65,1},{97,33},{2,66}... | collective-permute-start | bytes 1179656 | tf_op jit(solution)/shard_map/ppermute | solution.py:20
  110.0 35.0 %collective-permute-start.14 = (bf16[768,1536]{1,0:T(8,128)(2,1)}, bf16[768,1536]{1,0:T(8,128)(2,1)S(1)}, u32[]{:S(2)}, u32[]{:S(2)}) collective-permute-start(bf16[768,1536]{1,0:T(8,128)(2,1)} %constant_dynamic-update-slice_fusion.8), channel_id=1, source_target_pairs={{0,1},{1,0},{2,3},{3,2},{4,5},{5,4},{6,7},{7,6},{8,9},{9,8},{10,11... | collective-permute-start | bytes 7077896 | tf_op jit(solution)/shard_map/ppermute | solution.py:24
  123.0 11.0 %collective-permute-start.21 = (bf16[384,256]{1,0:T(8,128)(2,1)S(1)}, bf16[384,256]{1,0:T(8,128)(2,1)S(1)}, u32[]{:S(2)}, u32[]{:S(2)}) collective-permute-start(bf16[384,256]{1,0:T(8,128)(2,1)S(1)} %get-tuple-element.63), channel_id=1, source_target_pairs={{0,8},{8,16},{16,24},{24,0},{1,9},{9,17},{17,25},{25,1},{2,10},{10... | collective-permute-start | bytes 589832 | tf_op jit(solution)/shard_map/ppermute | solution.py:20
  123.1 11.0 %collective-permute-start.22 = (bf16[384,256]{1,0:T(8,128)(2,1)S(1)}, bf16[384,256]{1,0:T(8,128)(2,1)S(1)}, u32[]{:S(2)}, u32[]{:S(2)}) collective-permute-start(bf16[384,256]{1,0:T(8,128)(2,1)S(1)} %get-tuple-element.63), channel_id=1, source_target_pairs={{0,16},{8,24},{16,0},{24,8},{1,17},{9,25},{17,1},{25,9},{2,18},{10... | collective-permute-start | bytes 589832 | tf_op jit(solution)/shard_map/ppermute | solution.py:20
  124.3 11.4 %collective-permute-start.23 = (bf16[384,256]{1,0:T(8,128)(2,1)S(1)}, bf16[384,256]{1,0:T(8,128)(2,1)S(1)}, u32[]{:S(2)}, u32[]{:S(2)}) collective-permute-start(bf16[384,256]{1,0:T(8,128)(2,1)S(1)} %get-tuple-element.63), channel_id=1, source_target_pairs={{0,24},{8,0},{16,8},{24,16},{1,25},{9,1},{17,9},{25,17},{2,26},{10... | collective-permute-start | bytes 589832 | tf_op jit(solution)/shard_map/ppermute | solution.py:20
  134.1 9.2 %collective-permute-start.11 = (bf16[384,256]{1,0:T(8,128)(2,1)S(1)}, bf16[384,256]{1,0:T(8,128)(2,1)S(1)}, u32[]{:S(2)}, u32[]{:S(2)}) collective-permute-start(bf16[384,256]{1,0:T(8,128)(2,1)S(1)} %get-tuple-element.64), channel_id=1, source_target_pairs={{0,2},{2,4},{4,6},{6,0},{1,3},{3,5},{5,7},{7,1},{8,10},{10,12},{12... | collective-permute-start | bytes 589832 | tf_op jit(solution)/shard_map/ppermute | solution.py:20
  134.1 9.2 %collective-permute-start.12 = (bf16[384,256]{1,0:T(8,128)(2,1)S(1)}, bf16[384,256]{1,0:T(8,128)(2,1)S(1)}, u32[]{:S(2)}, u32[]{:S(2)}) collective-permute-start(bf16[384,256]{1,0:T(8,128)(2,1)S(1)} %get-tuple-element.64), channel_id=1, source_target_pairs={{0,4},{2,6},{4,0},{6,2},{1,5},{3,7},{5,1},{7,3},{8,12},{10,14},{12... | collective-permute-start | bytes 589832 | tf_op jit(solution)/shard_map/ppermute | solution.py:20
  135.6 9.4 %collective-permute-start.13 = (bf16[384,256]{1,0:T(8,128)(2,1)S(1)}, bf16[384,256]{1,0:T(8,128)(2,1)S(1)}, u32[]{:S(2)}, u32[]{:S(2)}) collective-permute-start(bf16[384,256]{1,0:T(8,128)(2,1)S(1)} %get-tuple-element.64), channel_id=1, source_target_pairs={{0,6},{2,0},{4,2},{6,4},{1,7},{3,1},{5,3},{7,5},{8,14},{10,8},{12,... | collective-permute-start | bytes 589832 | tf_op jit(solution)/shard_map/ppermute | solution.py:20
  140.4 11.5 %collective-permute-start.25 = (bf16[384,256]{0,1:T(8,128)(2,1)S(1)}, bf16[384,256]{0,1:T(8,128)(2,1)S(1)}, u32[]{:S(2)}, u32[]{:S(2)}) collective-permute-start(bf16[384,256]{0,1:T(8,128)(2,1)S(1)} %get-tuple-element.30), channel_id=1, source_target_pairs={{0,2},{2,4},{4,6},{6,0},{1,3},{3,5},{5,7},{7,1},{8,10},{10,12},{12... | collective-permute-start | bytes 589832 | tf_op jit(solution)/shard_map/ppermute | solution.py:20
  143.3 8.6 %collective-permute-start.26 = (bf16[384,256]{0,1:T(8,128)(2,1)S(1)}, bf16[384,256]{0,1:T(8,128)(2,1)S(1)}, u32[]{:S(2)}, u32[]{:S(2)}) collective-permute-start(bf16[384,256]{0,1:T(8,128)(2,1)S(1)} %get-tuple-element.32), channel_id=1, source_target_pairs={{0,4},{2,6},{4,0},{6,2},{1,5},{3,7},{5,1},{7,3},{8,12},{10,14},{12... | collective-permute-start | bytes 589832 | tf_op jit(solution)/shard_map/ppermute | solution.py:20
  143.3 9.5 %collective-permute-start.27 = (bf16[384,256]{0,1:T(8,128)(2,1)S(1)}, bf16[384,256]{0,1:T(8,128)(2,1)S(1)}, u32[]{:S(2)}, u32[]{:S(2)}) collective-permute-start(bf16[384,256]{0,1:T(8,128)(2,1)S(1)} %get-tuple-element.31), channel_id=1, source_target_pairs={{0,6},{2,0},{4,2},{6,4},{1,7},{3,1},{5,3},{7,5},{8,14},{10,8},{12,... | collective-permute-start | bytes 589832 | tf_op jit(solution)/shard_map/ppermute | solution.py:20
  149.1 5.8 %collective-permute-start.15 = (bf16[384,256]{0,1:T(8,128)(2,1)S(1)}, bf16[384,256]{0,1:T(8,128)(2,1)S(1)}, u32[]{:S(2)}, u32[]{:S(2)}) collective-permute-start(bf16[384,256]{0,1:T(8,128)(2,1)S(1)} %get-tuple-element.33), channel_id=1, source_target_pairs={{0,8},{8,16},{16,24},{24,0},{1,9},{9,17},{17,25},{25,1},{2,10},{10... | collective-permute-start | bytes 589832 | tf_op jit(solution)/shard_map/ppermute | solution.py:20
  149.2 8.8 %collective-permute-start.16 = (bf16[384,256]{0,1:T(8,128)(2,1)S(1)}, bf16[384,256]{0,1:T(8,128)(2,1)S(1)}, u32[]{:S(2)}, u32[]{:S(2)}) collective-permute-start(bf16[384,256]{0,1:T(8,128)(2,1)S(1)} %get-tuple-element.35), channel_id=1, source_target_pairs={{0,16},{8,24},{16,0},{24,8},{1,17},{9,25},{17,1},{25,9},{2,18},{10... | collective-permute-start | bytes 589832 | tf_op jit(solution)/shard_map/ppermute | solution.py:20
  151.9 6.1 %collective-permute-start.17 = (bf16[384,256]{0,1:T(8,128)(2,1)S(1)}, bf16[384,256]{0,1:T(8,128)(2,1)S(1)}, u32[]{:S(2)}, u32[]{:S(2)}) collective-permute-start(bf16[384,256]{0,1:T(8,128)(2,1)S(1)} %get-tuple-element.34), channel_id=1, source_target_pairs={{0,24},{8,0},{16,8},{24,16},{1,25},{9,1},{17,9},{25,17},{2,26},{10... | collective-permute-start | bytes 589832 | tf_op jit(solution)/shard_map/ppermute | solution.py:20
  159.3 7.7 %collective-permute-start.28 = (bf16[192,512]{0,1:T(8,128)(2,1)}, bf16[192,512]{0,1:T(8,128)(2,1)S(1)}, u32[]{:S(2)}, u32[]{:S(2)}) collective-permute-start(bf16[192,512]{0,1:T(8,128)(2,1)} %get-tuple-element.57), channel_id=1, source_target_pairs={{0,1},{1,0},{2,3},{3,2},{4,5},{5,4},{6,7},{7,6},{8,9},{9,8},{10,11... | collective-permute-start | bytes 589832 | tf_op jit(solution)/shard_map/ppermute | solution.py:24
  170.7 1.6 collective-permute-start.29
  172.7 7.9 %collective-permute-start.30 = (bf16[384,256]{0,1:T(8,128)(2,1)S(1)}, bf16[384,256]{0,1:T(8,128)(2,1)S(1)}, u32[]{:S(2)}, u32[]{:S(2)}) collective-permute-start(bf16[384,256]{0,1:T(8,128)(2,1)S(1)} %get-tuple-element.46), channel_id=1, source_target_pairs={{0,8},{8,16},{16,24},{24,0},{1,9},{9,17},{17,25},{25,1},{2,10},{10... | collective-permute-start | bytes 589832 | tf_op jit(solution)/shard_map/ppermute | solution.py:20
  172.8 12.3 %collective-permute-start.31 = (bf16[384,256]{0,1:T(8,128)(2,1)S(1)}, bf16[384,256]{0,1:T(8,128)(2,1)S(1)}, u32[]{:S(2)}, u32[]{:S(2)}) collective-permute-start(bf16[384,256]{0,1:T(8,128)(2,1)S(1)} %get-tuple-element.46), channel_id=1, source_target_pairs={{0,16},{8,24},{16,0},{24,8},{1,17},{9,25},{17,1},{25,9},{2,18},{10... | collective-permute-start | bytes 589832 | tf_op jit(solution)/shard_map/ppermute | solution.py:20
  176.0 9.1 %collective-permute-start.32 = (bf16[384,256]{0,1:T(8,128)(2,1)S(1)}, bf16[384,256]{0,1:T(8,128)(2,1)S(1)}, u32[]{:S(2)}, u32[]{:S(2)}) collective-permute-start(bf16[384,256]{0,1:T(8,128)(2,1)S(1)} %get-tuple-element.46), channel_id=1, source_target_pairs={{0,24},{8,0},{16,8},{24,16},{1,25},{9,1},{17,9},{25,17},{2,26},{10... | collective-permute-start | bytes 589832 | tf_op jit(solution)/shard_map/ppermute | solution.py:20
  176.0 16.2 %collective-permute-start.36 = (bf16[384,256]{0,1:T(8,128)(2,1)S(1)}, bf16[384,256]{0,1:T(8,128)(2,1)S(1)}, u32[]{:S(2)}, u32[]{:S(2)}) collective-permute-start(bf16[384,256]{0,1:T(8,128)(2,1)S(1)} %get-tuple-element.48), channel_id=1, source_target_pairs={{0,2},{2,4},{4,6},{6,0},{1,3},{3,5},{5,7},{7,1},{8,10},{10,12},{12... | collective-permute-start | bytes 589832 | tf_op jit(solution)/shard_map/ppermute | solution.py:20
  176.2 16.7 %collective-permute-start.37 = (bf16[384,256]{0,1:T(8,128)(2,1)S(1)}, bf16[384,256]{0,1:T(8,128)(2,1)S(1)}, u32[]{:S(2)}, u32[]{:S(2)}) collective-permute-start(bf16[384,256]{0,1:T(8,128)(2,1)S(1)} %get-tuple-element.48), channel_id=1, source_target_pairs={{0,4},{2,6},{4,0},{6,2},{1,5},{3,7},{5,1},{7,3},{8,12},{10,14},{12... | collective-permute-start | bytes 589832 | tf_op jit(solution)/shard_map/ppermute | solution.py:20
  180.6 12.4 %collective-permute-start.38 = (bf16[384,256]{0,1:T(8,128)(2,1)S(1)}, bf16[384,256]{0,1:T(8,128)(2,1)S(1)}, u32[]{:S(2)}, u32[]{:S(2)}) collective-permute-start(bf16[384,256]{0,1:T(8,128)(2,1)S(1)} %get-tuple-element.48), channel_id=1, source_target_pairs={{0,6},{2,0},{4,2},{6,4},{1,7},{3,1},{5,3},{7,5},{8,14},{10,8},{12,... | collective-permute-start | bytes 589832 | tf_op jit(solution)/shard_map/ppermute | solution.py:20
  188.8 11.0 %collective-permute-start.33 = (bf16[384,256]{1,0:T(8,128)(2,1)S(1)}, bf16[384,256]{1,0:T(8,128)(2,1)S(1)}, u32[]{:S(2)}, u32[]{:S(2)}) collective-permute-start(bf16[384,256]{1,0:T(8,128)(2,1)S(1)} %pad_maximum_fusion.3), channel_id=1, source_target_pairs={{0,6},{2,0},{4,2},{6,4},{1,7},{3,1},{5,3},{7,5},{8,14},{10,8},{12,... | collective-permute-start | bytes 589832 | tf_op jit(solution)/shard_map/ppermute | solution.py:20
  192.1 8.2 %collective-permute-start.34 = (bf16[384,256]{1,0:T(8,128)(2,1)S(1)}, bf16[384,256]{1,0:T(8,128)(2,1)S(1)}, u32[]{:S(2)}, u32[]{:S(2)}) collective-permute-start(bf16[384,256]{1,0:T(8,128)(2,1)S(1)} %pad_maximum_fusion.4), channel_id=1, source_target_pairs={{0,4},{2,6},{4,0},{6,2},{1,5},{3,7},{5,1},{7,3},{8,12},{10,14},{12... | collective-permute-start | bytes 589832 | tf_op jit(solution)/shard_map/ppermute | solution.py:20
  192.3 12.1 %collective-permute-start.35 = (bf16[384,256]{1,0:T(8,128)(2,1)S(1)}, bf16[384,256]{1,0:T(8,128)(2,1)S(1)}, u32[]{:S(2)}, u32[]{:S(2)}) collective-permute-start(bf16[384,256]{1,0:T(8,128)(2,1)S(1)} %pad_maximum_fusion.5), channel_id=1, source_target_pairs={{0,2},{2,4},{4,6},{6,0},{1,3},{3,5},{5,7},{7,1},{8,10},{10,12},{12... | collective-permute-start | bytes 589832 | tf_op jit(solution)/shard_map/ppermute | solution.py:20
  196.4 10.6 %collective-permute-start.39 = (bf16[384,256]{1,0:T(8,128)(2,1)S(1)}, bf16[384,256]{1,0:T(8,128)(2,1)S(1)}, u32[]{:S(2)}, u32[]{:S(2)}) collective-permute-start(bf16[384,256]{1,0:T(8,128)(2,1)S(1)} %pad_maximum_fusion.6), channel_id=1, source_target_pairs={{0,24},{8,0},{16,8},{24,16},{1,25},{9,1},{17,9},{25,17},{2,26},{10... | collective-permute-start | bytes 589832 | tf_op jit(solution)/shard_map/ppermute | solution.py:20
  199.3 7.7 %collective-permute-start.40 = (bf16[384,256]{1,0:T(8,128)(2,1)S(1)}, bf16[384,256]{1,0:T(8,128)(2,1)S(1)}, u32[]{:S(2)}, u32[]{:S(2)}) collective-permute-start(bf16[384,256]{1,0:T(8,128)(2,1)S(1)} %pad_maximum_fusion.7), channel_id=1, source_target_pairs={{0,16},{8,24},{16,0},{24,8},{1,17},{9,25},{17,1},{25,9},{2,18},{10... | collective-permute-start | bytes 589832 | tf_op jit(solution)/shard_map/ppermute | solution.py:20
  199.8 12.2 %collective-permute-start.41 = (bf16[384,256]{1,0:T(8,128)(2,1)S(1)}, bf16[384,256]{1,0:T(8,128)(2,1)S(1)}, u32[]{:S(2)}, u32[]{:S(2)}) collective-permute-start(bf16[384,256]{1,0:T(8,128)(2,1)S(1)} %pad_maximum_fusion.8), channel_id=1, source_target_pairs={{0,8},{8,16},{16,24},{24,0},{1,9},{9,17},{17,25},{25,1},{2,10},{10... | collective-permute-start | bytes 589832 | tf_op jit(solution)/shard_map/ppermute | solution.py:20
  212.1 19.9 %collective-permute-start.42 = (bf16[384,512]{1,0:T(8,128)(2,1)S(1)}, bf16[384,512]{1,0:T(8,128)(2,1)S(1)}, u32[]{:S(2)}, u32[]{:S(2)}) collective-permute-start(bf16[384,512]{1,0:T(8,128)(2,1)S(1)} %pad_maximum_fusion.2), channel_id=1, source_target_pairs={{0,32},{32,64},{64,96},{96,0},{1,33},{33,65},{65,97},{97,1},{2,34}... | collective-permute-start | bytes 1179656 | tf_op jit(solution)/shard_map/ppermute | solution.py:20
  212.3 21.6 %collective-permute-start.43 = (bf16[384,512]{1,0:T(8,128)(2,1)S(1)}, bf16[384,512]{1,0:T(8,128)(2,1)S(1)}, u32[]{:S(2)}, u32[]{:S(2)}) collective-permute-start(bf16[384,512]{1,0:T(8,128)(2,1)S(1)} %pad_maximum_fusion.2), channel_id=1, source_target_pairs={{0,64},{32,96},{64,0},{96,32},{1,65},{33,97},{65,1},{97,33},{2,66}... | collective-permute-start | bytes 1179656 | tf_op jit(solution)/shard_map/ppermute | solution.py:20
  212.4 22.1 %collective-permute-start.44 = (bf16[384,512]{1,0:T(8,128)(2,1)S(1)}, bf16[384,512]{1,0:T(8,128)(2,1)S(1)}, u32[]{:S(2)}, u32[]{:S(2)}) collective-permute-start(bf16[384,512]{1,0:T(8,128)(2,1)S(1)} %pad_maximum_fusion.2), channel_id=1, source_target_pairs={{0,96},{32,0},{64,32},{96,64},{1,97},{33,1},{65,33},{97,65},{2,98}... | collective-permute-start | bytes 1179656 | tf_op jit(solution)/shard_map/ppermute | solution.py:20
  235.2 5.0 %collective-permute-start.45 = (f32[192,1024]{1,0:T(8,128)S(1)}, f32[192,1024]{1,0:T(8,128)}, u32[]{:S(2)}, u32[]{:S(2)}) collective-permute-start(f32[192,1024]{1,0:T(8,128)S(1)} %slice.209), channel_id=1, source_target_pairs={{0,1},{1,0},{2,3},{3,2},{4,5},{5,4},{6,7},{7,6},{8,9},{9,8},{10,11... | collective-permute-start | bytes 2359304 | tf_op jit(solution)/shard_map/ppermute | solution.py:24
  (11 other events, 113.1 us)
Sparse Core Ops, SparseCore 0:
  13.4 83.2 all-gather.1

commit v2 on v0

v2 whole, which is shorter than its diff:
```python
import jax
import jax.numpy as jnp
from jax import lax
from jax.experimental import pallas as pl
from jax.experimental.pallas import tpu as pltpu
from jax.sharding import Mesh, PartitionSpec as P

beta_first = 0.95
beta_second = 0.95
bias_first = 1.0 - 0.95**10
bias_second = 1.0 - 0.95**10
epsilon = 1e-08
learn_rate = 0.02
weight_decay = 0.1

RING = 4
CHUNKS = 2
bf16 = jnp.bfloat16
f32 = jnp.float32
VMEM_LIMIT = 40 * 1024 * 1024


def shift(value, axis, distance):
    return lax.ppermute(value, axis, [(i, (i + distance) % RING) for i in range(RING)])


def swap(value):
    return lax.ppermute(value, "core", [(0, 1), (1, 0)])


def total(pieces):
    return sum(piece.astype(f32) for piece in pieces)


def call(kernel, place, operands, outs, flops, scratch=()):
    moved = sum(a.size * a.dtype.itemsize for a in operands)
    moved += sum(s.size * jnp.dtype(s.dtype).itemsize for s in outs)
    return pl.pallas_call(
        kernel,
        out_shape=outs,
        in_specs=[pl.BlockSpec(memory_space=pltpu.SMEM)]
        + [pl.BlockSpec(memory_space=pltpu.VMEM)] * len(operands),
        out_specs=[pl.BlockSpec(memory_space=pltpu.VMEM)] * len(outs),
        scratch_shapes=list(scratch),
        cost_estimate=pl.CostEstimate(flops=flops, bytes_accessed=moved, transcendentals=0),
        compiler_params=pltpu.CompilerParams(vmem_limit_bytes=VMEM_LIMIT),
    )(place, *operands)


def at(index, width):
    return pl.ds(pl.multiple_of(lax.rem(index + RING, RING) * width, width), width)


def right_kernel(place, own, other, here, before, after, far_low, far_high, *refs):
    outs, basis, grad = refs[:RING], refs[RING], refs[RING + 1]
    x, z = place[0], place[1]
    rows, depth = own.shape[0], here.shape[0]
    grad[:rows] = own[...]
    grad[rows:] = other[...]
    basis[at(z, depth)] = here[...]
    basis[at(z - 1, depth)] = before[...]
    basis[at(z + 1, depth)] = after[...]
    start = lax.rem(z + 2, RING) * depth
    basis[pl.ds(pl.multiple_of(start, depth), depth // 2)] = far_low[...]
    basis[pl.ds(pl.multiple_of(start + depth // 2, depth // 2), depth // 2)] = far_high[...]
    width = outs[0].shape[1]
    for d in range(RING):
        outs[d][...] = jnp.dot(
            grad[...], basis[:, at(x + d, width)], preferred_element_type=f32
        ).astype(bf16)


def left_kernel(place, *refs):
    pieces, left, left_other = refs[:RING], refs[RING], refs[RING + 1]
    outs, stack, stack_other = refs[RING + 2 : 2 * RING + 2], refs[-2], refs[-1]
    y, z = place[2], place[1]
    rows = pieces[0].shape[0] // 2
    for d in range(RING):
        stack[at(y - d, rows)] = pieces[d][:rows]
        stack_other[at(y - d, rows)] = pieces[d][rows:]
    chunk = outs[0].shape[0]
    over = (((0,), (0,)), ((), ()))
    for d in range(RING):
        columns = at(z + d, chunk)
        value = lax.dot_general(stack[...], left[:, columns], over, preferred_element_type=f32)
        value += lax.dot_general(
            stack_other[...], left_other[:, columns], over, preferred_element_type=f32
        )
        outs[d][...] = value.T.astype(bf16)


def back_kernel(place, *refs):
    pieces, left, left_other = refs[:RING], refs[RING], refs[RING + 1]
    outs, stack = refs[RING + 2 : 2 * RING + 2], refs[-1]
    y, z, core = place[2], place[1], place[3]
    chunk = pieces[0].shape[0]
    rows = chunk // 2
    for d in range(RING):
        start = lax.rem(z - d + RING, RING) * chunk
        stack[pl.ds(pl.multiple_of(start + core * rows, rows), rows)] = pieces[d][:rows]
        stack[pl.ds(pl.multiple_of(start + (1 - core) * rows, rows), rows)] = pieces[d][rows:]
    for d in range(RING):
        lines = at(y - d, rows)
        outs[d][:rows] = jnp.dot(left[lines], stack[...], preferred_element_type=f32).astype(bf16)
        outs[d][rows:] = jnp.dot(
            left_other[lines], stack[...], preferred_element_type=f32
        ).astype(bf16)


def final_kernel(place, *refs):
    pieces, basis = refs[:RING], refs[RING]
    so_far, (own, other) = refs[RING + 1 : -2], refs[-2:]
    x = place[0]
    rows, width = own.shape[0], pieces[0].shape[1]
    over = (((1,), (1,)), ((), ()))
    value = sum(
        lax.dot_general(pieces[d][...], basis[:, at(x - d, width)], over, preferred_element_type=f32)
        for d in range(RING)
    )
    if so_far:
        own[...] = so_far[0][...] + value[:rows]
        other[...] = so_far[1][...] + value[rows:]
    else:
        own[...] = value[:rows]
        other[...] = value[rows:]


def moment_kernel(place, own, other, one, two, *refs):
    new_one, new_two, normed = refs[-3:]
    step = pl.program_id(0)
    rotated = jnp.where(step == 0, own[...].astype(f32), other[...].astype(f32))
    first = beta_first * one[...] + (1.0 - beta_first) * rotated
    second = beta_second * two[...] + (1.0 - beta_second) * rotated * rotated
    new_one[...] = first
    new_two[...] = second
    normed[0] = (first / bias_first / (jnp.sqrt(second / bias_second) + epsilon)).astype(bf16)


def moments(place, chunk, own, other, one, two, so_far):
    rows, width = own.shape

    def block(step, place):
        return (0, lax.rem(place[3] + step, 2) * CHUNKS + chunk)

    whole = pl.BlockSpec((rows, width), lambda step, place: (0, 0))
    part = pl.BlockSpec((rows, width), block)
    like = jax.ShapeDtypeStruct(one.shape, f32)
    kept = [pl.BlockSpec(memory_space=pl.ANY)] * len(so_far)
    return pl.pallas_call(
        moment_kernel,
        out_shape=[like, like, jax.ShapeDtypeStruct((2, rows, width), bf16)],
        grid_spec=pltpu.PrefetchScalarGridSpec(
            num_scalar_prefetch=1,
            grid=(2,),
            in_specs=[whole, whole, part, part, *kept],
            out_specs=[part, part, pl.BlockSpec((1, rows, width), lambda step, place: (step, 0, 0))],
        ),
        input_output_aliases={5: 0, 6: 1} if so_far else {},
        cost_estimate=pl.CostEstimate(flops=rows * width * 30, bytes_accessed=rows * width * 40, transcendentals=0),
        compiler_params=pltpu.CompilerParams(vmem_limit_bytes=VMEM_LIMIT),
    )(place, own, other, one, two, *so_far)


def per_device(grad_parts, weights, moment_one, moment_two, left_basis, right_basis):
    x, z, y, core = (lax.axis_index(name) for name in ("x", "z", "y", "core"))
    place = jnp.stack([x, z, y, core]).astype(jnp.int32)
    first = core == 0
    rows, features = left_basis.shape
    columns = weights.shape[1]
    half = columns // 2
    width = half // CHUNKS
    spread = features // RING
    both = 2 * rows

    def of_core(value, which):
        return jnp.concatenate(
            [value[:, (2 * k + which) * half : (2 * k + which + 1) * half] for k in range(RING)], axis=1
        )

    zero, one = of_core(right_basis, 0), of_core(right_basis, 1)
    arrived = swap(jnp.where(first, one, zero))
    pair = jnp.where(first, jnp.concatenate([zero, arrived]), jnp.concatenate([arrived, one]))
    lines = [pair] + [shift(pair, "y", d) for d in (1, 2, 3)]
    turned = jnp.stack(lines)
    by_y = jnp.concatenate(
        [lax.dynamic_index_in_dim(turned, (y - k) % RING, 0, keepdims=False) for k in range(RING)]
    )

    split = jnp.stack([grad_parts[0][:, k * columns : (k + 1) * columns] for k in range(RING)])
    gradient = total(list(lax.all_to_all(split, "x", 0, 0, tiled=True))).astype(bf16)
    gradient_other = swap(gradient)

    split = jnp.stack(
        [
            jnp.concatenate(
                [left_basis[:, j * spread + k * both : j * spread + (k + 1) * both] for j in range(RING)], axis=1
            )
            for k in range(RING)
        ]
    )
    left = lax.all_to_all(split, "y", 0, 0, tiled=True).reshape(RING * rows, spread)
    left_other = swap(left)

    bases, values = [], []
    for chunk in range(CHUNKS):
        here = jnp.concatenate(
            [by_y[:, k * half + chunk * width : k * half + (chunk + 1) * width] for k in range(RING)], axis=1
        )
        middle = here.shape[0] // 2
        before, after = shift(here, "z", 1), shift(here, "z", -1)
        low, high = shift(before[:middle], "z", 1), shift(after[middle:], "z", -1)
        piece = jax.ShapeDtypeStruct((both, width), bf16)
        *parts, basis = call(
            right_kernel,
            place,
            [gradient, gradient_other, here, before, after, low, high],
            [piece] * RING + [jax.ShapeDtypeStruct((columns, RING * width), bf16)],
            2 * both * columns * RING * width,
            [pltpu.VMEM((both, columns), bf16)],
        )
        bases.append(basis)
        values.append(total([parts[0]] + [shift(parts[d], "x", d) for d in (1, 2, 3)]).astype(bf16))

    sums = []
    for value in values:
        pieces = [value] + [shift(value, "y", d) for d in (1, 2, 3)]
        parts = call(
            left_kernel,
            place,
            [*pieces, left, left_other],
            [jax.ShapeDtypeStruct((both, width), bf16)] * RING,
            2 * 2 * left.size * width,
            [pltpu.VMEM((RING * rows, width), bf16)] * 2,
        )
        sums.append(total([parts[0]] + [shift(parts[d], "z", d) for d in (1, 2, 3)]).astype(bf16))

    so_far, normed = (), []
    for chunk, value in enumerate(sums):
        upper, lower = value[:rows], value[rows:]
        own = jnp.where(first, upper, lower)
        other = swap(jnp.where(first, lower, upper))
        *so_far, scaled = moments(place, chunk, own, other, moment_one, moment_two, so_far)
        normed.append(jnp.concatenate([scaled[0], swap(scaled[1])]))
    new_one, new_two = so_far

    backs = []
    for value in normed:
        pieces = [value] + [shift(value, "z", d) for d in (1, 2, 3)]
        parts = call(
            back_kernel,
            place,
            [*pieces, left, left_other],
            [jax.ShapeDtypeStruct((both, width), bf16)] * RING,
            2 * 2 * left.size * width,
            [pltpu.VMEM((spread, width), bf16)],
        )
        backs.append(total([parts[0]] + [shift(parts[d], "y", -d) for d in (1, 2, 3)]).astype(bf16))

    so_far = []
    for value, basis in zip(backs, bases):
        pieces = [value] + [shift(value, "x", d) for d in (1, 2, 3)]
        so_far = call(
            final_kernel,
            place,
            [*pieces, basis, *so_far],
            [jax.ShapeDtypeStruct((rows, columns), f32)] * 2,
            2 * both * columns * RING * width,
        )
    update = so_far[0] + swap(so_far[1])
    new_weights = weights - learn_rate * (update + weight_decay * weights)
    return (new_weights, new_one, new_two, update)


def solution(mesh):
    grid = Mesh(mesh.devices.reshape(RING, RING, RING, 2), ("x", "z", "y", "core"))
    fsdp = ("z", "y", "core")
    placed = P(fsdp, "x")
    return jax.shard_map(
        per_device,
        mesh=grid,
        in_specs=(
            P("x", fsdp, None),
            placed,
            placed,
            placed,
            P(fsdp, None),
            P(("x", *fsdp), None),
        ),
        out_specs=(placed, placed, placed, placed),
        check_vma=False,
    )
```

time: 326 us -> 211 us (0.65)
  waiting for transfers between devices: 278 us -> 73.9 us
  starting transfers between devices: 0.25 us -> 90.5 us
  matrix products: 29.5 us -> 0 us
  Pallas kernels: 0 us -> 25.6 us
  between operations: 15.5 us -> 0.99 us
  local copies, waits for them, and re-layouts: 0.02 us -> 9.69 us
  other arithmetic: 2.84 us -> 9.24 us
    reduce_scatter x3 -> x0, waiting for transfers between devices: 161 us -> none  [the longest x1 106 us: per_device(): lax.psum_scatter(whole_term.astype(jnp.bfloat16), 'fsdp', scatter_dimensi...]
    all_gather x3 -> x0, waiting for transfers between devices: 116 us -> none  [the longest x1 64.3 us: per_device(): lax.all_gather(normed, 'fsdp', axis=0, tiled=True)]
    ppermute x0 -> x55, starting transfers between devices: none -> 81 us  [the longest x47 58.1 us: shift(): lax.ppermute(value, axis, [(i, (i + distance) % RING) for i in range(RING)])]
    ppermute x0 -> x55, waiting for transfers between devices: none -> 53.9 us  [the longest x47 52 us: shift(): lax.ppermute(value, axis, [(i, (i + distance) % RING) for i in range(RING)])]
    dot_general x4 -> x0, matrix products: 29.5 us -> none  [the longest x1 8.12 us: per_device(): lax.dot_general(full_rows, basis_block, (((1,), (1,)), ((), ())), preferr...]
    pallas_call x0 -> x10, Pallas kernels: none -> 25.6 us  [the longest x8 22.2 us: call(): pl.pallas_call(kernel, out_shape=outs, in_specs=[pl.BlockSpec(memory_spac...]
    all_to_all x0 -> x2, waiting for transfers between devices: none -> 20 us  [the longest x1 20 us: per_device(): lax.all_to_all(split, 'y', 0, 0, tiled=True).reshape(RING * rows, spread)]
    all_to_all x0 -> x2, starting transfers between devices: none -> 9.5 us  [the longest x1 5.14 us: per_device(): lax.all_to_all(split, 'y', 0, 0, tiled=True).reshape(RING * rows, spread)]
  transfers between devices with their start and end apart: 6 -> 57, of which waited for: 6 -> 21; matrix products, arithmetic and copies ran while one was open for 2% -> 7% of each run, Pallas kernels for 0% -> 11%
where the time goes in v2:
time: 211 us; the launch traced here: 210 us
  starting transfers between devices  90.5 us (43%)
  waiting for transfers between devices  73.9 us (35%)
  Pallas kernels  25.6 us (12%)
  local copies, waits for them, and re-layouts  9.69 us (5%)
  other arithmetic  9.24 us (4%)
    ppermute x47, starting transfers between devices, shift(): lax.ppermute(value, axis, [(i, (i + distance) % RING) for i in range(RING)])  58.1 us
    ppermute x47, waiting for transfers between devices, shift(): lax.ppermute(value, axis, [(i, (i + distance) % RING) for i in range(RING)])  52 us
    ppermute x8, starting transfers between devices, swap(): return lax.ppermute(value, 'core', [(0, 1), (1, 0)])  22.9 us
    pallas_call x8, Pallas kernels, call(): pl.pallas_call(kernel, out_shape=outs, in_specs=[pl.BlockSpec(memory_spac...  22.2 us
    all_to_all x1, waiting for transfers between devices, per_device(): lax.all_to_all(split, 'y', 0, 0, tiled=True).reshape(RING * rows, spread)  20 us
    slice x4, local copies, waits for them, and re-layouts, per_device(): low, high = (shift(before[:middle], 'z', 1), shift(after[middle:], 'z', -1))  5.97 us
    all_to_all x1, starting transfers between devices, per_device(): lax.all_to_all(split, 'y', 0, 0, tiled=True).reshape(RING * rows, spread)  5.14 us
    all_to_all x1, starting transfers between devices, per_device(): lax.all_to_all(split, 'x', 0, 0, tiled=True)  4.35 us
  transfers between devices with their start and end apart: 57, of which 21 were waited for; matrix products, arithmetic and copies ran while one was open for 7% of the time, Pallas kernels for 11%

profile of v2, /device:TPU:1, one launch (start us, length us, event | category | flops | bytes accessed | tf_op | source)
XLA Modules:
  0.0 210.0 jit_solution(11795433227620845826)
XLA Ops:
  0.6 2.0 fusion.3
  2.8 1.7 pad_maximum_fusion
  4.5 5.1 %all-to-all-start.1 = ((bf16[4,192,1536]{2,1,0:T(8,128)(2,1)}), bf16[4,192,1536]{2,1,0:T(8,128)(2,1)S(1)}, u32[]{:S(2)}, u32[]{:S(2)}) async-start(bf16[4,192,1536]{2,1,0:T(8,128)(2,1)} %pad_maximum_fusion), calls=%async_computation.1 | async-start | bytes 4718592 | tf_op jit(solution)/shard_map/all_to_all | solution.py:201
  12.3 3.0 %collective-permute-start.4 = (bf16[64,2048]{1,0:T(8,128)(2,1)S(1)}, bf16[64,2048]{1,0:T(8,128)(2,1)S(1)}, u32[]{:S(2)}, u32[]{:S(2)}) collective-permute-start(bf16[64,2048]{1,0:T(8,128)(2,1)S(1)} %maximum_select_fusion.1), channel_id=1, source_target_pairs={{0,6},{2,0},{4,2},{6,4},{1,7},{3,1},{5,3},{7,5},{8,14},{10,8},{12,... | collective-permute-start | bytes 786440 | tf_op jit(solution)/shard_map/ppermute | solution.py:24
  17.9 20.0 %all-to-all-done.1 = bf16[4,192,1536]{2,1,0:T(8,128)(2,1)S(1)} async-done(((bf16[4,192,1536]{2,1,0:T(8,128)(2,1)}), bf16[4,192,1536]{2,1,0:T(8,128)(2,1)S(1)}, u32[]{:S(2)}, u32[]{:S(2)}) %all-to-all-start.1) | async-done | bytes 2359328 | tf_op jit(solution)/shard_map/all_to_all | solution.py:201
  37.9 4.4 %all-to-all-start = ((bf16[4,192,1024]{2,1,0:T(8,128)(2,1)}), bf16[4,192,1024]{2,1,0:T(8,128)(2,1)}, u32[]{:S(2)}, u32[]{:S(2)}) async-start(bf16[4,192,1024]{2,1,0:T(8,128)(2,1)} %pad_maximum_fusion.1), calls=%async_computation | async-start | bytes 3145728 | tf_op jit(solution)/shard_map/all_to_all | solution.py:190
  43.6 5.3 %collective-permute-done.2 = bf16[64,2048]{1,0:T(8,128)(2,1)} collective-permute-done((bf16[64,2048]{1,0:T(8,128)(2,1)S(1)}, bf16[64,2048]{1,0:T(8,128)(2,1)}, u32[]{:S(2)}, u32[]{:S(2)}) %collective-permute-start.2) | collective-permute-done | bytes 262176 | tf_op jit(solution)/shard_map/ppermute | solution.py:24
  50.2 1.9 collective-permute-start.15
  52.4 1.7 collective-permute-start.20
  54.1 2.2 %collective-permute-start.21 = (bf16[256,1024]{1,0:T(8,128)(2,1)S(1)}, bf16[256,1024]{1,0:T(8,128)(2,1)}, u32[]{:S(2)}, u32[]{:S(2)}) collective-permute-start(bf16[256,1024]{1,0:T(8,128)(2,1)S(1)} %pad_maximum_fusion.5.here), channel_id=1, source_target_pairs={{0,24},{8,0},{16,8},{24,16},{1,25},{9,1},{17,9},{25,17},{2,26},{10... | collective-permute-start | bytes 1572872 | tf_op jit(solution)/shard_map/ppermute | solution.py:24
  56.5 2.7 %collective-permute-start.6 = (bf16[256,1024]{1,0:T(8,128)(2,1)S(1)}, bf16[256,1024]{1,0:T(8,128)(2,1)}, u32[]{:S(2)}, u32[]{:S(2)}) collective-permute-start(bf16[256,1024]{1,0:T(8,128)(2,1)S(1)} %pad_maximum_fusion.4.here), channel_id=1, source_target_pairs={{0,24},{8,0},{16,8},{24,16},{1,25},{9,1},{17,9},{25,17},{2,26},{10... | collective-permute-start | bytes 1572872 | tf_op jit(solution)/shard_map/ppermute | solution.py:24
  59.1 2.4 %fusion.own = bf16[192,1024]{1,0:T(8,128)(2,1)} fusion(bf16[4,192,1024]{2,1,0:T(8,128)(2,1)} %all-to-all-done), kind=kLoop, calls=%fused_computation.12 | loop fusion | flops 1572864 | bytes 1966080 | tf_op jit(solution)/shard_map/add | solution.py:32
  61.5 7.1 %collective-permute-done.20.before = bf16[256,1024]{1,0:T(8,128)(2,1)} collective-permute-done((bf16[256,1024]{1,0:T(8,128)(2,1)S(1)}, bf16[256,1024]{1,0:T(8,128)(2,1)}, u32[]{:S(2)}, u32[]{:S(2)}) %collective-permute-start.20) | collective-permute-done | bytes 524320 | tf_op jit(solution)/shard_map/ppermute | solution.py:24
  69.4 1.7 slice.208
  71.1 1.7 slice.209
  72.7 7.1 %collective-permute-done.5.before = bf16[256,1024]{1,0:T(8,128)(2,1)} collective-permute-done((bf16[256,1024]{1,0:T(8,128)(2,1)S(1)}, bf16[256,1024]{1,0:T(8,128)(2,1)}, u32[]{:S(2)}, u32[]{:S(2)}) %collective-permute-start.5) | collective-permute-done | bytes 524320 | tf_op jit(solution)/shard_map/ppermute | solution.py:24
  81.1 1.7 slice.200
  87.2 2.8 %shard_map.95 = (bf16[384,256]{1,0:T(8,128)(2,1)S(1)}, bf16[384,256]{1,0:T(8,128)(2,1)S(1)}, bf16[384,256]{1,0:T(8,128)(2,1)S(1)}, bf16[384,256]{1,0:T(8,128)(2,1)S(1)}, bf16[1024,1024]{1,0:T(8,128)(2,1)S(1)}) custom-call(s32[4]{0:T(128)S(1)} %pad_add_fusion.place, bf16[192,1024]{1,0:T(8,128)(2,1)} %fusion.own, ...), custom_call_target="tpu_custom_call" | custom-call | flops 805306368 | bytes 5767168 | tf_op jit(solution)/shard_map/pallas_call | solution.py:38
  90.0 2.8 %collective-permute-start.26 = (bf16[384,256]{1,0:T(8,128)(2,1)S(1)}, bf16[384,256]{1,0:T(8,128)(2,1)S(1)}, u32[]{:S(2)}, u32[]{:S(2)}) collective-permute-start(bf16[384,256]{1,0:T(8,128)(2,1)S(1)} %get-tuple-element.51), channel_id=1, source_target_pairs={{0,96},{32,0},{64,32},{96,64},{1,97},{33,1},{65,33},{97,65},{2,98}... | collective-permute-start | bytes 589832 | tf_op jit(solution)/shard_map/ppermute | solution.py:24
  93.9 2.7 %shard_map.93 = (bf16[384,256]{1,0:T(8,128)(2,1)S(1)}, bf16[384,256]{1,0:T(8,128)(2,1)S(1)}, bf16[384,256]{1,0:T(8,128)(2,1)S(1)}, bf16[384,256]{1,0:T(8,128)(2,1)S(1)}, bf16[1024,1024]{1,0:T(8,128)(2,1)S(1)}) custom-call(s32[4]{0:T(128)S(1)} %pad_add_fusion.place, bf16[192,1024]{1,0:T(8,128)(2,1)} %fusion.own, ...), custom_call_target="tpu_custom_call" | custom-call | flops 805306368 | bytes 5767168 | tf_op jit(solution)/shard_map/pallas_call | solution.py:38
  96.6 2.2 %collective-permute-start.11 = (bf16[384,256]{1,0:T(8,128)(2,1)S(1)}, bf16[384,256]{1,0:T(8,128)(2,1)S(1)}, u32[]{:S(2)}, u32[]{:S(2)}) collective-permute-start(bf16[384,256]{1,0:T(8,128)(2,1)S(1)} %get-tuple-element.43), channel_id=1, source_target_pairs={{0,96},{32,0},{64,32},{96,64},{1,97},{33,1},{65,33},{97,65},{2,98}... | collective-permute-start | bytes 589832 | tf_op jit(solution)/shard_map/ppermute | solution.py:24
  99.9 1.6 collective-permute-start.9
  101.6 4.5 %collective-permute-done.24 = bf16[384,256]{1,0:T(8,128)(2,1)S(1)} collective-permute-done((bf16[384,256]{1,0:T(8,128)(2,1)S(1)}, bf16[384,256]{1,0:T(8,128)(2,1)S(1)}, u32[]{:S(2)}, u32[]{:S(2)}) %collective-permute-start.24) | collective-permute-done | bytes 196640 | tf_op jit(solution)/shard_map/ppermute | solution.py:24
  107.0 1.8 collective-permute-start.28
  109.8 3.2 %collective-permute-done.9 = bf16[384,256]{1,0:T(8,128)(2,1)S(1)} collective-permute-done((bf16[384,256]{1,0:T(8,128)(2,1)S(1)}, bf16[384,256]{1,0:T(8,128)(2,1)S(1)}, u32[]{:S(2)}, u32[]{:S(2)}) %collective-permute-start.9) | collective-permute-done | bytes 196640 | tf_op jit(solution)/shard_map/ppermute | solution.py:24
  116.2 3.7 %shard_map.96 = (bf16[384,256]{1,0:T(8,128)(2,1)S(1)}, bf16[384,256]{1,0:T(8,128)(2,1)S(1)}, bf16[384,256]{1,0:T(8,128)(2,1)S(1)}, bf16[384,256]{1,0:T(8,128)(2,1)S(1)}) custom-call(s32[4]{0:T(128)S(1)} %pad_add_fusion.place, bf16[384,256]{1,0:T(8,128)(2,1)S(1)} %add_convert_fusion.4.refs_0_, bf16[384,256]{1,0:T(8,128)(2,1)S(1)} %collective-permute-done.27.refs_1_, ...), custom_call_target="tpu_custom_call" | custom-call | flops 1207959552 | bytes 6291456 | tf_op jit(solution)/shard_map/pallas_call | solution.py:38
  119.9 1.6 collective-permute-start.32
  121.5 2.6 %collective-permute-start.31 = (bf16[384,256]{1,0:T(8,128)(2,1)S(1)}, bf16[384,256]{1,0:T(8,128)(2,1)S(1)}, u32[]{:S(2)}, u32[]{:S(2)}) collective-permute-start(bf16[384,256]{1,0:T(8,128)(2,1)S(1)} %get-tuple-element.54), channel_id=1, source_target_pairs={{0,16},{8,24},{16,0},{24,8},{1,17},{9,25},{17,1},{25,9},{2,18},{10... | collective-permute-start | bytes 589832 | tf_op jit(solution)/shard_map/ppermute | solution.py:24
  124.2 3.3 %collective-permute-start.30 = (bf16[384,256]{1,0:T(8,128)(2,1)S(1)}, bf16[384,256]{1,0:T(8,128)(2,1)S(1)}, u32[]{:S(2)}, u32[]{:S(2)}) collective-permute-start(bf16[384,256]{1,0:T(8,128)(2,1)S(1)} %get-tuple-element.53), channel_id=1, source_target_pairs={{0,8},{8,16},{16,24},{24,0},{1,9},{9,17},{17,25},{25,1},{2,10},{10... | collective-permute-start | bytes 589832 | tf_op jit(solution)/shard_map/ppermute | solution.py:24
  127.5 3.7 %shard_map.94 = (bf16[384,256]{1,0:T(8,128)(2,1)S(1)}, bf16[384,256]{1,0:T(8,128)(2,1)S(1)}, bf16[384,256]{1,0:T(8,128)(2,1)S(1)}, bf16[384,256]{1,0:T(8,128)(2,1)S(1)}) custom-call(s32[4]{0:T(128)S(1)} %pad_add_fusion.place, bf16[384,256]{1,0:T(8,128)(2,1)S(1)} %add_convert_fusion.6.refs_0_, bf16[384,256]{1,0:T(8,128)(2,1)S(1)} %collective-permute-done.12.refs_1_, ...), custom_call_target="tpu_custom_call" | custom-call | flops 1207959552 | bytes 6291456 | tf_op jit(solution)/shard_map/pallas_call | solution.py:38
  133.3 10.1 %collective-permute-start.33 = (bf16[192,256]{1,0:T(8,128)(2,1)S(1)}, bf16[192,256]{1,0:T(8,128)(2,1)S(1)}, u32[]{:S(2)}, u32[]{:S(2)}) collective-permute-start(bf16[192,256]{1,0:T(8,128)(2,1)S(1)} %get-tuple-element.122), channel_id=1, source_target_pairs={{0,1},{1,0},{2,3},{3,2},{4,5},{5,4},{6,7},{7,6},{8,9},{9,8},{10,11... | collective-permute-start | bytes 294920 | tf_op jit(solution)/shard_map/ppermute | solution.py:28
  143.7 4.7 %collective-permute-start.19 = (bf16[192,256]{1,0:T(8,128)(2,1)S(1)}, bf16[192,256]{1,0:T(8,128)(2,1)S(1)}, u32[]{:S(2)}, u32[]{:S(2)}) collective-permute-start(bf16[192,256]{1,0:T(8,128)(2,1)S(1)} %get-tuple-element.124), channel_id=1, source_target_pairs={{0,1},{1,0},{2,3},{3,2},{4,5},{5,4},{6,7},{7,6},{8,9},{9,8},{10,11... | collective-permute-start | bytes 294920 | tf_op jit(solution)/shard_map/ppermute | solution.py:28
  148.4 1.7 shard_map.97
  150.2 1.7 shard_map.98
  155.9 1.9 collective-permute-start.36
  157.8 6.7 %collective-permute-done.45.refs_1_ = bf16[384,256]{1,0:T(8,128)(2,1)S(1)} collective-permute-done((bf16[384,256]{1,0:T(8,128)(2,1)S(1)}, bf16[384,256]{1,0:T(8,128)(2,1)S(1)}, u32[]{:S(2)}, u32[]{:S(2)}) %collective-permute-start.45) | collective-permute-done | bytes 196640 | tf_op jit(solution)/shard_map/ppermute | solution.py:24
  164.8 3.1 %shard_map.100 = (bf16[384,256]{1,0:T(8,128)(2,1)S(1)}, bf16[384,256]{1,0:T(8,128)(2,1)S(1)}, bf16[384,256]{1,0:T(8,128)(2,1)S(1)}, bf16[384,256]{1,0:T(8,128)(2,1)S(1)}) custom-call(s32[4]{0:T(128)S(1)} %pad_add_fusion.place, bf16[384,256]{1,0:T(8,128)(2,1)S(1)} %pad_maximum_fusion.7.refs_0_, bf16[384,256]{1,0:T(8,128)(2,1)S(1)} %collective-permute-done.45.refs_1_, ...), custom_call_target="tpu_custom_call" | custom-call | flops 1207959552 | bytes 6291456 | tf_op jit(solution)/shard_map/pallas_call | solution.py:38
  169.1 3.8 %collective-permute-start.49 = (bf16[384,256]{1,0:T(8,128)(2,1)S(1)}, bf16[384,256]{1,0:T(8,128)(2,1)S(1)}, u32[]{:S(2)}, u32[]{:S(2)}) collective-permute-start(bf16[384,256]{1,0:T(8,128)(2,1)S(1)} %get-tuple-element.67), channel_id=1, source_target_pairs={{0,4},{2,6},{4,0},{6,2},{1,5},{3,7},{5,1},{7,3},{8,12},{10,14},{12... | collective-permute-start | bytes 589832 | tf_op jit(solution)/shard_map/ppermute | solution.py:24
  173.3 3.1 %shard_map.99 = (bf16[384,256]{1,0:T(8,128)(2,1)S(1)}, bf16[384,256]{1,0:T(8,128)(2,1)S(1)}, bf16[384,256]{1,0:T(8,128)(2,1)S(1)}, bf16[384,256]{1,0:T(8,128)(2,1)S(1)}) custom-call(s32[4]{0:T(128)S(1)} %pad_add_fusion.place, bf16[384,256]{1,0:T(8,128)(2,1)S(1)} %pad_maximum_fusion.6.refs_0_, bf16[384,256]{1,0:T(8,128)(2,1)S(1)} %collective-permute-done.35.refs_1_, ...), custom_call_target="tpu_custom_call" | custom-call | flops 1207959552 | bytes 6291456 | tf_op jit(solution)/shard_map/pallas_call | solution.py:38
  177.6 3.7 %collective-permute-start.39 = (bf16[384,256]{1,0:T(8,128)(2,1)S(1)}, bf16[384,256]{1,0:T(8,128)(2,1)S(1)}, u32[]{:S(2)}, u32[]{:S(2)}) collective-permute-start(bf16[384,256]{1,0:T(8,128)(2,1)S(1)} %get-tuple-element.61), channel_id=1, source_target_pairs={{0,4},{2,6},{4,0},{6,2},{1,5},{3,7},{5,1},{7,3},{8,12},{10,14},{12... | collective-permute-start | bytes 589832 | tf_op jit(solution)/shard_map/ppermute | solution.py:24
  181.6 1.8 collective-permute-start.52
  184.4 5.0 %collective-permute-done.39 = bf16[384,256]{1,0:T(8,128)(2,1)S(1)} collective-permute-done((bf16[384,256]{1,0:T(8,128)(2,1)S(1)}, bf16[384,256]{1,0:T(8,128)(2,1)S(1)}, u32[]{:S(2)}, u32[]{:S(2)}) %collective-permute-start.39) | collective-permute-done | bytes 196640 | tf_op jit(solution)/shard_map/ppermute | solution.py:24
  190.5 1.7 collective-permute-start.43
  193.8 3.4 %collective-permute-done.41.refs_1_ = bf16[384,256]{1,0:T(8,128)(2,1)S(1)} collective-permute-done((bf16[384,256]{1,0:T(8,128)(2,1)S(1)}, bf16[384,256]{1,0:T(8,128)(2,1)S(1)}, u32[]{:S(2)}, u32[]{:S(2)}) %collective-permute-start.41) | collective-permute-done | bytes 196640 | tf_op jit(solution)/shard_map/ppermute | solution.py:24
  197.2 1.8 collective-permute-done.42.refs_2_
  198.9 2.5 %collective-permute-done.43.refs_3_ = bf16[384,256]{1,0:T(8,128)(2,1)S(1)} collective-permute-done((bf16[384,256]{1,0:T(8,128)(2,1)S(1)}, bf16[384,256]{1,0:T(8,128)(2,1)S(1)}, u32[]{:S(2)}, u32[]{:S(2)}) %collective-permute-start.43) | collective-permute-done | bytes 196640 | tf_op jit(solution)/shard_map/ppermute | solution.py:24
  203.0 3.7 %collective-permute-start.54 = (f32[192,1024]{1,0:T(8,128)S(1)}, f32[192,1024]{1,0:T(8,128)S(1)}, u32[]{:S(2)}, u32[]{:S(2)}) collective-permute-start(f32[192,1024]{1,0:T(8,128)S(1)} %get-tuple-element.73), channel_id=1, source_target_pairs={{0,1},{1,0},{2,3},{3,2},{4,5},{5,4},{6,7},{7,6},{8,9},{9,8},{10,11... | collective-permute-start | bytes 2359304 | tf_op jit(solution)/shard_map/ppermute | solution.py:28
  206.7 1.9 collective-permute-done.54
  (119 shorter events, 38.7 us)
Async XLA Ops:
  4.5 33.4 %all-to-all-start.1 = ((bf16[4,192,1536]{2,1,0:T(8,128)(2,1)}), bf16[4,192,1536]{2,1,0:T(8,128)(2,1)S(1)}, u32[]{:S(2)}, u32[]{:S(2)}) async-start(bf16[4,192,1536]{2,1,0:T(8,128)(2,1)} %pad_maximum_fusion), calls=%async_computation.1 | async-start | bytes 4718592 | tf_op jit(solution)/shard_map/all_to_all | solution.py:201
  12.3 29.9 %collective-permute-start.4 = (bf16[64,2048]{1,0:T(8,128)(2,1)S(1)}, bf16[64,2048]{1,0:T(8,128)(2,1)S(1)}, u32[]{:S(2)}, u32[]{:S(2)}) collective-permute-start(bf16[64,2048]{1,0:T(8,128)(2,1)S(1)} %maximum_select_fusion.1), channel_id=1, source_target_pairs={{0,6},{2,0},{4,2},{6,4},{1,7},{3,1},{5,3},{7,5},{8,14},{10,8},{12,... | collective-permute-start | bytes 786440 | tf_op jit(solution)/shard_map/ppermute | solution.py:24
  15.4 28.3 %collective-permute-start.3 = (bf16[64,2048]{1,0:T(8,128)(2,1)S(1)}, bf16[64,2048]{1,0:T(8,128)(2,1)}, u32[]{:S(2)}, u32[]{:S(2)}) collective-permute-start(bf16[64,2048]{1,0:T(8,128)(2,1)S(1)} %maximum_select_fusion.1), channel_id=1, source_target_pairs={{0,4},{2,6},{4,0},{6,2},{1,5},{3,7},{5,1},{7,3},{8,12},{10,14},{12... | collective-permute-start | bytes 786440 | tf_op jit(solution)/shard_map/ppermute | solution.py:24
  15.9 33.0 %collective-permute-start.2 = (bf16[64,2048]{1,0:T(8,128)(2,1)S(1)}, bf16[64,2048]{1,0:T(8,128)(2,1)}, u32[]{:S(2)}, u32[]{:S(2)}) collective-permute-start(bf16[64,2048]{1,0:T(8,128)(2,1)S(1)} %maximum_select_fusion.1), channel_id=1, source_target_pairs={{0,2},{2,4},{4,6},{6,0},{1,3},{3,5},{5,7},{7,1},{8,10},{10,12},{12... | collective-permute-start | bytes 786440 | tf_op jit(solution)/shard_map/ppermute | solution.py:24
  37.9 21.2 %all-to-all-start = ((bf16[4,192,1024]{2,1,0:T(8,128)(2,1)}), bf16[4,192,1024]{2,1,0:T(8,128)(2,1)}, u32[]{:S(2)}, u32[]{:S(2)}) async-start(bf16[4,192,1024]{2,1,0:T(8,128)(2,1)} %pad_maximum_fusion.1), calls=%async_computation | async-start | bytes 3145728 | tf_op jit(solution)/shard_map/all_to_all | solution.py:190
  50.2 66.0 %collective-permute-start.15 = (bf16[768,1536]{1,0:T(8,128)(2,1)S(1)}, bf16[768,1536]{1,0:T(8,128)(2,1)}, u32[]{:S(2)}, u32[]{:S(2)}) collective-permute-start(bf16[768,1536]{1,0:T(8,128)(2,1)S(1)} %bitcast.48), channel_id=1, source_target_pairs={{0,1},{1,0},{2,3},{3,2},{4,5},{5,4},{6,7},{7,6},{8,9},{9,8},{10,11... | collective-permute-start | bytes 7077896 | tf_op jit(solution)/shard_map/ppermute | solution.py:28
  52.4 16.2 %collective-permute-start.20 = (bf16[256,1024]{1,0:T(8,128)(2,1)S(1)}, bf16[256,1024]{1,0:T(8,128)(2,1)}, u32[]{:S(2)}, u32[]{:S(2)}) collective-permute-start(bf16[256,1024]{1,0:T(8,128)(2,1)S(1)} %pad_maximum_fusion.5.here), channel_id=1, source_target_pairs={{0,8},{8,16},{16,24},{24,0},{1,9},{9,17},{17,25},{25,1},{2,10},{10... | collective-permute-start | bytes 1572872 | tf_op jit(solution)/shard_map/ppermute | solution.py:24
  54.1 17.0 %collective-permute-start.21 = (bf16[256,1024]{1,0:T(8,128)(2,1)S(1)}, bf16[256,1024]{1,0:T(8,128)(2,1)}, u32[]{:S(2)}, u32[]{:S(2)}) collective-permute-start(bf16[256,1024]{1,0:T(8,128)(2,1)S(1)} %pad_maximum_fusion.5.here), channel_id=1, source_target_pairs={{0,24},{8,0},{16,8},{24,16},{1,25},{9,1},{17,9},{25,17},{2,26},{10... | collective-permute-start | bytes 1572872 | tf_op jit(solution)/shard_map/ppermute | solution.py:24
  56.4 23.5 %collective-permute-start.5 = (bf16[256,1024]{1,0:T(8,128)(2,1)S(1)}, bf16[256,1024]{1,0:T(8,128)(2,1)}, u32[]{:S(2)}, u32[]{:S(2)}) collective-permute-start(bf16[256,1024]{1,0:T(8,128)(2,1)S(1)} %pad_maximum_fusion.4.here), channel_id=1, source_target_pairs={{0,8},{8,16},{16,24},{24,0},{1,9},{9,17},{17,25},{25,1},{2,10},{10... | collective-permute-start | bytes 1572872 | tf_op jit(solution)/shard_map/ppermute | solution.py:24
  56.5 26.3 %collective-permute-start.6 = (bf16[256,1024]{1,0:T(8,128)(2,1)S(1)}, bf16[256,1024]{1,0:T(8,128)(2,1)}, u32[]{:S(2)}, u32[]{:S(2)}) collective-permute-start(bf16[256,1024]{1,0:T(8,128)(2,1)S(1)} %pad_maximum_fusion.4.here), channel_id=1, source_target_pairs={{0,24},{8,0},{16,8},{24,16},{1,25},{9,1},{17,9},{25,17},{2,26},{10... | collective-permute-start | bytes 1572872 | tf_op jit(solution)/shard_map/ppermute | solution.py:24
  68.6 18.6 %collective-permute-start = (bf16[192,1024]{1,0:T(8,128)(2,1)}, bf16[192,1024]{1,0:T(8,128)(2,1)}, u32[]{:S(2)}, u32[]{:S(2)}) collective-permute-start(bf16[192,1024]{1,0:T(8,128)(2,1)} %fusion.own), channel_id=1, source_target_pairs={{0,1},{1,0},{2,3},{3,2},{4,5},{5,4},{6,7},{7,6},{8,9},{9,8},{10,11... | collective-permute-start | bytes 1179656 | tf_op jit(solution)/shard_map/ppermute | solution.py:28
  71.1 14.4 %collective-permute-start.22 = (bf16[128,1024]{1,0:T(8,128)(2,1)}, bf16[128,1024]{1,0:T(8,128)(2,1)}, u32[]{:S(2)}, u32[]{:S(2)}) collective-permute-start(bf16[128,1024]{1,0:T(8,128)(2,1)} %slice.208), channel_id=1, source_target_pairs={{0,8},{8,16},{16,24},{24,0},{1,9},{9,17},{17,25},{25,1},{2,10},{10... | collective-permute-start | bytes 786440 | tf_op jit(solution)/shard_map/ppermute | solution.py:24
  82.8 10.5 %collective-permute-start.7 = (bf16[128,1024]{1,0:T(8,128)(2,1)}, bf16[128,1024]{1,0:T(8,128)(2,1)}, u32[]{:S(2)}, u32[]{:S(2)}) collective-permute-start(bf16[128,1024]{1,0:T(8,128)(2,1)} %slice.200), channel_id=1, source_target_pairs={{0,8},{8,16},{16,24},{24,0},{1,9},{9,17},{17,25},{25,1},{2,10},{10... | collective-permute-start | bytes 786440 | tf_op jit(solution)/shard_map/ppermute | solution.py:24
  85.5 8.4 %collective-permute-start.8 = (bf16[128,1024]{1,0:T(8,128)(2,1)S(1)}, bf16[128,1024]{1,0:T(8,128)(2,1)S(1)}, u32[]{:S(2)}, u32[]{:S(2)}) collective-permute-start(bf16[128,1024]{1,0:T(8,128)(2,1)S(1)} %slice.201), channel_id=1, source_target_pairs={{0,24},{8,0},{16,8},{24,16},{1,25},{9,1},{17,9},{25,17},{2,26},{10... | collective-permute-start | bytes 786440 | tf_op jit(solution)/shard_map/ppermute | solution.py:24
  90.0 8.7 %collective-permute-start.26 = (bf16[384,256]{1,0:T(8,128)(2,1)S(1)}, bf16[384,256]{1,0:T(8,128)(2,1)S(1)}, u32[]{:S(2)}, u32[]{:S(2)}) collective-permute-start(bf16[384,256]{1,0:T(8,128)(2,1)S(1)} %get-tuple-element.51), channel_id=1, source_target_pairs={{0,96},{32,0},{64,32},{96,64},{1,97},{33,1},{65,33},{97,65},{2,98}... | collective-permute-start | bytes 589832 | tf_op jit(solution)/shard_map/ppermute | solution.py:24
  93.3 12.8 %collective-permute-start.24 = (bf16[384,256]{1,0:T(8,128)(2,1)S(1)}, bf16[384,256]{1,0:T(8,128)(2,1)S(1)}, u32[]{:S(2)}, u32[]{:S(2)}) collective-permute-start(bf16[384,256]{1,0:T(8,128)(2,1)S(1)} %get-tuple-element.49), channel_id=1, source_target_pairs={{0,32},{32,64},{64,96},{96,0},{1,33},{33,65},{65,97},{97,1},{2,34}... | collective-permute-start | bytes 589832 | tf_op jit(solution)/shard_map/ppermute | solution.py:24
  96.6 10.4 %collective-permute-start.11 = (bf16[384,256]{1,0:T(8,128)(2,1)S(1)}, bf16[384,256]{1,0:T(8,128)(2,1)S(1)}, u32[]{:S(2)}, u32[]{:S(2)}) collective-permute-start(bf16[384,256]{1,0:T(8,128)(2,1)S(1)} %get-tuple-element.43), channel_id=1, source_target_pairs={{0,96},{32,0},{64,32},{96,64},{1,97},{33,1},{65,33},{97,65},{2,98}... | collective-permute-start | bytes 589832 | tf_op jit(solution)/shard_map/ppermute | solution.py:24
  98.7 10.1 %collective-permute-start.10 = (bf16[384,256]{1,0:T(8,128)(2,1)S(1)}, bf16[384,256]{1,0:T(8,128)(2,1)S(1)}, u32[]{:S(2)}, u32[]{:S(2)}) collective-permute-start(bf16[384,256]{1,0:T(8,128)(2,1)S(1)} %get-tuple-element.42), channel_id=1, source_target_pairs={{0,64},{32,96},{64,0},{96,32},{1,65},{33,97},{65,1},{97,33},{2,66}... | collective-permute-start | bytes 589832 | tf_op jit(solution)/shard_map/ppermute | solution.py:24
  99.9 13.1 %collective-permute-start.9 = (bf16[384,256]{1,0:T(8,128)(2,1)S(1)}, bf16[384,256]{1,0:T(8,128)(2,1)S(1)}, u32[]{:S(2)}, u32[]{:S(2)}) collective-permute-start(bf16[384,256]{1,0:T(8,128)(2,1)S(1)} %get-tuple-element.41), channel_id=1, source_target_pairs={{0,32},{32,64},{64,96},{96,0},{1,33},{33,65},{65,97},{97,1},{2,34}... | collective-permute-start | bytes 589832 | tf_op jit(solution)/shard_map/ppermute | solution.py:24
  107.0 8.4 %collective-permute-start.28 = (bf16[384,256]{1,0:T(8,128)(2,1)S(1)}, bf16[384,256]{1,0:T(8,128)(2,1)S(1)}, u32[]{:S(2)}, u32[]{:S(2)}) collective-permute-start(bf16[384,256]{1,0:T(8,128)(2,1)S(1)} %add_convert_fusion.4.refs_0_), channel_id=1, source_target_pairs={{0,4},{2,6},{4,0},{6,2},{1,5},{3,7},{5,1},{7,3},{8,12},{10,14},{12... | collective-permute-start | bytes 589832 | tf_op jit(solution)/shard_map/ppermute | solution.py:24
  113.1 11.1 %collective-permute-start.12 = (bf16[384,256]{1,0:T(8,128)(2,1)S(1)}, bf16[384,256]{1,0:T(8,128)(2,1)S(1)}, u32[]{:S(2)}, u32[]{:S(2)}) collective-permute-start(bf16[384,256]{1,0:T(8,128)(2,1)S(1)} %add_convert_fusion.6.refs_0_), channel_id=1, source_target_pairs={{0,2},{2,4},{4,6},{6,0},{1,3},{3,5},{5,7},{7,1},{8,10},{10,12},{12... | collective-permute-start | bytes 589832 | tf_op jit(solution)/shard_map/ppermute | solution.py:24
  113.8 13.7 %collective-permute-start.13 = (bf16[384,256]{1,0:T(8,128)(2,1)S(1)}, bf16[384,256]{1,0:T(8,128)(2,1)S(1)}, u32[]{:S(2)}, u32[]{:S(2)}) collective-permute-start(bf16[384,256]{1,0:T(8,128)(2,1)S(1)} %add_convert_fusion.6.refs_0_), channel_id=1, source_target_pairs={{0,4},{2,6},{4,0},{6,2},{1,5},{3,7},{5,1},{7,3},{8,12},{10,14},{12... | collective-permute-start | bytes 589832 | tf_op jit(solution)/shard_map/ppermute | solution.py:24
  115.4 12.1 %collective-permute-start.14 = (bf16[384,256]{1,0:T(8,128)(2,1)S(1)}, bf16[384,256]{1,0:T(8,128)(2,1)S(1)}, u32[]{:S(2)}, u32[]{:S(2)}) collective-permute-start(bf16[384,256]{1,0:T(8,128)(2,1)S(1)} %add_convert_fusion.6.refs_0_), channel_id=1, source_target_pairs={{0,6},{2,0},{4,2},{6,4},{1,7},{3,1},{5,3},{7,5},{8,14},{10,8},{12,... | collective-permute-start | bytes 589832 | tf_op jit(solution)/shard_map/ppermute | solution.py:24
  119.9 13.2 %collective-permute-start.32 = (bf16[384,256]{1,0:T(8,128)(2,1)S(1)}, bf16[384,256]{1,0:T(8,128)(2,1)S(1)}, u32[]{:S(2)}, u32[]{:S(2)}) collective-permute-start(bf16[384,256]{1,0:T(8,128)(2,1)S(1)} %get-tuple-element.55), channel_id=1, source_target_pairs={{0,24},{8,0},{16,8},{24,16},{1,25},{9,1},{17,9},{25,17},{2,26},{10... | collective-permute-start | bytes 589832 | tf_op jit(solution)/shard_map/ppermute | solution.py:24
  121.5 11.6 %collective-permute-start.31 = (bf16[384,256]{1,0:T(8,128)(2,1)S(1)}, bf16[384,256]{1,0:T(8,128)(2,1)S(1)}, u32[]{:S(2)}, u32[]{:S(2)}) collective-permute-start(bf16[384,256]{1,0:T(8,128)(2,1)S(1)} %get-tuple-element.54), channel_id=1, source_target_pairs={{0,16},{8,24},{16,0},{24,8},{1,17},{9,25},{17,1},{25,9},{2,18},{10... | collective-permute-start | bytes 589832 | tf_op jit(solution)/shard_map/ppermute | solution.py:24
  124.2 9.0 %collective-permute-start.30 = (bf16[384,256]{1,0:T(8,128)(2,1)S(1)}, bf16[384,256]{1,0:T(8,128)(2,1)S(1)}, u32[]{:S(2)}, u32[]{:S(2)}) collective-permute-start(bf16[384,256]{1,0:T(8,128)(2,1)S(1)} %get-tuple-element.53), channel_id=1, source_target_pairs={{0,8},{8,16},{16,24},{24,0},{1,9},{9,17},{17,25},{25,1},{2,10},{10... | collective-permute-start | bytes 589832 | tf_op jit(solution)/shard_map/ppermute | solution.py:24
  131.2 12.1 %collective-permute-start.18 = (bf16[384,256]{1,0:T(8,128)(2,1)S(1)}, bf16[384,256]{1,0:T(8,128)(2,1)S(1)}, u32[]{:S(2)}, u32[]{:S(2)}) collective-permute-start(bf16[384,256]{1,0:T(8,128)(2,1)S(1)} %get-tuple-element.47), channel_id=1, source_target_pairs={{0,24},{8,0},{16,8},{24,16},{1,25},{9,1},{17,9},{25,17},{2,26},{10... | collective-permute-start | bytes 589832 | tf_op jit(solution)/shard_map/ppermute | solution.py:24
  131.6 11.8 %collective-permute-start.17 = (bf16[384,256]{1,0:T(8,128)(2,1)S(1)}, bf16[384,256]{1,0:T(8,128)(2,1)S(1)}, u32[]{:S(2)}, u32[]{:S(2)}) collective-permute-start(bf16[384,256]{1,0:T(8,128)(2,1)S(1)} %get-tuple-element.46), channel_id=1, source_target_pairs={{0,16},{8,24},{16,0},{24,8},{1,17},{9,25},{17,1},{25,9},{2,18},{10... | collective-permute-start | bytes 589832 | tf_op jit(solution)/shard_map/ppermute | solution.py:24
  133.1 10.4 %collective-permute-start.16 = (bf16[384,256]{1,0:T(8,128)(2,1)S(1)}, bf16[384,256]{1,0:T(8,128)(2,1)S(1)}, u32[]{:S(2)}, u32[]{:S(2)}) collective-permute-start(bf16[384,256]{1,0:T(8,128)(2,1)S(1)} %get-tuple-element.45), channel_id=1, source_target_pairs={{0,8},{8,16},{16,24},{24,0},{1,9},{9,17},{17,25},{25,1},{2,10},{10... | collective-permute-start | bytes 589832 | tf_op jit(solution)/shard_map/ppermute | solution.py:24
  133.3 15.1 %collective-permute-start.33 = (bf16[192,256]{1,0:T(8,128)(2,1)S(1)}, bf16[192,256]{1,0:T(8,128)(2,1)S(1)}, u32[]{:S(2)}, u32[]{:S(2)}) collective-permute-start(bf16[192,256]{1,0:T(8,128)(2,1)S(1)} %get-tuple-element.122), channel_id=1, source_target_pairs={{0,1},{1,0},{2,3},{3,2},{4,5},{5,4},{6,7},{7,6},{8,9},{9,8},{10,11... | collective-permute-start | bytes 294920 | tf_op jit(solution)/shard_map/ppermute | solution.py:28
  152.5 12.0 %collective-permute-start.45 = (bf16[384,256]{1,0:T(8,128)(2,1)S(1)}, bf16[384,256]{1,0:T(8,128)(2,1)S(1)}, u32[]{:S(2)}, u32[]{:S(2)}) collective-permute-start(bf16[384,256]{1,0:T(8,128)(2,1)S(1)} %pad_maximum_fusion.7.refs_0_), channel_id=1, source_target_pairs={{0,8},{8,16},{16,24},{24,0},{1,9},{9,17},{17,25},{25,1},{2,10},{10... | collective-permute-start | bytes 589832 | tf_op jit(solution)/shard_map/ppermute | solution.py:24
  152.6 11.9 %collective-permute-start.46 = (bf16[384,256]{1,0:T(8,128)(2,1)S(1)}, bf16[384,256]{1,0:T(8,128)(2,1)S(1)}, u32[]{:S(2)}, u32[]{:S(2)}) collective-permute-start(bf16[384,256]{1,0:T(8,128)(2,1)S(1)} %pad_maximum_fusion.7.refs_0_), channel_id=1, source_target_pairs={{0,16},{8,24},{16,0},{24,8},{1,17},{9,25},{17,1},{25,9},{2,18},{10... | collective-permute-start | bytes 589832 | tf_op jit(solution)/shard_map/ppermute | solution.py:24
  154.1 10.7 %collective-permute-start.47 = (bf16[384,256]{1,0:T(8,128)(2,1)S(1)}, bf16[384,256]{1,0:T(8,128)(2,1)S(1)}, u32[]{:S(2)}, u32[]{:S(2)}) collective-permute-start(bf16[384,256]{1,0:T(8,128)(2,1)S(1)} %pad_maximum_fusion.7.refs_0_), channel_id=1, source_target_pairs={{0,24},{8,0},{16,8},{24,16},{1,25},{9,1},{17,9},{25,17},{2,26},{10... | collective-permute-start | bytes 589832 | tf_op jit(solution)/shard_map/ppermute | solution.py:24
  155.3 17.6 %collective-permute-start.35 = (bf16[384,256]{1,0:T(8,128)(2,1)S(1)}, bf16[384,256]{1,0:T(8,128)(2,1)S(1)}, u32[]{:S(2)}, u32[]{:S(2)}) collective-permute-start(bf16[384,256]{1,0:T(8,128)(2,1)S(1)} %pad_maximum_fusion.6.refs_0_), channel_id=1, source_target_pairs={{0,8},{8,16},{16,24},{24,0},{1,9},{9,17},{17,25},{25,1},{2,10},{10... | collective-permute-start | bytes 589832 | tf_op jit(solution)/shard_map/ppermute | solution.py:24
  155.9 17.0 %collective-permute-start.36 = (bf16[384,256]{1,0:T(8,128)(2,1)S(1)}, bf16[384,256]{1,0:T(8,128)(2,1)S(1)}, u32[]{:S(2)}, u32[]{:S(2)}) collective-permute-start(bf16[384,256]{1,0:T(8,128)(2,1)S(1)} %pad_maximum_fusion.6.refs_0_), channel_id=1, source_target_pairs={{0,16},{8,24},{16,0},{24,8},{1,17},{9,25},{17,1},{25,9},{2,18},{10... | collective-permute-start | bytes 589832 | tf_op jit(solution)/shard_map/ppermute | solution.py:24
  164.5 8.8 %collective-permute-start.37 = (bf16[384,256]{1,0:T(8,128)(2,1)S(1)}, bf16[384,256]{1,0:T(8,128)(2,1)S(1)}, u32[]{:S(2)}, u32[]{:S(2)}) collective-permute-start(bf16[384,256]{1,0:T(8,128)(2,1)S(1)} %pad_maximum_fusion.6.refs_0_), channel_id=1, source_target_pairs={{0,24},{8,0},{16,8},{24,16},{1,25},{9,1},{17,9},{25,17},{2,26},{10... | collective-permute-start | bytes 589832 | tf_op jit(solution)/shard_map/ppermute | solution.py:24
  167.9 13.4 %collective-permute-start.50 = (bf16[384,256]{1,0:T(8,128)(2,1)S(1)}, bf16[384,256]{1,0:T(8,128)(2,1)S(1)}, u32[]{:S(2)}, u32[]{:S(2)}) collective-permute-start(bf16[384,256]{1,0:T(8,128)(2,1)S(1)} %get-tuple-element.68), channel_id=1, source_target_pairs={{0,2},{2,4},{4,6},{6,0},{1,3},{3,5},{5,7},{7,1},{8,10},{10,12},{12... | collective-permute-start | bytes 589832 | tf_op jit(solution)/shard_map/ppermute | solution.py:24
  169.1 12.3 %collective-permute-start.49 = (bf16[384,256]{1,0:T(8,128)(2,1)S(1)}, bf16[384,256]{1,0:T(8,128)(2,1)S(1)}, u32[]{:S(2)}, u32[]{:S(2)}) collective-permute-start(bf16[384,256]{1,0:T(8,128)(2,1)S(1)} %get-tuple-element.67), channel_id=1, source_target_pairs={{0,4},{2,6},{4,0},{6,2},{1,5},{3,7},{5,1},{7,3},{8,12},{10,14},{12... | collective-permute-start | bytes 589832 | tf_op jit(solution)/shard_map/ppermute | solution.py:24
  172.9 8.4 %collective-permute-start.48 = (bf16[384,256]{1,0:T(8,128)(2,1)S(1)}, bf16[384,256]{1,0:T(8,128)(2,1)S(1)}, u32[]{:S(2)}, u32[]{:S(2)}) collective-permute-start(bf16[384,256]{1,0:T(8,128)(2,1)S(1)} %get-tuple-element.66), channel_id=1, source_target_pairs={{0,6},{2,0},{4,2},{6,4},{1,7},{3,1},{5,3},{7,5},{8,14},{10,8},{12,... | collective-permute-start | bytes 589832 | tf_op jit(solution)/shard_map/ppermute | solution.py:24
  176.4 7.9 %collective-permute-start.40 = (bf16[384,256]{1,0:T(8,128)(2,1)S(1)}, bf16[384,256]{1,0:T(8,128)(2,1)S(1)}, u32[]{:S(2)}, u32[]{:S(2)}) collective-permute-start(bf16[384,256]{1,0:T(8,128)(2,1)S(1)} %get-tuple-element.62), channel_id=1, source_target_pairs={{0,2},{2,4},{4,6},{6,0},{1,3},{3,5},{5,7},{7,1},{8,10},{10,12},{12... | collective-permute-start | bytes 589832 | tf_op jit(solution)/shard_map/ppermute | solution.py:24
  177.6 11.7 %collective-permute-start.39 = (bf16[384,256]{1,0:T(8,128)(2,1)S(1)}, bf16[384,256]{1,0:T(8,128)(2,1)S(1)}, u32[]{:S(2)}, u32[]{:S(2)}) collective-permute-start(bf16[384,256]{1,0:T(8,128)(2,1)S(1)} %get-tuple-element.61), channel_id=1, source_target_pairs={{0,4},{2,6},{4,0},{6,2},{1,5},{3,7},{5,1},{7,3},{8,12},{10,14},{12... | collective-permute-start | bytes 589832 | tf_op jit(solution)/shard_map/ppermute | solution.py:24
  181.3 8.0 %collective-permute-start.38 = (bf16[384,256]{1,0:T(8,128)(2,1)S(1)}, bf16[384,256]{1,0:T(8,128)(2,1)S(1)}, u32[]{:S(2)}, u32[]{:S(2)}) collective-permute-start(bf16[384,256]{1,0:T(8,128)(2,1)S(1)} %get-tuple-element.60), channel_id=1, source_target_pairs={{0,6},{2,0},{4,2},{6,4},{1,7},{3,1},{5,3},{7,5},{8,14},{10,8},{12,... | collective-permute-start | bytes 589832 | tf_op jit(solution)/shard_map/ppermute | solution.py:24
  181.5 9.0 %collective-permute-start.51 = (bf16[384,256]{1,0:T(8,128)(2,1)S(1)}, bf16[384,256]{1,0:T(8,128)(2,1)S(1)}, u32[]{:S(2)}, u32[]{:S(2)}) collective-permute-start(bf16[384,256]{1,0:T(8,128)(2,1)S(1)} %add_convert_fusion.1.refs_0_), channel_id=1, source_target_pairs={{0,32},{32,64},{64,96},{96,0},{1,33},{33,65},{65,97},{97,1},{2,34}... | collective-permute-start | bytes 589832 | tf_op jit(solution)/shard_map/ppermute | solution.py:24
  181.6 10.7 %collective-permute-start.52 = (bf16[384,256]{1,0:T(8,128)(2,1)S(1)}, bf16[384,256]{1,0:T(8,128)(2,1)S(1)}, u32[]{:S(2)}, u32[]{:S(2)}) collective-permute-start(bf16[384,256]{1,0:T(8,128)(2,1)S(1)} %add_convert_fusion.1.refs_0_), channel_id=1, source_target_pairs={{0,64},{32,96},{64,0},{96,32},{1,65},{33,97},{65,1},{97,33},{2,66}... | collective-permute-start | bytes 589832 | tf_op jit(solution)/shard_map/ppermute | solution.py:24
  184.4 7.9 %collective-permute-start.53 = (bf16[384,256]{1,0:T(8,128)(2,1)S(1)}, bf16[384,256]{1,0:T(8,128)(2,1)S(1)}, u32[]{:S(2)}, u32[]{:S(2)}) collective-permute-start(bf16[384,256]{1,0:T(8,128)(2,1)S(1)} %add_convert_fusion.1.refs_0_), channel_id=1, source_target_pairs={{0,96},{32,0},{64,32},{96,64},{1,97},{33,1},{65,33},{97,65},{2,98}... | collective-permute-start | bytes 589832 | tf_op jit(solution)/shard_map/ppermute | solution.py:24
  189.4 7.7 %collective-permute-start.41 = (bf16[384,256]{1,0:T(8,128)(2,1)S(1)}, bf16[384,256]{1,0:T(8,128)(2,1)S(1)}, u32[]{:S(2)}, u32[]{:S(2)}) collective-permute-start(bf16[384,256]{1,0:T(8,128)(2,1)S(1)} %add_convert_fusion.2.refs_0_), channel_id=1, source_target_pairs={{0,32},{32,64},{64,96},{96,0},{1,33},{33,65},{65,97},{97,1},{2,34}... | collective-permute-start | bytes 589832 | tf_op jit(solution)/shard_map/ppermute | solution.py:24
  189.5 9.4 %collective-permute-start.42 = (bf16[384,256]{1,0:T(8,128)(2,1)S(1)}, bf16[384,256]{1,0:T(8,128)(2,1)S(1)}, u32[]{:S(2)}, u32[]{:S(2)}) collective-permute-start(bf16[384,256]{1,0:T(8,128)(2,1)S(1)} %add_convert_fusion.2.refs_0_), channel_id=1, source_target_pairs={{0,64},{32,96},{64,0},{96,32},{1,65},{33,97},{65,1},{97,33},{2,66}... | collective-permute-start | bytes 589832 | tf_op jit(solution)/shard_map/ppermute | solution.py:24
  190.5 10.9 %collective-permute-start.43 = (bf16[384,256]{1,0:T(8,128)(2,1)S(1)}, bf16[384,256]{1,0:T(8,128)(2,1)S(1)}, u32[]{:S(2)}, u32[]{:S(2)}) collective-permute-start(bf16[384,256]{1,0:T(8,128)(2,1)S(1)} %add_convert_fusion.2.refs_0_), channel_id=1, source_target_pairs={{0,96},{32,0},{64,32},{96,64},{1,97},{33,1},{65,33},{97,65},{2,98}... | collective-permute-start | bytes 589832 | tf_op jit(solution)/shard_map/ppermute | solution.py:24
  (13 other events, 96.5 us)

commit v3 on v0

v3 whole, which is shorter than its diff:
```python
import functools

import jax
import jax.numpy as jnp
from jax import lax
from jax.experimental import pallas as pl
from jax.experimental.pallas import tpu as pltpu
from jax.sharding import Mesh, PartitionSpec as P

beta_first = 0.95
beta_second = 0.95
bias_first = 1.0 - 0.95**10
bias_second = 1.0 - 0.95**10
epsilon = 1e-08
learn_rate = 0.02
weight_decay = 0.1

RING = 4
CHUNKS = 2
bf16 = jnp.bfloat16
f32 = jnp.float32
VMEM_LIMIT = 40 * 1024 * 1024


def shift(value, axis, distance):
    return lax.ppermute(value, axis, [(i, (i + distance) % RING) for i in range(RING)])


def swap(value):
    return lax.ppermute(value, "core", [(0, 1), (1, 0)])


def gather(value, axis):
    return [value] + [shift(value, axis, d) for d in (1, 2, 3)]


def spread(parts, axis, sign=1):
    return [parts[0]] + [shift(parts[d], axis, sign * d) for d in (1, 2, 3)]


def shape(rows, columns, kind=bf16):
    return jax.ShapeDtypeStruct((rows, columns), kind)


def call(kernel, place, operands, outs, flops=0, scratch=(), after=()):
    def body(place, *refs):
        kernel(place, *refs[: len(operands)], *refs[len(operands) + len(after) :])

    moved = sum(a.size * a.dtype.itemsize for a in operands)
    moved += sum(s.size * jnp.dtype(s.dtype).itemsize for s in outs)
    return pl.pallas_call(
        body,
        out_shape=outs,
        in_specs=[pl.BlockSpec(memory_space=pltpu.SMEM)]
        + [pl.BlockSpec(memory_space=pltpu.VMEM)] * len(operands)
        + [pl.BlockSpec(memory_space=pl.ANY)] * len(after),
        out_specs=[pl.BlockSpec(memory_space=pltpu.VMEM)] * len(outs),
        scratch_shapes=list(scratch),
        cost_estimate=pl.CostEstimate(flops=flops, bytes_accessed=moved, transcendentals=0),
        compiler_params=pltpu.CompilerParams(vmem_limit_bytes=VMEM_LIMIT),
    )(place, *operands, *after)


def at(index, width):
    return pl.ds(pl.multiple_of(lax.rem(index + RING, RING) * width, width), width)


def side(which, width):
    return pl.ds(pl.multiple_of(which * width, width), width)


def strips_kernel(place, value, out):
    width = out.shape[2] // RING
    for k in range(RING):
        for j in range(RING):
            start = (j * RING + k) * width
            out[k, :, j * width : (j + 1) * width] = value[:, start : start + width]


def lend_kernel(place, value, out):
    out[...] = value[:, side(1 - place[3], out.shape[1])]


def join_kernel(place, value, arrived, *outs):
    rows, width = value.shape[0], outs[0].shape[1]
    for chunk, out in enumerate(outs):
        out[:rows] = value[:, side(place[3] * CHUNKS + chunk, width)]
        out[rows:] = arrived[:, chunk * width : (chunk + 1) * width]


def stack_kernel(place, own, arrived, out):
    rows = own.shape[0]
    out[side(place[3], rows)] = own[...]
    out[side(1 - place[3], rows)] = arrived[...]


def left_kernel(place, *refs):
    pieces, left, left_other = refs[:RING], refs[RING], refs[RING + 1]
    outs, stack, stack_other = refs[RING + 2 : 2 * RING + 2], refs[-2], refs[-1]
    rows, chunk = pieces[0].shape[0] // 2, outs[0].shape[0]
    for d in range(RING):
        stack[at(place[2] - d, rows)] = pieces[d][:rows]
        stack_other[at(place[2] - d, rows)] = pieces[d][rows:]
    over = (((0,), (0,)), ((), ()))
    for d in range(RING):
        columns = at(place[1] + d, chunk)
        value = lax.dot_general(stack[...], left[:, columns], over, preferred_element_type=f32)
        value += lax.dot_general(
            stack_other[...], left_other[:, columns], over, preferred_element_type=f32
        )
        outs[d][...] = value.T.astype(bf16)


def sum_kernel(absolute, place, *refs):
    pieces, own, other = refs[:RING], refs[RING], refs[RING + 1]
    rows = own.shape[0]
    for k, out in enumerate((own, other)):
        which = k + place[3] * (1 - 2 * k) if absolute else k
        lines = side(which, rows) if absolute else slice(k * rows, (k + 1) * rows)
        out[...] = sum(piece[lines].astype(f32) for piece in pieces).astype(bf16)


def right_kernel(place, *refs):
    own, arrived, basis = refs[:CHUNKS], refs[CHUNKS : 2 * CHUNKS], refs[2 * CHUNKS]
    outs, rows = refs[2 * CHUNKS + 1 : -1], refs[-1]
    width = own[0].shape[1]
    for chunk in range(CHUNKS):
        rows[:, side(place[3] * CHUNKS + chunk, width)] = own[chunk][...]
        rows[:, side((1 - place[3]) * CHUNKS + chunk, width)] = arrived[chunk][...]
    for chunk in range(CHUNKS):
        for d in range(RING):
            for core in range(2):
                block = (lax.rem(place[0] + d, RING) * 2 + core) * CHUNKS + chunk
                outs[chunk * RING + d][:, core * width : (core + 1) * width] = jnp.dot(
                    rows[...], basis[:, side(block, width)], preferred_element_type=f32
                ).astype(bf16)


def moment_kernel(place, *refs):
    pieces, one, two = refs[:RING], refs[RING], refs[RING + 1]
    new_one, new_two, kept, lent = refs[-4:]
    core = pl.program_id(0)
    rotated = sum(piece[...].astype(f32) for piece in pieces)
    first = beta_first * one[...] + (1.0 - beta_first) * rotated
    second = beta_second * two[...] + (1.0 - beta_second) * rotated * rotated
    new_one[...] = first
    new_two[...] = second
    normed = (first / bias_first / (jnp.sqrt(second / bias_second) + epsilon)).astype(bf16)

    @pl.when(core == place[3])
    def _():
        kept[...] = normed

    @pl.when(core != place[3])
    def _():
        lent[...] = normed


def moments(place, chunk, pieces, one, two, so_far):
    rows, width = pieces[0].shape[0], pieces[0].shape[1] // 2
    piece = pl.BlockSpec((rows, width), lambda core, place: (0, core))
    part = pl.BlockSpec((rows, width), lambda core, place: (0, core * CHUNKS + chunk))
    whole = pl.BlockSpec((rows, width), lambda core, place: (0, 0))
    return pl.pallas_call(
        moment_kernel,
        out_shape=[shape(*one.shape, f32)] * 2 + [shape(rows, width)] * 2,
        grid_spec=pltpu.PrefetchScalarGridSpec(
            num_scalar_prefetch=1,
            grid=(2,),
            in_specs=[piece] * RING + [part, part] + [pl.BlockSpec(memory_space=pl.ANY)] * len(so_far),
            out_specs=[part, part, whole, whole],
        ),
        input_output_aliases={RING + 3: 0, RING + 4: 1} if so_far else {},
        compiler_params=pltpu.CompilerParams(vmem_limit_bytes=VMEM_LIMIT),
    )(place, *pieces, one, two, *so_far)


def back_kernel(place, *refs):
    pieces, left, left_other = refs[:RING], refs[RING], refs[RING + 1]
    outs, stack = refs[RING + 2 : 2 * RING + 2], refs[-1]
    chunk = pieces[0].shape[0]
    rows = chunk // 2
    for d in range(RING):
        stack[at(place[1] - d, chunk)] = pieces[d][...]
    for d in range(RING):
        lines = at(place[2] - d, rows)
        outs[d][:rows] = jnp.dot(left[lines], stack[...], preferred_element_type=f32).astype(bf16)
        outs[d][rows:] = jnp.dot(
            left_other[lines], stack[...], preferred_element_type=f32
        ).astype(bf16)


def beside_kernel(place, own, arrived, out):
    width = own.shape[1]
    out[:, side(place[3], width)] = own[...]
    out[:, side(1 - place[3], width)] = arrived[...]


def final_kernel(chunk, place, *refs):
    pieces, basis = refs[:RING], refs[RING]
    width = pieces[0].shape[1] // 2
    over = (((1,), (1,)), ((), ()))
    value = None
    for d in range(RING):
        for core in range(2):
            block = (lax.rem(place[0] - d + RING, RING) * 2 + core) * CHUNKS + chunk
            term = lax.dot_general(
                pieces[d][:, core * width : (core + 1) * width],
                basis[:, side(block, width)],
                over,
                preferred_element_type=f32,
            )
            value = term if value is None else value + term
    rest = refs[RING + 1 :]
    if chunk > 0:
        value = value + rest[0][...]
        rest = rest[1:]
    if chunk == CHUNKS - 1:
        weights, new_weights, update = rest
        update[...] = value
        new_weights[...] = weights[...] - learn_rate * (value + weight_decay * weights[...])
    else:
        rest[0][...] = value


def per_device(grad_parts, weights, moment_one, moment_two, left_basis, right_basis):
    place = jnp.stack([lax.axis_index(name) for name in ("x", "z", "y", "core")]).astype(jnp.int32)
    rows, features = left_basis.shape
    columns = weights.shape[1]
    half = columns // 2
    width = half // CHUNKS
    strip = features // RING
    both = 2 * rows

    (parts,) = call(strips_kernel, place, [left_basis], [jax.ShapeDtypeStruct((RING, rows, strip), bf16)])
    left = lax.all_to_all(parts, "y", 0, 0, tiled=True).reshape(RING * rows, strip)
    left_other = swap(left)

    gradient = lax.psum_scatter(grad_parts[0], "x", scatter_dimension=1, tiled=True)
    (lent,) = call(lend_kernel, place, [gradient], [shape(rows, half)])
    chunks = call(
        join_kernel, place, [gradient, swap(lent)], [shape(both, width)] * CHUNKS
    )
    basis = lax.all_gather(right_basis, ("z", "y", "core"), axis=0, tiled=True)

    kept, arrived = [], []
    for value in chunks:
        parts = call(
            left_kernel,
            place,
            [*gather(value, "y"), left, left_other],
            [shape(both, width)] * RING,
            4 * left.size * width,
            [pltpu.VMEM((RING * rows, width), bf16)] * 2,
        )
        own, other = call(
            functools.partial(sum_kernel, True), place, spread(parts, "z"), [shape(rows, width)] * 2
        )
        kept.append(own)
        arrived.append(swap(other))

    parts = call(
        right_kernel,
        place,
        [*kept, *arrived, basis],
        [shape(rows, 2 * width)] * (RING * CHUNKS),
        2 * rows * columns * RING * columns,
        [pltpu.VMEM((rows, columns), bf16)],
    )
    so_far, chunks = (), []
    for chunk in range(CHUNKS):
        pieces = spread(parts[chunk * RING : (chunk + 1) * RING], "x")
        *so_far, own, lent = moments(place, chunk, pieces, moment_one, moment_two, so_far)
        chunks.append(call(stack_kernel, place, [own, swap(lent)], [shape(both, width)])[0])
    new_one, new_two = so_far

    so_far = []
    for chunk, value in enumerate(chunks):
        parts = call(
            back_kernel,
            place,
            [*gather(value, "z"), left, left_other],
            [shape(both, width)] * RING,
            4 * left.size * width,
            [pltpu.VMEM((strip, width), bf16)],
        )
        own, other = call(
            functools.partial(sum_kernel, False), place, spread(parts, "y", -1), [shape(rows, width)] * 2
        )
        (value,) = call(beside_kernel, place, [own, swap(other)], [shape(rows, 2 * width)])
        last = chunk == CHUNKS - 1
        so_far = call(
            functools.partial(final_kernel, chunk),
            place,
            [*gather(value, "x"), basis, *so_far, *([weights] if last else [])],
            [shape(rows, columns, f32)] * (2 if last else 1),
            2 * rows * basis.size // CHUNKS,
        )
    new_weights, update = so_far
    return (new_weights, new_one, new_two, update)


def solution(mesh):
    grid = Mesh(mesh.devices.reshape(RING, RING, RING, 2), ("x", "z", "y", "core"))
    fsdp = ("z", "y", "core")
    placed = P(fsdp, "x")
    return jax.shard_map(
        per_device,
        mesh=grid,
        in_specs=(
            P("x", fsdp, None),
            placed,
            placed,
            placed,
            P(fsdp, None),
            P(("x", *fsdp), None),
        ),
        out_specs=(placed, placed, placed, placed),
        check_vma=False,
    )
```

time: 326 us -> 203 us (0.62)
  waiting for transfers between devices: 278 us -> 51.5 us
  starting transfers between devices: 0.25 us -> 60.3 us
  blocking collectives: 0 us -> 37.3 us
  Pallas kernels: 0 us -> 32 us
  matrix products: 29.5 us -> 0 us
  local copies, waits for them, and re-layouts: 0.02 us -> 6.07 us
    reduce_scatter x3 -> x1, waiting for transfers between devices: 161 us -> 0.01 us  [per_device(): lax.psum_scatter(grad_parts[0], 'x', scatter_dimension=1, tiled=True)]
    all_gather x3 -> x1, waiting for transfers between devices: 116 us -> 0.01 us  [per_device(): basis = lax.all_gather(right_basis, ('z', 'y', 'core'), axis=0, tiled=True)]
    ppermute x0 -> x44, starting transfers between devices: none -> 60.2 us  [the longest x36 51.1 us: shift(): lax.ppermute(value, axis, [(i, (i + distance) % RING) for i in range(RING)])]
    ppermute x0 -> x44, waiting for transfers between devices: none -> 50.3 us  [the longest x36 43.7 us: shift(): lax.ppermute(value, axis, [(i, (i + distance) % RING) for i in range(RING)])]
    all_to_all x0 -> x1, blocking collectives: none -> 37.3 us  [per_device(): lax.all_to_all(parts, 'y', 0, 0, tiled=True).reshape(RING * rows, strip)]
    pallas_call x0 -> x20, Pallas kernels: none -> 32 us  [the longest x18 28.1 us: call(): pl.pallas_call(body, out_shape=outs, in_specs=[pl.BlockSpec(memory_space=...]
    dot_general x4 -> x0, matrix products: 29.5 us -> none  [the longest x1 8.12 us: per_device(): lax.dot_general(full_rows, basis_block, (((1,), (1,)), ((), ())), preferr...]
    unnamed x6 -> x16, local copies, waits for them, and re-layouts: 0.02 us -> 6.07 us
  transfers between devices with their start and end apart: 6 -> 46, of which waited for: 6 -> 19; matrix products, arithmetic and copies ran while one was open for 2% -> 0% of each run, Pallas kernels for 0% -> 13%
where the time goes in v3:
time: 203 us
  starting transfers between devices  60.3 us (30%)
  waiting for transfers between devices  51.5 us (25%)
  blocking collectives  37.3 us (18%)
  Pallas kernels  32 us (16%)
  between operations  15.7 us (8%)
  local copies, waits for them, and re-layouts  6.07 us (3%)
    ppermute x36, starting transfers between devices, shift(): lax.ppermute(value, axis, [(i, (i + distance) % RING) for i in range(RING)])  51.1 us
    ppermute x36, waiting for transfers between devices, shift(): lax.ppermute(value, axis, [(i, (i + distance) % RING) for i in range(RING)])  43.7 us
    all_to_all x1, blocking collectives, per_device(): lax.all_to_all(parts, 'y', 0, 0, tiled=True).reshape(RING * rows, strip)  37.3 us
    pallas_call x18, Pallas kernels, call(): pl.pallas_call(body, out_shape=outs, in_specs=[pl.BlockSpec(memory_space=...  28.1 us
    ppermute x8, starting transfers between devices, swap(): return lax.ppermute(value, 'core', [(0, 1), (1, 0)])  9.05 us
    ppermute x8, waiting for transfers between devices, swap(): return lax.ppermute(value, 'core', [(0, 1), (1, 0)])  6.63 us
    unnamed x16, local copies, waits for them, and re-layouts  6.07 us
  transfers between devices with their start and end apart: 46, of which 19 were waited for; matrix products, arithmetic and copies ran while one was open for 0% of the time, Pallas kernels for 13%

profile of v3, /device:TPU:1, one launch (start us, length us, event | category | flops | bytes accessed | tf_op | source)
XLA Modules:
  0.0 202.9 jit_solution(9866978974602804261)
XLA Ops:
  9.4 1.7 copy-done.3
  11.8 37.3 %all_to_all.5 = bf16[4,192,1536]{2,1,0:T(8,128)(2,1)S(1)} all-to-all(bf16[4,192,1536]{2,1,0:T(8,128)(2,1)S(1)} %shard_map.95), channel_id=1, replica_groups=mesh['x'=4,'z'=4,'y'=4,'core'=2] {'y'}, dimensions={0} | all-to-all | bytes 4718592 | tf_op jit(solution)/shard_map/all_to_all | solution.py:236
  49.1 1.9 collective-permute-start.4
  52.6 2.9 %collective-permute-done.refs_1_ = bf16[192,512]{1,0:T(8,128)(2,1)S(1)} collective-permute-done((bf16[192,512]{1,0:T(8,128)(2,1)S(1)}, bf16[192,512]{1,0:T(8,128)(2,1)S(1)}, u32[]{:S(2)}, u32[]{:S(2)}) %collective-permute-start) | collective-permute-done | bytes 196640 | tf_op jit(solution)/shard_map/ppermute | solution.py:30
  57.8 2.2 %collective-permute-start.10 = (bf16[384,256]{1,0:T(8,128)(2,1)S(1)}, bf16[384,256]{1,0:T(8,128)(2,1)S(1)}, u32[]{:S(2)}, u32[]{:S(2)}) collective-permute-start(bf16[384,256]{1,0:T(8,128)(2,1)S(1)} %get-tuple-element.54.refs_0_), channel_id=1, source_target_pairs={{0,6},{2,0},{4,2},{6,4},{1,7},{3,1},{5,3},{7,5},{8,14},{10,8},{12,... | collective-permute-start | bytes 589832 | tf_op jit(solution)/shard_map/ppermute | solution.py:26
  60.0 6.7 %collective-permute-done.3.refs_3_ = bf16[384,256]{1,0:T(8,128)(2,1)S(1)} collective-permute-done((bf16[384,256]{1,0:T(8,128)(2,1)S(1)}, bf16[384,256]{1,0:T(8,128)(2,1)S(1)}, u32[]{:S(2)}, u32[]{:S(2)}) %collective-permute-start.3) | collective-permute-done | bytes 196640 | tf_op jit(solution)/shard_map/ppermute | solution.py:26
  66.7 1.3 collective-permute-start.9
  68.0 1.6 collective-permute-done.2.refs_2_
  69.6 6.1 %collective-permute-start.8 = (bf16[384,256]{1,0:T(8,128)(2,1)S(1)}, bf16[384,256]{1,0:T(8,128)(2,1)S(1)}, u32[]{:S(2)}, u32[]{:S(2)}) collective-permute-start(bf16[384,256]{1,0:T(8,128)(2,1)S(1)} %get-tuple-element.54.refs_0_), channel_id=1, source_target_pairs={{0,2},{2,4},{4,6},{6,0},{1,3},{3,5},{5,7},{7,1},{8,10},{10,12},{12... | collective-permute-start | bytes 589832 | tf_op jit(solution)/shard_map/ppermute | solution.py:26
  75.7 3.7 %shard_map.96 = (bf16[384,256]{1,0:T(8,128)(2,1)S(1)}, bf16[384,256]{1,0:T(8,128)(2,1)S(1)}, bf16[384,256]{1,0:T(8,128)(2,1)S(1)}, bf16[384,256]{1,0:T(8,128)(2,1)S(1)}) custom-call(s32[4]{0:T(128)S(1)} %pad_add_fusion.place, bf16[384,256]{1,0:T(8,128)(2,1)S(1)} %get-tuple-element.48.refs_0_, bf16[384,256]{1,0:T(8,128)(2,1)S(1)} %collective-permute-done.1.refs_1_, ...), custom_call_target="tpu_custom_call" | custom-call | flops 1207959552 | bytes 6291456 | tf_op jit(solution)/shard_map/pallas_call | solution.py:51
  79.4 1.4 collective-permute-start.5
  80.8 4.3 %collective-permute-start.6 = (bf16[384,256]{1,0:T(8,128)(2,1)S(1)}, bf16[384,256]{1,0:T(8,128)(2,1)S(1)}, u32[]{:S(2)}, u32[]{:S(2)}) collective-permute-start(bf16[384,256]{1,0:T(8,128)(2,1)S(1)} %get-tuple-element.51), channel_id=1, source_target_pairs={{0,16},{8,24},{16,0},{24,8},{1,17},{9,25},{17,1},{25,9},{2,18},{10... | collective-permute-start | bytes 589832 | tf_op jit(solution)/shard_map/ppermute | solution.py:26
  86.9 3.7 %shard_map.98 = (bf16[384,256]{1,0:T(8,128)(2,1)S(1)}, bf16[384,256]{1,0:T(8,128)(2,1)S(1)}, bf16[384,256]{1,0:T(8,128)(2,1)S(1)}, bf16[384,256]{1,0:T(8,128)(2,1)S(1)}) custom-call(s32[4]{0:T(128)S(1)} %pad_add_fusion.place, bf16[384,256]{1,0:T(8,128)(2,1)S(1)} %get-tuple-element.54.refs_0_, bf16[384,256]{1,0:T(8,128)(2,1)S(1)} %collective-permute-done.8.refs_1_, ...), custom_call_target="tpu_custom_call" | custom-call | flops 1207959552 | bytes 6291456 | tf_op jit(solution)/shard_map/pallas_call | solution.py:51
  90.6 1.5 collective-permute-start.11
  92.1 2.6 %collective-permute-start.12 = (bf16[384,256]{1,0:T(8,128)(2,1)S(1)}, bf16[384,256]{1,0:T(8,128)(2,1)S(1)}, u32[]{:S(2)}, u32[]{:S(2)}) collective-permute-start(bf16[384,256]{1,0:T(8,128)(2,1)S(1)} %get-tuple-element.57), channel_id=1, source_target_pairs={{0,16},{8,24},{16,0},{24,8},{1,17},{9,25},{17,1},{25,9},{2,18},{10... | collective-permute-start | bytes 589832 | tf_op jit(solution)/shard_map/ppermute | solution.py:26
  96.4 1.4 collective-permute-start.14
  97.8 5.6 %collective-permute-done.12.refs_2_ = bf16[384,256]{1,0:T(8,128)(2,1)S(1)} collective-permute-done((bf16[384,256]{1,0:T(8,128)(2,1)S(1)}, bf16[384,256]{1,0:T(8,128)(2,1)S(1)}, u32[]{:S(2)}, u32[]{:S(2)}) %collective-permute-start.12) | collective-permute-done | bytes 196640 | tf_op jit(solution)/shard_map/ppermute | solution.py:26
  104.0 1.4 collective-permute-start.15
  106.4 3.4 %copy-done = bf16[1024,4096]{1,0:T(8,128)(2,1)S(1)} copy-done((bf16[1024,4096]{1,0:T(8,128)(2,1)S(1)}, bf16[1024,4096]{1,0:T(8,128)(2,1)}, u32[]{:S(2)}) %copy-start) | copy-done | bytes 8388632
  109.8 2.4 %shard_map.100 = (bf16[192,512]{1,0:T(8,128)(2,1)S(1)}, bf16[192,512]{1,0:T(8,128)(2,1)S(1)}, bf16[192,512]{1,0:T(8,128)(2,1)S(1)}, bf16[192,512]{1,0:T(8,128)(2...) custom-call(s32[4]{0:T(128)S(1)} %pad_add_fusion.place, ...), custom_call_target="tpu_custom_call" | custom-call | flops 1610612736 | bytes 10354688 | tf_op jit(solution)/shard_map/pallas_call | solution.py:51
  112.2 1.4 collective-permute-start.19
  113.6 2.4 %collective-permute-start.20 = (bf16[192,512]{1,0:T(8,128)(2,1)S(1)}, bf16[192,512]{1,0:T(8,128)(2,1)S(1)}, u32[]{:S(2)}, u32[]{:S(2)}) collective-permute-start(bf16[192,512]{1,0:T(8,128)(2,1)S(1)} %get-tuple-element.68), channel_id=1, source_target_pairs={{0,64},{32,96},{64,0},{96,32},{1,65},{33,97},{65,1},{97,33},{2,66}... | collective-permute-start | bytes 589832 | tf_op jit(solution)/shard_map/ppermute | solution.py:26
  116.1 1.2 collective-permute-start.21
  118.4 1.4 collective-permute-done.19.refs_1_
  119.8 1.2 collective-permute-start.18
  121.0 4.0 %collective-permute-done.20.refs_2_ = bf16[192,512]{1,0:T(8,128)(2,1)S(1)} collective-permute-done((bf16[192,512]{1,0:T(8,128)(2,1)S(1)}, bf16[192,512]{1,0:T(8,128)(2,1)S(1)}, u32[]{:S(2)}, u32[]{:S(2)}) %collective-permute-start.20) | collective-permute-done | bytes 196640 | tf_op jit(solution)/shard_map/ppermute | solution.py:26
  125.0 1.9 shard_map.101
  126.9 1.9 collective-permute-start.33
  130.4 2.0 collective-permute-start.36
  133.6 1.9 shard_map.102
  135.5 1.2 collective-permute-start.22
  138.3 2.3 %collective-permute-start.25 = (bf16[384,256]{1,0:T(8,128)(2,1)S(1)}, bf16[384,256]{1,0:T(8,128)(2,1)S(1)}, u32[]{:S(2)}, u32[]{:S(2)}) collective-permute-start(bf16[384,256]{1,0:T(8,128)(2,1)S(1)} %shard_map.103.refs_0_), channel_id=1, source_target_pairs={{0,24},{8,0},{16,8},{24,16},{1,25},{9,1},{17,9},{25,17},{2,26},{10... | collective-permute-start | bytes 589832 | tf_op jit(solution)/shard_map/ppermute | solution.py:26
  141.5 3.4 %collective-permute-done.34.refs_1_ = bf16[384,256]{1,0:T(8,128)(2,1)S(1)} collective-permute-done((bf16[384,256]{1,0:T(8,128)(2,1)S(1)}, bf16[384,256]{1,0:T(8,128)(2,1)S(1)}, u32[]{:S(2)}, u32[]{:S(2)}) %collective-permute-start.34) | collective-permute-done | bytes 196640 | tf_op jit(solution)/shard_map/ppermute | solution.py:26
  144.9 3.1 %shard_map.108 = (bf16[384,256]{1,0:T(8,128)(2,1)S(1)}, bf16[384,256]{1,0:T(8,128)(2,1)S(1)}, bf16[384,256]{1,0:T(8,128)(2,1)S(1)}, bf16[384,256]{1,0:T(8,128)(2,1)S(1)}) custom-call(s32[4]{0:T(128)S(1)} %pad_add_fusion.place, bf16[384,256]{1,0:T(8,128)(2,1)S(1)} %shard_map.107.refs_0_, bf16[384,256]{1,0:T(8,128)(2,1)S(1)} %collective-permute-done.34.refs_1_, ...), custom_call_target="tpu_custom_call" | custom-call | flops 1207959552 | bytes 6291456 | tf_op jit(solution)/shard_map/pallas_call | solution.py:51
  148.9 1.2 collective-permute-start.38
  150.6 2.8 %collective-permute-done.23.refs_1_ = bf16[384,256]{1,0:T(8,128)(2,1)S(1)} collective-permute-done((bf16[384,256]{1,0:T(8,128)(2,1)S(1)}, bf16[384,256]{1,0:T(8,128)(2,1)S(1)}, u32[]{:S(2)}, u32[]{:S(2)}) %collective-permute-start.23) | collective-permute-done | bytes 196640 | tf_op jit(solution)/shard_map/ppermute | solution.py:26
  153.3 3.1 %shard_map.104 = (bf16[384,256]{1,0:T(8,128)(2,1)S(1)}, bf16[384,256]{1,0:T(8,128)(2,1)S(1)}, bf16[384,256]{1,0:T(8,128)(2,1)S(1)}, bf16[384,256]{1,0:T(8,128)(2,1)S(1)}) custom-call(s32[4]{0:T(128)S(1)} %pad_add_fusion.place, bf16[384,256]{1,0:T(8,128)(2,1)S(1)} %shard_map.103.refs_0_, bf16[384,256]{1,0:T(8,128)(2,1)S(1)} %collective-permute-done.23.refs_1_, ...), custom_call_target="tpu_custom_call" | custom-call | flops 1207959552 | bytes 6291456 | tf_op jit(solution)/shard_map/pallas_call | solution.py:51
  157.4 1.2 collective-permute-start.27
  159.1 2.4 %collective-permute-done.39.refs_3_ = bf16[384,256]{1,0:T(8,128)(2,1)S(1)} collective-permute-done((bf16[384,256]{1,0:T(8,128)(2,1)S(1)}, bf16[384,256]{1,0:T(8,128)(2,1)S(1)}, u32[]{:S(2)}, u32[]{:S(2)}) %collective-permute-start.39) | collective-permute-done | bytes 196640 | tf_op jit(solution)/shard_map/ppermute | solution.py:26
  164.2 2.5 %collective-permute-start.43 = (bf16[192,512]{1,0:T(8,128)(2,1)S(1)}, bf16[192,512]{1,0:T(8,128)(2,1)S(1)}, u32[]{:S(2)}, u32[]{:S(2)}) collective-permute-start(bf16[192,512]{1,0:T(8,128)(2,1)S(1)} %shard_map.110.refs_0_), channel_id=1, source_target_pairs={{0,96},{32,0},{64,32},{96,64},{1,97},{33,1},{65,33},{97,65},{2,98}... | collective-permute-start | bytes 589832 | tf_op jit(solution)/shard_map/ppermute | solution.py:26
  166.7 3.2 %collective-permute-done.28.refs_3_ = bf16[384,256]{1,0:T(8,128)(2,1)S(1)} collective-permute-done((bf16[384,256]{1,0:T(8,128)(2,1)S(1)}, bf16[384,256]{1,0:T(8,128)(2,1)S(1)}, u32[]{:S(2)}, u32[]{:S(2)}) %collective-permute-start.28) | collective-permute-done | bytes 196640 | tf_op jit(solution)/shard_map/ppermute | solution.py:26
  171.1 2.6 %collective-permute-start.42 = (bf16[192,512]{1,0:T(8,128)(2,1)S(1)}, bf16[192,512]{1,0:T(8,128)(2,1)S(1)}, u32[]{:S(2)}, u32[]{:S(2)}) collective-permute-start(bf16[192,512]{1,0:T(8,128)(2,1)S(1)} %shard_map.110.refs_0_), channel_id=1, source_target_pairs={{0,64},{32,96},{64,0},{96,32},{1,65},{33,97},{65,1},{97,33},{2,66}... | collective-permute-start | bytes 589832 | tf_op jit(solution)/shard_map/ppermute | solution.py:26
  174.7 2.4 %collective-permute-start.32 = (bf16[192,512]{1,0:T(8,128)(2,1)S(1)}, bf16[192,512]{1,0:T(8,128)(2,1)S(1)}, u32[]{:S(2)}, u32[]{:S(2)}) collective-permute-start(bf16[192,512]{1,0:T(8,128)(2,1)S(1)} %shard_map.106.refs_0_), channel_id=1, source_target_pairs={{0,96},{32,0},{64,32},{96,64},{1,97},{33,1},{65,33},{97,65},{2,98}... | collective-permute-start | bytes 589832 | tf_op jit(solution)/shard_map/ppermute | solution.py:26
  179.1 5.0 %collective-permute-done.41.refs_1_ = bf16[192,512]{1,0:T(8,128)(2,1)S(1)} collective-permute-done((bf16[192,512]{1,0:T(8,128)(2,1)S(1)}, bf16[192,512]{1,0:T(8,128)(2,1)S(1)}, u32[]{:S(2)}, u32[]{:S(2)}) %collective-permute-start.41) | collective-permute-done | bytes 196640 | tf_op jit(solution)/shard_map/ppermute | solution.py:26
  184.1 2.1 %shard_map.111.refs_5_ = f32[192,1024]{1,0:T(8,128)S(1)} custom-call(s32[4]{0:T(128)S(1)} %pad_add_fusion.place, bf16[192,512]{1,0:T(8,128)(2,1)S(1)} %shard_map.110.refs_0_, bf16[192,512]{1,0:T(8,128)(2,1)S(1)} %collective-permute-done.41.refs_1_, bf16[192,512]{1,0:T(8,128)(2,1)S(1)} %collective-permute-done.42.refs_2_, ...), custom_call_target="tpu_custom_call" | custom-call | flops 805306368 | bytes 9961472 | tf_op jit(solution)/shard_map/pallas_call | solution.py:51
  186.2 1.4 collective-permute-done.31.refs_2_
  187.6 4.6 %collective-permute-done.30.refs_1_ = bf16[192,512]{1,0:T(8,128)(2,1)S(1)} collective-permute-done((bf16[192,512]{1,0:T(8,128)(2,1)S(1)}, bf16[192,512]{1,0:T(8,128)(2,1)S(1)}, u32[]{:S(2)}, u32[]{:S(2)}) %collective-permute-start.30) | collective-permute-done | bytes 196640 | tf_op jit(solution)/shard_map/ppermute | solution.py:26
  192.1 3.3 %shard_map.112 = (f32[192,1024]{1,0:T(8,128)}, f32[192,1024]{1,0:T(8,128)}) custom-call(s32[4]{0:T(128)S(1)} %pad_add_fusion.place, bf16[192,512]{1,0:T(8,128)(2,1)S(1)} %shard_map.106.refs_0_, bf16[192,512]{1,0:T(8,128)(2,1)S(1)} %collective-permute-done.30.refs_1_, bf16[192,512]{1,0:T(8,128)(2,1)S(1)} %collective-permute-done.31.refs_2_, ...), custom_call_target="tpu_custom_call" | custom-call | flops 805306368 | bytes 12320768 | tf_op jit(solution)/shard_map/pallas_call | solution.py:51
  (85 shorter events, 27.0 us)
Async XLA Ops:
  8.0 43.0 %reduce-scatter.2.cloned.1.call-start = ((), (), s32[]{:S(2)}) async-start(), calls=%async_computation.2 | async-start | bytes 1966080 | tf_op jit(solution)/shard_map/reduce_scatter | solution.py:239
  8.7 97.7 %all-gather.2.cloned.1.call-start = ((), (), s32[]{:S(2)}) async-start(), calls=%async_computation.3 | async-start | bytes 8650752 | tf_op jit(solution)/shard_map/all_gather | solution.py:244
  49.1 26.6 %collective-permute-start.4 = (bf16[768,1536]{1,0:T(8,128)(2,1)S(1)}, bf16[768,1536]{1,0:T(8,128)(2,1)}, u32[]{:S(2)}, u32[]{:S(2)}) collective-permute-start(bf16[768,1536]{1,0:T(8,128)(2,1)S(1)} %bitcast.8), channel_id=1, source_target_pairs={{0,1},{1,0},{2,3},{3,2},{4,5},{5,4},{6,7},{7,6},{8,9},{9,8},{10,11... | collective-permute-start | bytes 7077896 | tf_op jit(solution)/shard_map/ppermute | solution.py:30
  52.5 2.9 %collective-permute-start = (bf16[192,512]{1,0:T(8,128)(2,1)S(1)}, bf16[192,512]{1,0:T(8,128)(2,1)S(1)}, u32[]{:S(2)}, u32[]{:S(2)}) collective-permute-start(bf16[192,512]{1,0:T(8,128)(2,1)S(1)} %shard_map.93), channel_id=1, source_target_pairs={{0,1},{1,0},{2,3},{3,2},{4,5},{5,4},{6,7},{7,6},{8,9},{9,8},{10,11... | collective-permute-start | bytes 589832 | tf_op jit(solution)/shard_map/ppermute | solution.py:30
  56.0 10.7 %collective-permute-start.3 = (bf16[384,256]{1,0:T(8,128)(2,1)S(1)}, bf16[384,256]{1,0:T(8,128)(2,1)S(1)}, u32[]{:S(2)}, u32[]{:S(2)}) collective-permute-start(bf16[384,256]{1,0:T(8,128)(2,1)S(1)} %get-tuple-element.48.refs_0_), channel_id=1, source_target_pairs={{0,6},{2,0},{4,2},{6,4},{1,7},{3,1},{5,3},{7,5},{8,14},{10,8},{12,... | collective-permute-start | bytes 589832 | tf_op jit(solution)/shard_map/ppermute | solution.py:26
  57.1 12.5 %collective-permute-start.2 = (bf16[384,256]{1,0:T(8,128)(2,1)S(1)}, bf16[384,256]{1,0:T(8,128)(2,1)S(1)}, u32[]{:S(2)}, u32[]{:S(2)}) collective-permute-start(bf16[384,256]{1,0:T(8,128)(2,1)S(1)} %get-tuple-element.48.refs_0_), channel_id=1, source_target_pairs={{0,4},{2,6},{4,0},{6,2},{1,5},{3,7},{5,1},{7,3},{8,12},{10,14},{12... | collective-permute-start | bytes 589832 | tf_op jit(solution)/shard_map/ppermute | solution.py:26
  57.3 18.4 %collective-permute-start.1 = (bf16[384,256]{1,0:T(8,128)(2,1)S(1)}, bf16[384,256]{1,0:T(8,128)(2,1)S(1)}, u32[]{:S(2)}, u32[]{:S(2)}) collective-permute-start(bf16[384,256]{1,0:T(8,128)(2,1)S(1)} %get-tuple-element.48.refs_0_), channel_id=1, source_target_pairs={{0,2},{2,4},{4,6},{6,0},{1,3},{3,5},{5,7},{7,1},{8,10},{10,12},{12... | collective-permute-start | bytes 589832 | tf_op jit(solution)/shard_map/ppermute | solution.py:26
  57.8 27.4 %collective-permute-start.10 = (bf16[384,256]{1,0:T(8,128)(2,1)S(1)}, bf16[384,256]{1,0:T(8,128)(2,1)S(1)}, u32[]{:S(2)}, u32[]{:S(2)}) collective-permute-start(bf16[384,256]{1,0:T(8,128)(2,1)S(1)} %get-tuple-element.54.refs_0_), channel_id=1, source_target_pairs={{0,6},{2,0},{4,2},{6,4},{1,7},{3,1},{5,3},{7,5},{8,14},{10,8},{12,... | collective-permute-start | bytes 589832 | tf_op jit(solution)/shard_map/ppermute | solution.py:26
  66.7 19.2 %collective-permute-start.9 = (bf16[384,256]{1,0:T(8,128)(2,1)S(1)}, bf16[384,256]{1,0:T(8,128)(2,1)S(1)}, u32[]{:S(2)}, u32[]{:S(2)}) collective-permute-start(bf16[384,256]{1,0:T(8,128)(2,1)S(1)} %get-tuple-element.54.refs_0_), channel_id=1, source_target_pairs={{0,4},{2,6},{4,0},{6,2},{1,5},{3,7},{5,1},{7,3},{8,12},{10,14},{12... | collective-permute-start | bytes 589832 | tf_op jit(solution)/shard_map/ppermute | solution.py:26
  69.6 17.3 %collective-permute-start.8 = (bf16[384,256]{1,0:T(8,128)(2,1)S(1)}, bf16[384,256]{1,0:T(8,128)(2,1)S(1)}, u32[]{:S(2)}, u32[]{:S(2)}) collective-permute-start(bf16[384,256]{1,0:T(8,128)(2,1)S(1)} %get-tuple-element.54.refs_0_), channel_id=1, source_target_pairs={{0,2},{2,4},{4,6},{6,0},{1,3},{3,5},{5,7},{7,1},{8,10},{10,12},{12... | collective-permute-start | bytes 589832 | tf_op jit(solution)/shard_map/ppermute | solution.py:26
  79.4 15.2 %collective-permute-start.5 = (bf16[384,256]{1,0:T(8,128)(2,1)S(1)}, bf16[384,256]{1,0:T(8,128)(2,1)S(1)}, u32[]{:S(2)}, u32[]{:S(2)}) collective-permute-start(bf16[384,256]{1,0:T(8,128)(2,1)S(1)} %get-tuple-element.50), channel_id=1, source_target_pairs={{0,8},{8,16},{16,24},{24,0},{1,9},{9,17},{17,25},{25,1},{2,10},{10... | collective-permute-start | bytes 589832 | tf_op jit(solution)/shard_map/ppermute | solution.py:26
  80.8 14.9 %collective-permute-start.6 = (bf16[384,256]{1,0:T(8,128)(2,1)S(1)}, bf16[384,256]{1,0:T(8,128)(2,1)S(1)}, u32[]{:S(2)}, u32[]{:S(2)}) collective-permute-start(bf16[384,256]{1,0:T(8,128)(2,1)S(1)} %get-tuple-element.51), channel_id=1, source_target_pairs={{0,16},{8,24},{16,0},{24,8},{1,17},{9,25},{17,1},{25,9},{2,18},{10... | collective-permute-start | bytes 589832 | tf_op jit(solution)/shard_map/ppermute | solution.py:26
  85.2 10.5 %collective-permute-start.7 = (bf16[384,256]{1,0:T(8,128)(2,1)S(1)}, bf16[384,256]{1,0:T(8,128)(2,1)S(1)}, u32[]{:S(2)}, u32[]{:S(2)}) collective-permute-start(bf16[384,256]{1,0:T(8,128)(2,1)S(1)} %get-tuple-element.52), channel_id=1, source_target_pairs={{0,24},{8,0},{16,8},{24,16},{1,25},{9,1},{17,9},{25,17},{2,26},{10... | collective-permute-start | bytes 589832 | tf_op jit(solution)/shard_map/ppermute | solution.py:26
  90.6 7.2 %collective-permute-start.11 = (bf16[384,256]{1,0:T(8,128)(2,1)S(1)}, bf16[384,256]{1,0:T(8,128)(2,1)S(1)}, u32[]{:S(2)}, u32[]{:S(2)}) collective-permute-start(bf16[384,256]{1,0:T(8,128)(2,1)S(1)} %get-tuple-element.56), channel_id=1, source_target_pairs={{0,8},{8,16},{16,24},{24,0},{1,9},{9,17},{17,25},{25,1},{2,10},{10... | collective-permute-start | bytes 589832 | tf_op jit(solution)/shard_map/ppermute | solution.py:26
  92.1 11.3 %collective-permute-start.12 = (bf16[384,256]{1,0:T(8,128)(2,1)S(1)}, bf16[384,256]{1,0:T(8,128)(2,1)S(1)}, u32[]{:S(2)}, u32[]{:S(2)}) collective-permute-start(bf16[384,256]{1,0:T(8,128)(2,1)S(1)} %get-tuple-element.57), channel_id=1, source_target_pairs={{0,16},{8,24},{16,0},{24,8},{1,17},{9,25},{17,1},{25,9},{2,18},{10... | collective-permute-start | bytes 589832 | tf_op jit(solution)/shard_map/ppermute | solution.py:26
  94.6 8.7 %collective-permute-start.13 = (bf16[384,256]{1,0:T(8,128)(2,1)S(1)}, bf16[384,256]{1,0:T(8,128)(2,1)S(1)}, u32[]{:S(2)}, u32[]{:S(2)}) collective-permute-start(bf16[384,256]{1,0:T(8,128)(2,1)S(1)} %get-tuple-element.58), channel_id=1, source_target_pairs={{0,24},{8,0},{16,8},{24,16},{1,25},{9,1},{17,9},{25,17},{2,26},{10... | collective-permute-start | bytes 589832 | tf_op jit(solution)/shard_map/ppermute | solution.py:26
  96.4 9.1 %collective-permute-start.14 = (bf16[192,256]{1,0:T(8,128)(2,1)S(1)}, bf16[192,256]{1,0:T(8,128)(2,1)S(1)}, u32[]{:S(2)}, u32[]{:S(2)}) collective-permute-start(bf16[192,256]{1,0:T(8,128)(2,1)S(1)} %get-tuple-element.60), channel_id=1, source_target_pairs={{0,1},{1,0},{2,3},{3,2},{4,5},{5,4},{6,7},{7,6},{8,9},{9,8},{10,11... | collective-permute-start | bytes 294920 | tf_op jit(solution)/shard_map/ppermute | solution.py:30
  104.0 2.4 %collective-permute-start.15 = (bf16[192,256]{1,0:T(8,128)(2,1)S(1)}, bf16[192,256]{1,0:T(8,128)(2,1)S(1)}, u32[]{:S(2)}, u32[]{:S(2)}) collective-permute-start(bf16[192,256]{1,0:T(8,128)(2,1)S(1)} %get-tuple-element.61), channel_id=1, source_target_pairs={{0,1},{1,0},{2,3},{3,2},{4,5},{5,4},{6,7},{7,6},{8,9},{9,8},{10,11... | collective-permute-start | bytes 294920 | tf_op jit(solution)/shard_map/ppermute | solution.py:30
  112.2 7.6 %collective-permute-start.19 = (bf16[192,512]{1,0:T(8,128)(2,1)S(1)}, bf16[192,512]{1,0:T(8,128)(2,1)S(1)}, u32[]{:S(2)}, u32[]{:S(2)}) collective-permute-start(bf16[192,512]{1,0:T(8,128)(2,1)S(1)} %get-tuple-element.67), channel_id=1, source_target_pairs={{0,32},{32,64},{64,96},{96,0},{1,33},{33,65},{65,97},{97,1},{2,34}... | collective-permute-start | bytes 589832 | tf_op jit(solution)/shard_map/ppermute | solution.py:26
  113.6 11.4 %collective-permute-start.20 = (bf16[192,512]{1,0:T(8,128)(2,1)S(1)}, bf16[192,512]{1,0:T(8,128)(2,1)S(1)}, u32[]{:S(2)}, u32[]{:S(2)}) collective-permute-start(bf16[192,512]{1,0:T(8,128)(2,1)S(1)} %get-tuple-element.68), channel_id=1, source_target_pairs={{0,64},{32,96},{64,0},{96,32},{1,65},{33,97},{65,1},{97,33},{2,66}... | collective-permute-start | bytes 589832 | tf_op jit(solution)/shard_map/ppermute | solution.py:26
  116.1 8.9 %collective-permute-start.21 = (bf16[192,512]{1,0:T(8,128)(2,1)S(1)}, bf16[192,512]{1,0:T(8,128)(2,1)S(1)}, u32[]{:S(2)}, u32[]{:S(2)}) collective-permute-start(bf16[192,512]{1,0:T(8,128)(2,1)S(1)} %get-tuple-element.69), channel_id=1, source_target_pairs={{0,96},{32,0},{64,32},{96,64},{1,97},{33,1},{65,33},{97,65},{2,98}... | collective-permute-start | bytes 589832 | tf_op jit(solution)/shard_map/ppermute | solution.py:26
  117.2 16.0 %collective-permute-start.16 = (bf16[192,512]{1,0:T(8,128)(2,1)S(1)}, bf16[192,512]{1,0:T(8,128)(2,1)S(1)}, u32[]{:S(2)}, u32[]{:S(2)}) collective-permute-start(bf16[192,512]{1,0:T(8,128)(2,1)S(1)} %get-tuple-element.63), channel_id=1, source_target_pairs={{0,32},{32,64},{64,96},{96,0},{1,33},{33,65},{65,97},{97,1},{2,34}... | collective-permute-start | bytes 589832 | tf_op jit(solution)/shard_map/ppermute | solution.py:26
  117.5 16.1 %collective-permute-start.17 = (bf16[192,512]{1,0:T(8,128)(2,1)S(1)}, bf16[192,512]{1,0:T(8,128)(2,1)S(1)}, u32[]{:S(2)}, u32[]{:S(2)}) collective-permute-start(bf16[192,512]{1,0:T(8,128)(2,1)S(1)} %get-tuple-element.64), channel_id=1, source_target_pairs={{0,64},{32,96},{64,0},{96,32},{1,65},{33,97},{65,1},{97,33},{2,66}... | collective-permute-start | bytes 589832 | tf_op jit(solution)/shard_map/ppermute | solution.py:26
  119.8 13.8 %collective-permute-start.18 = (bf16[192,512]{1,0:T(8,128)(2,1)S(1)}, bf16[192,512]{1,0:T(8,128)(2,1)S(1)}, u32[]{:S(2)}, u32[]{:S(2)}) collective-permute-start(bf16[192,512]{1,0:T(8,128)(2,1)S(1)} %get-tuple-element.65), channel_id=1, source_target_pairs={{0,96},{32,0},{64,32},{96,64},{1,97},{33,1},{65,33},{97,65},{2,98}... | collective-permute-start | bytes 589832 | tf_op jit(solution)/shard_map/ppermute | solution.py:26
  126.9 2.9 %collective-permute-start.33 = (bf16[192,256]{1,0:T(8,128)(2,1)S(1)}, bf16[192,256]{1,0:T(8,128)(2,1)S(1)}, u32[]{:S(2)}, u32[]{:S(2)}) collective-permute-start(bf16[192,256]{1,0:T(8,128)(2,1)S(1)} %get-tuple-element.81), channel_id=1, source_target_pairs={{0,1},{1,0},{2,3},{3,2},{4,5},{5,4},{6,7},{7,6},{8,9},{9,8},{10,11... | collective-permute-start | bytes 294920 | tf_op jit(solution)/shard_map/ppermute | solution.py:30
  130.4 11.1 %collective-permute-start.36 = (bf16[384,256]{1,0:T(8,128)(2,1)S(1)}, bf16[384,256]{1,0:T(8,128)(2,1)S(1)}, u32[]{:S(2)}, u32[]{:S(2)}) collective-permute-start(bf16[384,256]{1,0:T(8,128)(2,1)S(1)} %shard_map.107.refs_0_), channel_id=1, source_target_pairs={{0,24},{8,0},{16,8},{24,16},{1,25},{9,1},{17,9},{25,17},{2,26},{10... | collective-permute-start | bytes 589832 | tf_op jit(solution)/shard_map/ppermute | solution.py:26
  132.3 9.2 %collective-permute-start.35 = (bf16[384,256]{1,0:T(8,128)(2,1)S(1)}, bf16[384,256]{1,0:T(8,128)(2,1)S(1)}, u32[]{:S(2)}, u32[]{:S(2)}) collective-permute-start(bf16[384,256]{1,0:T(8,128)(2,1)S(1)} %shard_map.107.refs_0_), channel_id=1, source_target_pairs={{0,16},{8,24},{16,0},{24,8},{1,17},{9,25},{17,1},{25,9},{2,18},{10... | collective-permute-start | bytes 589832 | tf_op jit(solution)/shard_map/ppermute | solution.py:26
  133.2 11.7 %collective-permute-start.34 = (bf16[384,256]{1,0:T(8,128)(2,1)S(1)}, bf16[384,256]{1,0:T(8,128)(2,1)S(1)}, u32[]{:S(2)}, u32[]{:S(2)}) collective-permute-start(bf16[384,256]{1,0:T(8,128)(2,1)S(1)} %shard_map.107.refs_0_), channel_id=1, source_target_pairs={{0,8},{8,16},{16,24},{24,0},{1,9},{9,17},{17,25},{25,1},{2,10},{10... | collective-permute-start | bytes 589832 | tf_op jit(solution)/shard_map/ppermute | solution.py:26
  133.6 50.5 %slice-start = ((s8[8388608]{0:T(1024)(128)(4,1)}), s8[4194304]{0:T(1024)(128)(4,1)S(1)}, s32[]{:S(2)}) async-start(s8[8388608]{0:T(1024)(128)(4,1)} %bitcast.6), calls=%async_computation.4 | async-start | bytes 8388608
  135.5 2.1 %collective-permute-start.22 = (bf16[192,256]{1,0:T(8,128)(2,1)S(1)}, bf16[192,256]{1,0:T(8,128)(2,1)S(1)}, u32[]{:S(2)}, u32[]{:S(2)}) collective-permute-start(bf16[192,256]{1,0:T(8,128)(2,1)S(1)} %get-tuple-element.73), channel_id=1, source_target_pairs={{0,1},{1,0},{2,3},{3,2},{4,5},{5,4},{6,7},{7,6},{8,9},{9,8},{10,11... | collective-permute-start | bytes 294920 | tf_op jit(solution)/shard_map/ppermute | solution.py:30
  138.3 45.9 %slice-start.1 = ((s8[8388608]{0:T(1024)(128)(4,1)}), s8[4194304]{0:T(1024)(128)(4,1)S(1)}, s32[]{:S(2)}) async-start(s8[8388608]{0:T(1024)(128)(4,1)} %bitcast.6), calls=%async_computation.5 | async-start | bytes 8388608
  138.3 11.9 %collective-permute-start.25 = (bf16[384,256]{1,0:T(8,128)(2,1)S(1)}, bf16[384,256]{1,0:T(8,128)(2,1)S(1)}, u32[]{:S(2)}, u32[]{:S(2)}) collective-permute-start(bf16[384,256]{1,0:T(8,128)(2,1)S(1)} %shard_map.103.refs_0_), channel_id=1, source_target_pairs={{0,24},{8,0},{16,8},{24,16},{1,25},{9,1},{17,9},{25,17},{2,26},{10... | collective-permute-start | bytes 589832 | tf_op jit(solution)/shard_map/ppermute | solution.py:26
  140.6 10.0 %collective-permute-start.24 = (bf16[384,256]{1,0:T(8,128)(2,1)S(1)}, bf16[384,256]{1,0:T(8,128)(2,1)S(1)}, u32[]{:S(2)}, u32[]{:S(2)}) collective-permute-start(bf16[384,256]{1,0:T(8,128)(2,1)S(1)} %shard_map.103.refs_0_), channel_id=1, source_target_pairs={{0,16},{8,24},{16,0},{24,8},{1,17},{9,25},{17,1},{25,9},{2,18},{10... | collective-permute-start | bytes 589832 | tf_op jit(solution)/shard_map/ppermute | solution.py:26
  141.5 11.8 %collective-permute-start.23 = (bf16[384,256]{1,0:T(8,128)(2,1)S(1)}, bf16[384,256]{1,0:T(8,128)(2,1)S(1)}, u32[]{:S(2)}, u32[]{:S(2)}) collective-permute-start(bf16[384,256]{1,0:T(8,128)(2,1)S(1)} %shard_map.103.refs_0_), channel_id=1, source_target_pairs={{0,8},{8,16},{16,24},{24,0},{1,9},{9,17},{17,25},{25,1},{2,10},{10... | collective-permute-start | bytes 589832 | tf_op jit(solution)/shard_map/ppermute | solution.py:26
  148.0 10.6 %collective-permute-start.37 = (bf16[384,256]{1,0:T(8,128)(2,1)S(1)}, bf16[384,256]{1,0:T(8,128)(2,1)S(1)}, u32[]{:S(2)}, u32[]{:S(2)}) collective-permute-start(bf16[384,256]{1,0:T(8,128)(2,1)S(1)} %get-tuple-element.83), channel_id=1, source_target_pairs={{0,6},{2,0},{4,2},{6,4},{1,7},{3,1},{5,3},{7,5},{8,14},{10,8},{12,... | collective-permute-start | bytes 589832 | tf_op jit(solution)/shard_map/ppermute | solution.py:26
  148.9 10.2 %collective-permute-start.38 = (bf16[384,256]{1,0:T(8,128)(2,1)S(1)}, bf16[384,256]{1,0:T(8,128)(2,1)S(1)}, u32[]{:S(2)}, u32[]{:S(2)}) collective-permute-start(bf16[384,256]{1,0:T(8,128)(2,1)S(1)} %get-tuple-element.84), channel_id=1, source_target_pairs={{0,4},{2,6},{4,0},{6,2},{1,5},{3,7},{5,1},{7,3},{8,12},{10,14},{12... | collective-permute-start | bytes 589832 | tf_op jit(solution)/shard_map/ppermute | solution.py:26
  150.1 11.3 %collective-permute-start.39 = (bf16[384,256]{1,0:T(8,128)(2,1)S(1)}, bf16[384,256]{1,0:T(8,128)(2,1)S(1)}, u32[]{:S(2)}, u32[]{:S(2)}) collective-permute-start(bf16[384,256]{1,0:T(8,128)(2,1)S(1)} %get-tuple-element.85), channel_id=1, source_target_pairs={{0,2},{2,4},{4,6},{6,0},{1,3},{3,5},{5,7},{7,1},{8,10},{10,12},{12... | collective-permute-start | bytes 589832 | tf_op jit(solution)/shard_map/ppermute | solution.py:26
  156.5 10.2 %collective-permute-start.26 = (bf16[384,256]{1,0:T(8,128)(2,1)S(1)}, bf16[384,256]{1,0:T(8,128)(2,1)S(1)}, u32[]{:S(2)}, u32[]{:S(2)}) collective-permute-start(bf16[384,256]{1,0:T(8,128)(2,1)S(1)} %get-tuple-element.75), channel_id=1, source_target_pairs={{0,6},{2,0},{4,2},{6,4},{1,7},{3,1},{5,3},{7,5},{8,14},{10,8},{12,... | collective-permute-start | bytes 589832 | tf_op jit(solution)/shard_map/ppermute | solution.py:26
  157.4 9.3 %collective-permute-start.27 = (bf16[384,256]{1,0:T(8,128)(2,1)S(1)}, bf16[384,256]{1,0:T(8,128)(2,1)S(1)}, u32[]{:S(2)}, u32[]{:S(2)}) collective-permute-start(bf16[384,256]{1,0:T(8,128)(2,1)S(1)} %get-tuple-element.76), channel_id=1, source_target_pairs={{0,4},{2,6},{4,0},{6,2},{1,5},{3,7},{5,1},{7,3},{8,12},{10,14},{12... | collective-permute-start | bytes 589832 | tf_op jit(solution)/shard_map/ppermute | solution.py:26
  158.6 11.3 %collective-permute-start.28 = (bf16[384,256]{1,0:T(8,128)(2,1)S(1)}, bf16[384,256]{1,0:T(8,128)(2,1)S(1)}, u32[]{:S(2)}, u32[]{:S(2)}) collective-permute-start(bf16[384,256]{1,0:T(8,128)(2,1)S(1)} %get-tuple-element.77), channel_id=1, source_target_pairs={{0,2},{2,4},{4,6},{6,0},{1,3},{3,5},{5,7},{7,1},{8,10},{10,12},{12... | collective-permute-start | bytes 589832 | tf_op jit(solution)/shard_map/ppermute | solution.py:26
  162.1 1.5 collective-permute-start.40
  164.2 13.4 %collective-permute-start.43 = (bf16[192,512]{1,0:T(8,128)(2,1)S(1)}, bf16[192,512]{1,0:T(8,128)(2,1)S(1)}, u32[]{:S(2)}, u32[]{:S(2)}) collective-permute-start(bf16[192,512]{1,0:T(8,128)(2,1)S(1)} %shard_map.110.refs_0_), channel_id=1, source_target_pairs={{0,96},{32,0},{64,32},{96,64},{1,97},{33,1},{65,33},{97,65},{2,98}... | collective-permute-start | bytes 589832 | tf_op jit(solution)/shard_map/ppermute | solution.py:26
  170.6 3.6 %collective-permute-start.29 = (bf16[192,256]{1,0:T(8,128)(2,1)S(1)}, bf16[192,256]{1,0:T(8,128)(2,1)S(1)}, u32[]{:S(2)}, u32[]{:S(2)}) collective-permute-start(bf16[192,256]{1,0:T(8,128)(2,1)S(1)} %get-tuple-element.79), channel_id=1, source_target_pairs={{0,1},{1,0},{2,3},{3,2},{4,5},{5,4},{6,7},{7,6},{8,9},{9,8},{10,11... | collective-permute-start | bytes 294920 | tf_op jit(solution)/shard_map/ppermute | solution.py:30
  171.1 8.0 %collective-permute-start.42 = (bf16[192,512]{1,0:T(8,128)(2,1)S(1)}, bf16[192,512]{1,0:T(8,128)(2,1)S(1)}, u32[]{:S(2)}, u32[]{:S(2)}) collective-permute-start(bf16[192,512]{1,0:T(8,128)(2,1)S(1)} %shard_map.110.refs_0_), channel_id=1, source_target_pairs={{0,64},{32,96},{64,0},{96,32},{1,65},{33,97},{65,1},{97,33},{2,66}... | collective-permute-start | bytes 589832 | tf_op jit(solution)/shard_map/ppermute | solution.py:26
  173.8 10.3 %collective-permute-start.41 = (bf16[192,512]{1,0:T(8,128)(2,1)S(1)}, bf16[192,512]{1,0:T(8,128)(2,1)S(1)}, u32[]{:S(2)}, u32[]{:S(2)}) collective-permute-start(bf16[192,512]{1,0:T(8,128)(2,1)S(1)} %shard_map.110.refs_0_), channel_id=1, source_target_pairs={{0,32},{32,64},{64,96},{96,0},{1,33},{33,65},{65,97},{97,1},{2,34}... | collective-permute-start | bytes 589832 | tf_op jit(solution)/shard_map/ppermute | solution.py:26
  174.7 11.4 %collective-permute-start.32 = (bf16[192,512]{1,0:T(8,128)(2,1)S(1)}, bf16[192,512]{1,0:T(8,128)(2,1)S(1)}, u32[]{:S(2)}, u32[]{:S(2)}) collective-permute-start(bf16[192,512]{1,0:T(8,128)(2,1)S(1)} %shard_map.106.refs_0_), channel_id=1, source_target_pairs={{0,96},{32,0},{64,32},{96,64},{1,97},{33,1},{65,33},{97,65},{2,98}... | collective-permute-start | bytes 589832 | tf_op jit(solution)/shard_map/ppermute | solution.py:26
  177.1 10.5 %collective-permute-start.31 = (bf16[192,512]{1,0:T(8,128)(2,1)S(1)}, bf16[192,512]{1,0:T(8,128)(2,1)S(1)}, u32[]{:S(2)}, u32[]{:S(2)}) collective-permute-start(bf16[192,512]{1,0:T(8,128)(2,1)S(1)} %shard_map.106.refs_0_), channel_id=1, source_target_pairs={{0,64},{32,96},{64,0},{96,32},{1,65},{33,97},{65,1},{97,33},{2,66}... | collective-permute-start | bytes 589832 | tf_op jit(solution)/shard_map/ppermute | solution.py:26
  177.6 14.5 %collective-permute-start.30 = (bf16[192,512]{1,0:T(8,128)(2,1)S(1)}, bf16[192,512]{1,0:T(8,128)(2,1)S(1)}, u32[]{:S(2)}, u32[]{:S(2)}) collective-permute-start(bf16[192,512]{1,0:T(8,128)(2,1)S(1)} %shard_map.106.refs_0_), channel_id=1, source_target_pairs={{0,32},{32,64},{64,96},{96,0},{1,33},{33,65},{65,97},{97,1},{2,34}... | collective-permute-start | bytes 589832 | tf_op jit(solution)/shard_map/ppermute | solution.py:26
  (6 other events, 53.9 us)
Sparse Core Ops, SparseCore 0:
  11.2 27.8 reduce-scatter.1
Sparse Core Ops, SparseCore 1:
  11.5 73.4 all-gather.1

commit v4 on v3

--- a/solution.py
+++ b/solution.py
@@ -75,6 +75,16 @@
         for j in range(RING):
             start = (j * RING + k) * width
             out[k, :, j * width : (j + 1) * width] = value[:, start : start + width]
+
+
+def held(value, after):
+    return pl.pallas_call(
+        lambda *refs: None,
+        out_shape=jax.ShapeDtypeStruct(value.shape, value.dtype),
+        in_specs=[pl.BlockSpec(memory_space=pl.ANY)] * (1 + len(after)),
+        out_specs=pl.BlockSpec(memory_space=pl.ANY),
+        input_output_aliases={0: 0},
+    )(value, *after)
 
 
 def lend_kernel(place, value, out):
@@ -234,14 +244,16 @@
 
     (parts,) = call(strips_kernel, place, [left_basis], [jax.ShapeDtypeStruct((RING, rows, strip), bf16)])
     left = lax.all_to_all(parts, "y", 0, 0, tiled=True).reshape(RING * rows, strip)
-    left_other = swap(left)
 
     gradient = lax.psum_scatter(grad_parts[0], "x", scatter_dimension=1, tiled=True)
-    (lent,) = call(lend_kernel, place, [gradient], [shape(rows, half)])
+    (lent,) = call(lend_kernel, place, [gradient], [shape(rows, half)], after=[left])
     chunks = call(
         join_kernel, place, [gradient, swap(lent)], [shape(both, width)] * CHUNKS
     )
     basis = lax.all_gather(right_basis, ("z", "y", "core"), axis=0, tiled=True)
+
+    left = held(left, chunks[:1])
+    left_other = swap(left)
 
     kept, arrived = [], []
     for value in chunks:

time: 203 us -> 202 us (level)
  Pallas kernels: 32 us -> 27.4 us
  starting transfers between devices: 60.3 us -> 64.1 us
  waiting for transfers between devices: 51.5 us -> 48 us
  local copies, waits for them, and re-layouts: 6.07 us -> 9.26 us
    pallas_call x18, Pallas kernels: 28.1 us -> 23.6 us  [call(): pl.pallas_call(body, out_shape=outs, in_specs=[pl.BlockSpec(memory_space=...]
    ppermute x36, starting transfers between devices: 51.1 us -> 54.6 us  [shift(): lax.ppermute(value, axis, [(i, (i + distance) % RING) for i in range(RING)])]
    unnamed x16 -> x26, local copies, waits for them, and re-layouts: 6.07 us -> 9.26 us
  transfers between devices with their start and end apart: 46 -> 46, of which waited for: 19 -> 20; matrix products, arithmetic and copies ran while one was open for 0% -> 0% of each run, Pallas kernels for 13% -> 11%
where the time goes in v4:
time: 202 us
  starting transfers between devices  64.1 us (32%)
  waiting for transfers between devices  48 us (24%)
  blocking collectives  37.3 us (18%)
  Pallas kernels  27.4 us (14%)
  between operations  15.7 us (8%)
  local copies, waits for them, and re-layouts  9.26 us (5%)
    ppermute x36, starting transfers between devices, shift(): lax.ppermute(value, axis, [(i, (i + distance) % RING) for i in range(RING)])  54.6 us
    ppermute x36, waiting for transfers between devices, shift(): lax.ppermute(value, axis, [(i, (i + distance) % RING) for i in range(RING)])  42 us
    all_to_all x1, blocking collectives, per_device(): lax.all_to_all(parts, 'y', 0, 0, tiled=True).reshape(RING * rows, strip)  37.3 us
    pallas_call x18, Pallas kernels, call(): pl.pallas_call(body, out_shape=outs, in_specs=[pl.BlockSpec(memory_space=...  23.6 us
    ppermute x8, starting transfers between devices, swap(): return lax.ppermute(value, 'core', [(0, 1), (1, 0)])  9.46 us
    unnamed x26, local copies, waits for them, and re-layouts  9.26 us
    ppermute x8, waiting for transfers between devices, swap(): return lax.ppermute(value, 'core', [(0, 1), (1, 0)])  4.85 us
  transfers between devices with their start and end apart: 46, of which 20 were waited for; matrix products, arithmetic and copies ran while one was open for 0% of the time, Pallas kernels for 11%

profile of v4, /device:TPU:1, one launch (start us, length us, event | category | flops | bytes accessed | tf_op | source)
XLA Modules:
  0.0 201.8 jit_solution(13007018227605632873)
XLA Ops:
  9.4 1.7 copy-done.6
  11.8 37.3 %all_to_all.5 = bf16[4,192,1536]{2,1,0:T(8,128)(2,1)S(1)} all-to-all(bf16[4,192,1536]{2,1,0:T(8,128)(2,1)S(1)} %shard_map.93), channel_id=1, replica_groups=mesh['x'=4,'z'=4,'y'=4,'core'=2] {'y'}, dimensions={0} | all-to-all | bytes 4718592 | tf_op jit(solution)/shard_map/all_to_all | solution.py:246
  49.1 1.3 copy-done.7
  50.9 1.9 collective-permute-start
  58.3 2.7 %collective-permute-start.10 = (bf16[384,256]{1,0:T(8,128)(2,1)S(1)}, bf16[384,256]{1,0:T(8,128)(2,1)S(1)}, u32[]{:S(2)}, u32[]{:S(2)}) collective-permute-start(bf16[384,256]{1,0:T(8,128)(2,1)S(1)} %get-tuple-element.54.refs_0_), channel_id=1, source_target_pairs={{0,6},{2,0},{4,2},{6,4},{1,7},{3,1},{5,3},{7,5},{8,14},{10,8},{12,... | collective-permute-start | bytes 589832 | tf_op jit(solution)/shard_map/ppermute | solution.py:26
  60.9 5.7 %collective-permute-done.3.refs_3_ = bf16[384,256]{1,0:T(8,128)(2,1)S(1)} collective-permute-done((bf16[384,256]{1,0:T(8,128)(2,1)S(1)}, bf16[384,256]{1,0:T(8,128)(2,1)S(1)}, u32[]{:S(2)}, u32[]{:S(2)}) %collective-permute-start.3) | collective-permute-done | bytes 196640 | tf_op jit(solution)/shard_map/ppermute | solution.py:26
  66.7 1.3 collective-permute-start.9
  69.1 6.6 %collective-permute-start.8 = (bf16[384,256]{1,0:T(8,128)(2,1)S(1)}, bf16[384,256]{1,0:T(8,128)(2,1)S(1)}, u32[]{:S(2)}, u32[]{:S(2)}) collective-permute-start(bf16[384,256]{1,0:T(8,128)(2,1)S(1)} %get-tuple-element.54.refs_0_), channel_id=1, source_target_pairs={{0,2},{2,4},{4,6},{6,0},{1,3},{3,5},{5,7},{7,1},{8,10},{10,12},{12... | collective-permute-start | bytes 589832 | tf_op jit(solution)/shard_map/ppermute | solution.py:26
  75.7 1.7 copy-done.1
  77.4 2.6 %shard_map.97 = (bf16[384,256]{1,0:T(8,128)(2,1)S(1)}, bf16[384,256]{1,0:T(8,128)(2,1)S(1)}, bf16[384,256]{1,0:T(8,128)(2,1)S(1)}, bf16[384,256]{1,0:T(8,128)(2,1)S(1)}) custom-call(s32[4]{0:T(128)S(1)} %pad_add_fusion.place, bf16[384,256]{1,0:T(8,128)(2,1)S(1)} %copy-done.9, bf16[384,256]{1,0:T(8,128)(2,1)S(1)} %collective-permute-done.1.refs_1_, ...), custom_call_target="tpu_custom_call" | custom-call | flops 1207959552 | bytes 6291456 | tf_op jit(solution)/shard_map/pallas_call | solution.py:51
  79.9 1.5 collective-permute-start.5
  81.5 3.3 %collective-permute-start.6 = (bf16[384,256]{1,0:T(8,128)(2,1)S(1)}, bf16[384,256]{1,0:T(8,128)(2,1)S(1)}, u32[]{:S(2)}, u32[]{:S(2)}) collective-permute-start(bf16[384,256]{1,0:T(8,128)(2,1)S(1)} %get-tuple-element.51), channel_id=1, source_target_pairs={{0,16},{8,24},{16,0},{24,8},{1,17},{9,25},{17,1},{25,9},{2,18},{10... | collective-permute-start | bytes 589832 | tf_op jit(solution)/shard_map/ppermute | solution.py:26
  85.5 1.4 collective-permute-done.8.refs_1_
  86.8 2.6 %shard_map.99 = (bf16[384,256]{1,0:T(8,128)(2,1)S(1)}, bf16[384,256]{1,0:T(8,128)(2,1)S(1)}, bf16[384,256]{1,0:T(8,128)(2,1)S(1)}, bf16[384,256]{1,0:T(8,128)(2,1)S(1)}) custom-call(s32[4]{0:T(128)S(1)} %pad_add_fusion.place, bf16[384,256]{1,0:T(8,128)(2,1)S(1)} %get-tuple-element.54.refs_0_, bf16[384,256]{1,0:T(8,128)(2,1)S(1)} %collective-permute-done.8.refs_1_, ...), custom_call_target="tpu_custom_call" | custom-call | flops 1207959552 | bytes 6291456 | tf_op jit(solution)/shard_map/pallas_call | solution.py:51
  89.4 1.5 collective-permute-start.11
  90.9 2.6 %collective-permute-start.12 = (bf16[384,256]{1,0:T(8,128)(2,1)S(1)}, bf16[384,256]{1,0:T(8,128)(2,1)S(1)}, u32[]{:S(2)}, u32[]{:S(2)}) collective-permute-start(bf16[384,256]{1,0:T(8,128)(2,1)S(1)} %get-tuple-element.57), channel_id=1, source_target_pairs={{0,16},{8,24},{16,0},{24,8},{1,17},{9,25},{17,1},{25,9},{2,18},{10... | collective-permute-start | bytes 589832 | tf_op jit(solution)/shard_map/ppermute | solution.py:26
  95.2 1.4 collective-permute-start.14
  96.6 1.4 collective-permute-done.11.refs_1_
  98.0 4.2 %collective-permute-done.12.refs_2_ = bf16[384,256]{1,0:T(8,128)(2,1)S(1)} collective-permute-done((bf16[384,256]{1,0:T(8,128)(2,1)S(1)}, bf16[384,256]{1,0:T(8,128)(2,1)S(1)}, u32[]{:S(2)}, u32[]{:S(2)}) %collective-permute-start.12) | collective-permute-done | bytes 196640 | tf_op jit(solution)/shard_map/ppermute | solution.py:26
  102.9 1.4 collective-permute-start.15
  105.2 3.4 %copy-done.3 = bf16[1024,4096]{1,0:T(8,128)(2,1)S(1)} copy-done((bf16[1024,4096]{1,0:T(8,128)(2,1)S(1)}, bf16[1024,4096]{1,0:T(8,128)(2,1)}, u32[]{:S(2)}) %copy-start.3) | copy-done | bytes 8388632
  108.6 2.4 %shard_map.101 = (bf16[192,512]{1,0:T(8,128)(2,1)S(1)}, bf16[192,512]{1,0:T(8,128)(2,1)S(1)}, bf16[192,512]{1,0:T(8,128)(2,1)S(1)}, bf16[192,512]{1,0:T(8,128)(2...) custom-call(s32[4]{0:T(128)S(1)} %pad_add_fusion.place, ...), custom_call_target="tpu_custom_call" | custom-call | flops 1610612736 | bytes 10354688 | tf_op jit(solution)/shard_map/pallas_call | solution.py:51
  111.1 1.4 collective-permute-start.19
  112.5 2.4 %collective-permute-start.20 = (bf16[192,512]{1,0:T(8,128)(2,1)S(1)}, bf16[192,512]{1,0:T(8,128)(2,1)S(1)}, u32[]{:S(2)}, u32[]{:S(2)}) collective-permute-start(bf16[192,512]{1,0:T(8,128)(2,1)S(1)} %get-tuple-element.68), channel_id=1, source_target_pairs={{0,64},{32,96},{64,0},{96,32},{1,65},{33,97},{65,1},{97,33},{2,66}... | collective-permute-start | bytes 589832 | tf_op jit(solution)/shard_map/ppermute | solution.py:26
  117.3 1.4 collective-permute-done.19.refs_1_
  119.9 4.0 %collective-permute-done.20.refs_2_ = bf16[192,512]{1,0:T(8,128)(2,1)S(1)} collective-permute-done((bf16[192,512]{1,0:T(8,128)(2,1)S(1)}, bf16[192,512]{1,0:T(8,128)(2,1)S(1)}, u32[]{:S(2)}, u32[]{:S(2)}) %collective-permute-start.20) | collective-permute-done | bytes 196640 | tf_op jit(solution)/shard_map/ppermute | solution.py:26
  123.8 1.9 shard_map.102
  125.8 2.0 collective-permute-start.33
  129.2 1.9 collective-permute-start.36
  132.5 1.9 shard_map.103
  137.1 2.3 %collective-permute-start.25 = (bf16[384,256]{1,0:T(8,128)(2,1)S(1)}, bf16[384,256]{1,0:T(8,128)(2,1)S(1)}, u32[]{:S(2)}, u32[]{:S(2)}) collective-permute-start(bf16[384,256]{1,0:T(8,128)(2,1)S(1)} %shard_map.104.refs_0_), channel_id=1, source_target_pairs={{0,24},{8,0},{16,8},{24,16},{1,25},{9,1},{17,9},{25,17},{2,26},{10... | collective-permute-start | bytes 589832 | tf_op jit(solution)/shard_map/ppermute | solution.py:26
  140.4 3.4 %collective-permute-done.34.refs_1_ = bf16[384,256]{1,0:T(8,128)(2,1)S(1)} collective-permute-done((bf16[384,256]{1,0:T(8,128)(2,1)S(1)}, bf16[384,256]{1,0:T(8,128)(2,1)S(1)}, u32[]{:S(2)}, u32[]{:S(2)}) %collective-permute-start.34) | collective-permute-done | bytes 196640 | tf_op jit(solution)/shard_map/ppermute | solution.py:26
  143.7 2.0 shard_map.109
  145.7 2.1 %collective-permute-start.37 = (bf16[384,256]{1,0:T(8,128)(2,1)S(1)}, bf16[384,256]{1,0:T(8,128)(2,1)S(1)}, u32[]{:S(2)}, u32[]{:S(2)}) collective-permute-start(bf16[384,256]{1,0:T(8,128)(2,1)S(1)} %get-tuple-element.83), channel_id=1, source_target_pairs={{0,6},{2,0},{4,2},{6,4},{1,7},{3,1},{5,3},{7,5},{8,14},{10,8},{12,... | collective-permute-start | bytes 589832 | tf_op jit(solution)/shard_map/ppermute | solution.py:26
  149.9 2.3 %collective-permute-done.23.refs_1_ = bf16[384,256]{1,0:T(8,128)(2,1)S(1)} collective-permute-done((bf16[384,256]{1,0:T(8,128)(2,1)S(1)}, bf16[384,256]{1,0:T(8,128)(2,1)S(1)}, u32[]{:S(2)}, u32[]{:S(2)}) %collective-permute-start.23) | collective-permute-done | bytes 196640 | tf_op jit(solution)/shard_map/ppermute | solution.py:26
  152.2 2.0 shard_map.105
  154.2 2.1 %collective-permute-start.26 = (bf16[384,256]{1,0:T(8,128)(2,1)S(1)}, bf16[384,256]{1,0:T(8,128)(2,1)S(1)}, u32[]{:S(2)}, u32[]{:S(2)}) collective-permute-start(bf16[384,256]{1,0:T(8,128)(2,1)S(1)} %get-tuple-element.75), channel_id=1, source_target_pairs={{0,6},{2,0},{4,2},{6,4},{1,7},{3,1},{5,3},{7,5},{8,14},{10,8},{12,... | collective-permute-start | bytes 589832 | tf_op jit(solution)/shard_map/ppermute | solution.py:26
  156.3 1.3 collective-permute-start.27
  158.4 2.0 %collective-permute-done.39.refs_3_ = bf16[384,256]{1,0:T(8,128)(2,1)S(1)} collective-permute-done((bf16[384,256]{1,0:T(8,128)(2,1)S(1)}, bf16[384,256]{1,0:T(8,128)(2,1)S(1)}, u32[]{:S(2)}, u32[]{:S(2)}) %collective-permute-start.39) | collective-permute-done | bytes 196640 | tf_op jit(solution)/shard_map/ppermute | solution.py:26
  163.1 2.4 %collective-permute-start.43 = (bf16[192,512]{1,0:T(8,128)(2,1)S(1)}, bf16[192,512]{1,0:T(8,128)(2,1)S(1)}, u32[]{:S(2)}, u32[]{:S(2)}) collective-permute-start(bf16[192,512]{1,0:T(8,128)(2,1)S(1)} %shard_map.111.refs_0_), channel_id=1, source_target_pairs={{0,96},{32,0},{64,32},{96,64},{1,97},{33,1},{65,33},{97,65},{2,98}... | collective-permute-start | bytes 589832 | tf_op jit(solution)/shard_map/ppermute | solution.py:26
  165.5 3.3 %collective-permute-done.28.refs_3_ = bf16[384,256]{1,0:T(8,128)(2,1)S(1)} collective-permute-done((bf16[384,256]{1,0:T(8,128)(2,1)S(1)}, bf16[384,256]{1,0:T(8,128)(2,1)S(1)}, u32[]{:S(2)}, u32[]{:S(2)}) %collective-permute-start.28) | collective-permute-done | bytes 196640 | tf_op jit(solution)/shard_map/ppermute | solution.py:26
  170.1 2.6 %collective-permute-start.42 = (bf16[192,512]{1,0:T(8,128)(2,1)S(1)}, bf16[192,512]{1,0:T(8,128)(2,1)S(1)}, u32[]{:S(2)}, u32[]{:S(2)}) collective-permute-start(bf16[192,512]{1,0:T(8,128)(2,1)S(1)} %shard_map.111.refs_0_), channel_id=1, source_target_pairs={{0,64},{32,96},{64,0},{96,32},{1,65},{33,97},{65,1},{97,33},{2,66}... | collective-permute-start | bytes 589832 | tf_op jit(solution)/shard_map/ppermute | solution.py:26
  173.6 2.4 %collective-permute-start.32 = (bf16[192,512]{1,0:T(8,128)(2,1)S(1)}, bf16[192,512]{1,0:T(8,128)(2,1)S(1)}, u32[]{:S(2)}, u32[]{:S(2)}) collective-permute-start(bf16[192,512]{1,0:T(8,128)(2,1)S(1)} %shard_map.107.refs_0_), channel_id=1, source_target_pairs={{0,96},{32,0},{64,32},{96,64},{1,97},{33,1},{65,33},{97,65},{2,98}... | collective-permute-start | bytes 589832 | tf_op jit(solution)/shard_map/ppermute | solution.py:26
  178.0 5.0 %collective-permute-done.41.refs_1_ = bf16[192,512]{1,0:T(8,128)(2,1)S(1)} collective-permute-done((bf16[192,512]{1,0:T(8,128)(2,1)S(1)}, bf16[192,512]{1,0:T(8,128)(2,1)S(1)}, u32[]{:S(2)}, u32[]{:S(2)}) %collective-permute-start.41) | collective-permute-done | bytes 196640 | tf_op jit(solution)/shard_map/ppermute | solution.py:26
  183.1 2.1 %shard_map.112.refs_5_ = f32[192,1024]{1,0:T(8,128)S(1)} custom-call(s32[4]{0:T(128)S(1)} %pad_add_fusion.place, bf16[192,512]{1,0:T(8,128)(2,1)S(1)} %shard_map.111.refs_0_, bf16[192,512]{1,0:T(8,128)(2,1)S(1)} %collective-permute-done.41.refs_1_, bf16[192,512]{1,0:T(8,128)(2,1)S(1)} %collective-permute-done.42.refs_2_, ...), custom_call_target="tpu_custom_call" | custom-call | flops 805306368 | bytes 9961472 | tf_op jit(solution)/shard_map/pallas_call | solution.py:51
  185.1 1.4 collective-permute-done.31.refs_2_
  186.5 4.6 %collective-permute-done.30.refs_1_ = bf16[192,512]{1,0:T(8,128)(2,1)S(1)} collective-permute-done((bf16[192,512]{1,0:T(8,128)(2,1)S(1)}, bf16[192,512]{1,0:T(8,128)(2,1)S(1)}, u32[]{:S(2)}, u32[]{:S(2)}) %collective-permute-start.30) | collective-permute-done | bytes 196640 | tf_op jit(solution)/shard_map/ppermute | solution.py:26
  191.1 3.3 %shard_map.113 = (f32[192,1024]{1,0:T(8,128)}, f32[192,1024]{1,0:T(8,128)}) custom-call(s32[4]{0:T(128)S(1)} %pad_add_fusion.place, bf16[192,512]{1,0:T(8,128)(2,1)S(1)} %shard_map.107.refs_0_, bf16[192,512]{1,0:T(8,128)(2,1)S(1)} %collective-permute-done.30.refs_1_, bf16[192,512]{1,0:T(8,128)(2,1)S(1)} %collective-permute-done.31.refs_2_, ...), custom_call_target="tpu_custom_call" | custom-call | flops 805306368 | bytes 12320768 | tf_op jit(solution)/shard_map/pallas_call | solution.py:51
  (96 shorter events, 32.9 us)
Async XLA Ops:
  8.0 41.1 %reduce-scatter.2.cloned.1.call-start = ((), (), s32[]{:S(2)}) async-start(), calls=%async_computation.2 | async-start | bytes 1966080 | tf_op jit(solution)/shard_map/reduce_scatter | solution.py:248
  8.7 96.5 %all-gather.2.cloned.1.call-start = ((), (), s32[]{:S(2)}) async-start(), calls=%async_computation.3 | async-start | bytes 8650752 | tf_op jit(solution)/shard_map/all_gather | solution.py:253
  50.9 3.0 %collective-permute-start = (bf16[192,512]{1,0:T(8,128)(2,1)S(1)}, bf16[192,512]{1,0:T(8,128)(2,1)S(1)}, u32[]{:S(2)}, u32[]{:S(2)}) collective-permute-start(bf16[192,512]{1,0:T(8,128)(2,1)S(1)} %shard_map.94), channel_id=1, source_target_pairs={{0,1},{1,0},{2,3},{3,2},{4,5},{5,4},{6,7},{7,6},{8,9},{9,8},{10,11... | collective-permute-start | bytes 589832 | tf_op jit(solution)/shard_map/ppermute | solution.py:30
  55.2 20.5 %collective-permute-start.4 = (bf16[768,1536]{1,0:T(8,128)(2,1)}, bf16[768,1536]{1,0:T(8,128)(2,1)S(1)}, u32[]{:S(2)}, u32[]{:S(2)}) collective-permute-start(bf16[768,1536]{1,0:T(8,128)(2,1)} %shard_map.96.refs_4_), channel_id=1, source_target_pairs={{0,1},{1,0},{2,3},{3,2},{4,5},{5,4},{6,7},{7,6},{8,9},{9,8},{10,11... | collective-permute-start | bytes 7077896 | tf_op jit(solution)/shard_map/ppermute | solution.py:30
  56.1 10.5 %collective-permute-start.3 = (bf16[384,256]{1,0:T(8,128)(2,1)S(1)}, bf16[384,256]{1,0:T(8,128)(2,1)S(1)}, u32[]{:S(2)}, u32[]{:S(2)}) collective-permute-start(bf16[384,256]{1,0:T(8,128)(2,1)S(1)} %copy-done.9), channel_id=1, source_target_pairs={{0,6},{2,0},{4,2},{6,4},{1,7},{3,1},{5,3},{7,5},{8,14},{10,8},{12,... | collective-permute-start | bytes 589832 | tf_op jit(solution)/shard_map/ppermute | solution.py:26
  57.0 12.1 %collective-permute-start.2 = (bf16[384,256]{1,0:T(8,128)(2,1)S(1)}, bf16[384,256]{1,0:T(8,128)(2,1)S(1)}, u32[]{:S(2)}, u32[]{:S(2)}) collective-permute-start(bf16[384,256]{1,0:T(8,128)(2,1)S(1)} %copy-done.9), channel_id=1, source_target_pairs={{0,4},{2,6},{4,0},{6,2},{1,5},{3,7},{5,1},{7,3},{8,12},{10,14},{12... | collective-permute-start | bytes 589832 | tf_op jit(solution)/shard_map/ppermute | solution.py:26
  58.3 17.5 %collective-permute-start.1 = (bf16[384,256]{1,0:T(8,128)(2,1)S(1)}, bf16[384,256]{1,0:T(8,128)(2,1)S(1)}, u32[]{:S(2)}, u32[]{:S(2)}) collective-permute-start(bf16[384,256]{1,0:T(8,128)(2,1)S(1)} %copy-done.9), channel_id=1, source_target_pairs={{0,2},{2,4},{4,6},{6,0},{1,3},{3,5},{5,7},{7,1},{8,10},{10,12},{12... | collective-permute-start | bytes 589832 | tf_op jit(solution)/shard_map/ppermute | solution.py:26
  58.3 26.5 %collective-permute-start.10 = (bf16[384,256]{1,0:T(8,128)(2,1)S(1)}, bf16[384,256]{1,0:T(8,128)(2,1)S(1)}, u32[]{:S(2)}, u32[]{:S(2)}) collective-permute-start(bf16[384,256]{1,0:T(8,128)(2,1)S(1)} %get-tuple-element.54.refs_0_), channel_id=1, source_target_pairs={{0,6},{2,0},{4,2},{6,4},{1,7},{3,1},{5,3},{7,5},{8,14},{10,8},{12,... | collective-permute-start | bytes 589832 | tf_op jit(solution)/shard_map/ppermute | solution.py:26
  66.7 18.8 %collective-permute-start.9 = (bf16[384,256]{1,0:T(8,128)(2,1)S(1)}, bf16[384,256]{1,0:T(8,128)(2,1)S(1)}, u32[]{:S(2)}, u32[]{:S(2)}) collective-permute-start(bf16[384,256]{1,0:T(8,128)(2,1)S(1)} %get-tuple-element.54.refs_0_), channel_id=1, source_target_pairs={{0,4},{2,6},{4,0},{6,2},{1,5},{3,7},{5,1},{7,3},{8,12},{10,14},{12... | collective-permute-start | bytes 589832 | tf_op jit(solution)/shard_map/ppermute | solution.py:26
  69.1 17.7 %collective-permute-start.8 = (bf16[384,256]{1,0:T(8,128)(2,1)S(1)}, bf16[384,256]{1,0:T(8,128)(2,1)S(1)}, u32[]{:S(2)}, u32[]{:S(2)}) collective-permute-start(bf16[384,256]{1,0:T(8,128)(2,1)S(1)} %get-tuple-element.54.refs_0_), channel_id=1, source_target_pairs={{0,2},{2,4},{4,6},{6,0},{1,3},{3,5},{5,7},{7,1},{8,10},{10,12},{12... | collective-permute-start | bytes 589832 | tf_op jit(solution)/shard_map/ppermute | solution.py:26
  79.9 13.6 %collective-permute-start.5 = (bf16[384,256]{1,0:T(8,128)(2,1)S(1)}, bf16[384,256]{1,0:T(8,128)(2,1)S(1)}, u32[]{:S(2)}, u32[]{:S(2)}) collective-permute-start(bf16[384,256]{1,0:T(8,128)(2,1)S(1)} %get-tuple-element.50), channel_id=1, source_target_pairs={{0,8},{8,16},{16,24},{24,0},{1,9},{9,17},{17,25},{25,1},{2,10},{10... | collective-permute-start | bytes 589832 | tf_op jit(solution)/shard_map/ppermute | solution.py:26
  81.5 13.1 %collective-permute-start.6 = (bf16[384,256]{1,0:T(8,128)(2,1)S(1)}, bf16[384,256]{1,0:T(8,128)(2,1)S(1)}, u32[]{:S(2)}, u32[]{:S(2)}) collective-permute-start(bf16[384,256]{1,0:T(8,128)(2,1)S(1)} %get-tuple-element.51), channel_id=1, source_target_pairs={{0,16},{8,24},{16,0},{24,8},{1,17},{9,25},{17,1},{25,9},{2,18},{10... | collective-permute-start | bytes 589832 | tf_op jit(solution)/shard_map/ppermute | solution.py:26
  84.8 9.8 %collective-permute-start.7 = (bf16[384,256]{1,0:T(8,128)(2,1)S(1)}, bf16[384,256]{1,0:T(8,128)(2,1)S(1)}, u32[]{:S(2)}, u32[]{:S(2)}) collective-permute-start(bf16[384,256]{1,0:T(8,128)(2,1)S(1)} %get-tuple-element.52), channel_id=1, source_target_pairs={{0,24},{8,0},{16,8},{24,16},{1,25},{9,1},{17,9},{25,17},{2,26},{10... | collective-permute-start | bytes 589832 | tf_op jit(solution)/shard_map/ppermute | solution.py:26
  89.4 8.6 %collective-permute-start.11 = (bf16[384,256]{1,0:T(8,128)(2,1)S(1)}, bf16[384,256]{1,0:T(8,128)(2,1)S(1)}, u32[]{:S(2)}, u32[]{:S(2)}) collective-permute-start(bf16[384,256]{1,0:T(8,128)(2,1)S(1)} %get-tuple-element.56), channel_id=1, source_target_pairs={{0,8},{8,16},{16,24},{24,0},{1,9},{9,17},{17,25},{25,1},{2,10},{10... | collective-permute-start | bytes 589832 | tf_op jit(solution)/shard_map/ppermute | solution.py:26
  90.9 11.3 %collective-permute-start.12 = (bf16[384,256]{1,0:T(8,128)(2,1)S(1)}, bf16[384,256]{1,0:T(8,128)(2,1)S(1)}, u32[]{:S(2)}, u32[]{:S(2)}) collective-permute-start(bf16[384,256]{1,0:T(8,128)(2,1)S(1)} %get-tuple-element.57), channel_id=1, source_target_pairs={{0,16},{8,24},{16,0},{24,8},{1,17},{9,25},{17,1},{25,9},{2,18},{10... | collective-permute-start | bytes 589832 | tf_op jit(solution)/shard_map/ppermute | solution.py:26
  93.5 8.7 %collective-permute-start.13 = (bf16[384,256]{1,0:T(8,128)(2,1)S(1)}, bf16[384,256]{1,0:T(8,128)(2,1)S(1)}, u32[]{:S(2)}, u32[]{:S(2)}) collective-permute-start(bf16[384,256]{1,0:T(8,128)(2,1)S(1)} %get-tuple-element.58), channel_id=1, source_target_pairs={{0,24},{8,0},{16,8},{24,16},{1,25},{9,1},{17,9},{25,17},{2,26},{10... | collective-permute-start | bytes 589832 | tf_op jit(solution)/shard_map/ppermute | solution.py:26
  95.2 9.1 %collective-permute-start.14 = (bf16[192,256]{1,0:T(8,128)(2,1)S(1)}, bf16[192,256]{1,0:T(8,128)(2,1)S(1)}, u32[]{:S(2)}, u32[]{:S(2)}) collective-permute-start(bf16[192,256]{1,0:T(8,128)(2,1)S(1)} %get-tuple-element.60), channel_id=1, source_target_pairs={{0,1},{1,0},{2,3},{3,2},{4,5},{5,4},{6,7},{7,6},{8,9},{9,8},{10,11... | collective-permute-start | bytes 294920 | tf_op jit(solution)/shard_map/ppermute | solution.py:30
  102.9 2.4 %collective-permute-start.15 = (bf16[192,256]{1,0:T(8,128)(2,1)S(1)}, bf16[192,256]{1,0:T(8,128)(2,1)S(1)}, u32[]{:S(2)}, u32[]{:S(2)}) collective-permute-start(bf16[192,256]{1,0:T(8,128)(2,1)S(1)} %get-tuple-element.61), channel_id=1, source_target_pairs={{0,1},{1,0},{2,3},{3,2},{4,5},{5,4},{6,7},{7,6},{8,9},{9,8},{10,11... | collective-permute-start | bytes 294920 | tf_op jit(solution)/shard_map/ppermute | solution.py:30
  111.1 7.6 %collective-permute-start.19 = (bf16[192,512]{1,0:T(8,128)(2,1)S(1)}, bf16[192,512]{1,0:T(8,128)(2,1)S(1)}, u32[]{:S(2)}, u32[]{:S(2)}) collective-permute-start(bf16[192,512]{1,0:T(8,128)(2,1)S(1)} %get-tuple-element.67), channel_id=1, source_target_pairs={{0,32},{32,64},{64,96},{96,0},{1,33},{33,65},{65,97},{97,1},{2,34}... | collective-permute-start | bytes 589832 | tf_op jit(solution)/shard_map/ppermute | solution.py:26
  112.5 11.3 %collective-permute-start.20 = (bf16[192,512]{1,0:T(8,128)(2,1)S(1)}, bf16[192,512]{1,0:T(8,128)(2,1)S(1)}, u32[]{:S(2)}, u32[]{:S(2)}) collective-permute-start(bf16[192,512]{1,0:T(8,128)(2,1)S(1)} %get-tuple-element.68), channel_id=1, source_target_pairs={{0,64},{32,96},{64,0},{96,32},{1,65},{33,97},{65,1},{97,33},{2,66}... | collective-permute-start | bytes 589832 | tf_op jit(solution)/shard_map/ppermute | solution.py:26
  114.9 8.9 %collective-permute-start.21 = (bf16[192,512]{1,0:T(8,128)(2,1)S(1)}, bf16[192,512]{1,0:T(8,128)(2,1)S(1)}, u32[]{:S(2)}, u32[]{:S(2)}) collective-permute-start(bf16[192,512]{1,0:T(8,128)(2,1)S(1)} %get-tuple-element.69), channel_id=1, source_target_pairs={{0,96},{32,0},{64,32},{96,64},{1,97},{33,1},{65,33},{97,65},{2,98}... | collective-permute-start | bytes 589832 | tf_op jit(solution)/shard_map/ppermute | solution.py:26
  116.1 16.0 %collective-permute-start.16 = (bf16[192,512]{1,0:T(8,128)(2,1)S(1)}, bf16[192,512]{1,0:T(8,128)(2,1)S(1)}, u32[]{:S(2)}, u32[]{:S(2)}) collective-permute-start(bf16[192,512]{1,0:T(8,128)(2,1)S(1)} %get-tuple-element.63), channel_id=1, source_target_pairs={{0,32},{32,64},{64,96},{96,0},{1,33},{33,65},{65,97},{97,1},{2,34}... | collective-permute-start | bytes 589832 | tf_op jit(solution)/shard_map/ppermute | solution.py:26
  116.4 16.1 %collective-permute-start.17 = (bf16[192,512]{1,0:T(8,128)(2,1)S(1)}, bf16[192,512]{1,0:T(8,128)(2,1)S(1)}, u32[]{:S(2)}, u32[]{:S(2)}) collective-permute-start(bf16[192,512]{1,0:T(8,128)(2,1)S(1)} %get-tuple-element.64), channel_id=1, source_target_pairs={{0,64},{32,96},{64,0},{96,32},{1,65},{33,97},{65,1},{97,33},{2,66}... | collective-permute-start | bytes 589832 | tf_op jit(solution)/shard_map/ppermute | solution.py:26
  118.7 13.8 %collective-permute-start.18 = (bf16[192,512]{1,0:T(8,128)(2,1)S(1)}, bf16[192,512]{1,0:T(8,128)(2,1)S(1)}, u32[]{:S(2)}, u32[]{:S(2)}) collective-permute-start(bf16[192,512]{1,0:T(8,128)(2,1)S(1)} %get-tuple-element.65), channel_id=1, source_target_pairs={{0,96},{32,0},{64,32},{96,64},{1,97},{33,1},{65,33},{97,65},{2,98}... | collective-permute-start | bytes 589832 | tf_op jit(solution)/shard_map/ppermute | solution.py:26
  125.8 2.9 %collective-permute-start.33 = (bf16[192,256]{1,0:T(8,128)(2,1)S(1)}, bf16[192,256]{1,0:T(8,128)(2,1)S(1)}, u32[]{:S(2)}, u32[]{:S(2)}) collective-permute-start(bf16[192,256]{1,0:T(8,128)(2,1)S(1)} %get-tuple-element.81), channel_id=1, source_target_pairs={{0,1},{1,0},{2,3},{3,2},{4,5},{5,4},{6,7},{7,6},{8,9},{9,8},{10,11... | collective-permute-start | bytes 294920 | tf_op jit(solution)/shard_map/ppermute | solution.py:30
  129.2 11.1 %collective-permute-start.36 = (bf16[384,256]{1,0:T(8,128)(2,1)S(1)}, bf16[384,256]{1,0:T(8,128)(2,1)S(1)}, u32[]{:S(2)}, u32[]{:S(2)}) collective-permute-start(bf16[384,256]{1,0:T(8,128)(2,1)S(1)} %shard_map.108.refs_0_), channel_id=1, source_target_pairs={{0,24},{8,0},{16,8},{24,16},{1,25},{9,1},{17,9},{25,17},{2,26},{10... | collective-permute-start | bytes 589832 | tf_op jit(solution)/shard_map/ppermute | solution.py:26
  131.2 9.2 %collective-permute-start.35 = (bf16[384,256]{1,0:T(8,128)(2,1)S(1)}, bf16[384,256]{1,0:T(8,128)(2,1)S(1)}, u32[]{:S(2)}, u32[]{:S(2)}) collective-permute-start(bf16[384,256]{1,0:T(8,128)(2,1)S(1)} %shard_map.108.refs_0_), channel_id=1, source_target_pairs={{0,16},{8,24},{16,0},{24,8},{1,17},{9,25},{17,1},{25,9},{2,18},{10... | collective-permute-start | bytes 589832 | tf_op jit(solution)/shard_map/ppermute | solution.py:26
  132.1 11.7 %collective-permute-start.34 = (bf16[384,256]{1,0:T(8,128)(2,1)S(1)}, bf16[384,256]{1,0:T(8,128)(2,1)S(1)}, u32[]{:S(2)}, u32[]{:S(2)}) collective-permute-start(bf16[384,256]{1,0:T(8,128)(2,1)S(1)} %shard_map.108.refs_0_), channel_id=1, source_target_pairs={{0,8},{8,16},{16,24},{24,0},{1,9},{9,17},{17,25},{25,1},{2,10},{10... | collective-permute-start | bytes 589832 | tf_op jit(solution)/shard_map/ppermute | solution.py:26
  132.5 50.6 %slice-start = ((s8[8388608]{0:T(1024)(128)(4,1)}), s8[4194304]{0:T(1024)(128)(4,1)S(1)}, s32[]{:S(2)}) async-start(s8[8388608]{0:T(1024)(128)(4,1)} %bitcast.8), calls=%async_computation.4 | async-start | bytes 8388608
  134.4 2.1 %collective-permute-start.22 = (bf16[192,256]{1,0:T(8,128)(2,1)S(1)}, bf16[192,256]{1,0:T(8,128)(2,1)S(1)}, u32[]{:S(2)}, u32[]{:S(2)}) collective-permute-start(bf16[192,256]{1,0:T(8,128)(2,1)S(1)} %get-tuple-element.73), channel_id=1, source_target_pairs={{0,1},{1,0},{2,3},{3,2},{4,5},{5,4},{6,7},{7,6},{8,9},{9,8},{10,11... | collective-permute-start | bytes 294920 | tf_op jit(solution)/shard_map/ppermute | solution.py:30
  137.1 45.9 %slice-start.1 = ((s8[8388608]{0:T(1024)(128)(4,1)}), s8[4194304]{0:T(1024)(128)(4,1)S(1)}, s32[]{:S(2)}) async-start(s8[8388608]{0:T(1024)(128)(4,1)} %bitcast.8), calls=%async_computation.5 | async-start | bytes 8388608
  137.1 12.0 %collective-permute-start.25 = (bf16[384,256]{1,0:T(8,128)(2,1)S(1)}, bf16[384,256]{1,0:T(8,128)(2,1)S(1)}, u32[]{:S(2)}, u32[]{:S(2)}) collective-permute-start(bf16[384,256]{1,0:T(8,128)(2,1)S(1)} %shard_map.104.refs_0_), channel_id=1, source_target_pairs={{0,24},{8,0},{16,8},{24,16},{1,25},{9,1},{17,9},{25,17},{2,26},{10... | collective-permute-start | bytes 589832 | tf_op jit(solution)/shard_map/ppermute | solution.py:26
  139.5 10.4 %collective-permute-start.24 = (bf16[384,256]{1,0:T(8,128)(2,1)S(1)}, bf16[384,256]{1,0:T(8,128)(2,1)S(1)}, u32[]{:S(2)}, u32[]{:S(2)}) collective-permute-start(bf16[384,256]{1,0:T(8,128)(2,1)S(1)} %shard_map.104.refs_0_), channel_id=1, source_target_pairs={{0,16},{8,24},{16,0},{24,8},{1,17},{9,25},{17,1},{25,9},{2,18},{10... | collective-permute-start | bytes 589832 | tf_op jit(solution)/shard_map/ppermute | solution.py:26
  140.4 11.8 %collective-permute-start.23 = (bf16[384,256]{1,0:T(8,128)(2,1)S(1)}, bf16[384,256]{1,0:T(8,128)(2,1)S(1)}, u32[]{:S(2)}, u32[]{:S(2)}) collective-permute-start(bf16[384,256]{1,0:T(8,128)(2,1)S(1)} %shard_map.104.refs_0_), channel_id=1, source_target_pairs={{0,8},{8,16},{16,24},{24,0},{1,9},{9,17},{17,25},{25,1},{2,10},{10... | collective-permute-start | bytes 589832 | tf_op jit(solution)/shard_map/ppermute | solution.py:26
  145.7 11.9 %collective-permute-start.37 = (bf16[384,256]{1,0:T(8,128)(2,1)S(1)}, bf16[384,256]{1,0:T(8,128)(2,1)S(1)}, u32[]{:S(2)}, u32[]{:S(2)}) collective-permute-start(bf16[384,256]{1,0:T(8,128)(2,1)S(1)} %get-tuple-element.83), channel_id=1, source_target_pairs={{0,6},{2,0},{4,2},{6,4},{1,7},{3,1},{5,3},{7,5},{8,14},{10,8},{12,... | collective-permute-start | bytes 589832 | tf_op jit(solution)/shard_map/ppermute | solution.py:26
  147.8 10.5 %collective-permute-start.38 = (bf16[384,256]{1,0:T(8,128)(2,1)S(1)}, bf16[384,256]{1,0:T(8,128)(2,1)S(1)}, u32[]{:S(2)}, u32[]{:S(2)}) collective-permute-start(bf16[384,256]{1,0:T(8,128)(2,1)S(1)} %get-tuple-element.84), channel_id=1, source_target_pairs={{0,4},{2,6},{4,0},{6,2},{1,5},{3,7},{5,1},{7,3},{8,12},{10,14},{12... | collective-permute-start | bytes 589832 | tf_op jit(solution)/shard_map/ppermute | solution.py:26
  149.1 11.3 %collective-permute-start.39 = (bf16[384,256]{1,0:T(8,128)(2,1)S(1)}, bf16[384,256]{1,0:T(8,128)(2,1)S(1)}, u32[]{:S(2)}, u32[]{:S(2)}) collective-permute-start(bf16[384,256]{1,0:T(8,128)(2,1)S(1)} %get-tuple-element.85), channel_id=1, source_target_pairs={{0,2},{2,4},{4,6},{6,0},{1,3},{3,5},{5,7},{7,1},{8,10},{10,12},{12... | collective-permute-start | bytes 589832 | tf_op jit(solution)/shard_map/ppermute | solution.py:26
  154.2 11.3 %collective-permute-start.26 = (bf16[384,256]{1,0:T(8,128)(2,1)S(1)}, bf16[384,256]{1,0:T(8,128)(2,1)S(1)}, u32[]{:S(2)}, u32[]{:S(2)}) collective-permute-start(bf16[384,256]{1,0:T(8,128)(2,1)S(1)} %get-tuple-element.75), channel_id=1, source_target_pairs={{0,6},{2,0},{4,2},{6,4},{1,7},{3,1},{5,3},{7,5},{8,14},{10,8},{12,... | collective-permute-start | bytes 589832 | tf_op jit(solution)/shard_map/ppermute | solution.py:26
  156.3 9.2 %collective-permute-start.27 = (bf16[384,256]{1,0:T(8,128)(2,1)S(1)}, bf16[384,256]{1,0:T(8,128)(2,1)S(1)}, u32[]{:S(2)}, u32[]{:S(2)}) collective-permute-start(bf16[384,256]{1,0:T(8,128)(2,1)S(1)} %get-tuple-element.76), channel_id=1, source_target_pairs={{0,4},{2,6},{4,0},{6,2},{1,5},{3,7},{5,1},{7,3},{8,12},{10,14},{12... | collective-permute-start | bytes 589832 | tf_op jit(solution)/shard_map/ppermute | solution.py:26
  157.6 11.3 %collective-permute-start.28 = (bf16[384,256]{1,0:T(8,128)(2,1)S(1)}, bf16[384,256]{1,0:T(8,128)(2,1)S(1)}, u32[]{:S(2)}, u32[]{:S(2)}) collective-permute-start(bf16[384,256]{1,0:T(8,128)(2,1)S(1)} %get-tuple-element.77), channel_id=1, source_target_pairs={{0,2},{2,4},{4,6},{6,0},{1,3},{3,5},{5,7},{7,1},{8,10},{10,12},{12... | collective-permute-start | bytes 589832 | tf_op jit(solution)/shard_map/ppermute | solution.py:26
  161.0 1.5 collective-permute-start.40
  163.1 13.4 %collective-permute-start.43 = (bf16[192,512]{1,0:T(8,128)(2,1)S(1)}, bf16[192,512]{1,0:T(8,128)(2,1)S(1)}, u32[]{:S(2)}, u32[]{:S(2)}) collective-permute-start(bf16[192,512]{1,0:T(8,128)(2,1)S(1)} %shard_map.111.refs_0_), channel_id=1, source_target_pairs={{0,96},{32,0},{64,32},{96,64},{1,97},{33,1},{65,33},{97,65},{2,98}... | collective-permute-start | bytes 589832 | tf_op jit(solution)/shard_map/ppermute | solution.py:26
  169.5 3.5 %collective-permute-start.29 = (bf16[192,256]{1,0:T(8,128)(2,1)S(1)}, bf16[192,256]{1,0:T(8,128)(2,1)S(1)}, u32[]{:S(2)}, u32[]{:S(2)}) collective-permute-start(bf16[192,256]{1,0:T(8,128)(2,1)S(1)} %get-tuple-element.79), channel_id=1, source_target_pairs={{0,1},{1,0},{2,3},{3,2},{4,5},{5,4},{6,7},{7,6},{8,9},{9,8},{10,11... | collective-permute-start | bytes 294920 | tf_op jit(solution)/shard_map/ppermute | solution.py:30
  170.1 8.0 %collective-permute-start.42 = (bf16[192,512]{1,0:T(8,128)(2,1)S(1)}, bf16[192,512]{1,0:T(8,128)(2,1)S(1)}, u32[]{:S(2)}, u32[]{:S(2)}) collective-permute-start(bf16[192,512]{1,0:T(8,128)(2,1)S(1)} %shard_map.111.refs_0_), channel_id=1, source_target_pairs={{0,64},{32,96},{64,0},{96,32},{1,65},{33,97},{65,1},{97,33},{2,66}... | collective-permute-start | bytes 589832 | tf_op jit(solution)/shard_map/ppermute | solution.py:26
  172.7 10.4 %collective-permute-start.41 = (bf16[192,512]{1,0:T(8,128)(2,1)S(1)}, bf16[192,512]{1,0:T(8,128)(2,1)S(1)}, u32[]{:S(2)}, u32[]{:S(2)}) collective-permute-start(bf16[192,512]{1,0:T(8,128)(2,1)S(1)} %shard_map.111.refs_0_), channel_id=1, source_target_pairs={{0,32},{32,64},{64,96},{96,0},{1,33},{33,65},{65,97},{97,1},{2,34}... | collective-permute-start | bytes 589832 | tf_op jit(solution)/shard_map/ppermute | solution.py:26
  173.6 11.5 %collective-permute-start.32 = (bf16[192,512]{1,0:T(8,128)(2,1)S(1)}, bf16[192,512]{1,0:T(8,128)(2,1)S(1)}, u32[]{:S(2)}, u32[]{:S(2)}) collective-permute-start(bf16[192,512]{1,0:T(8,128)(2,1)S(1)} %shard_map.107.refs_0_), channel_id=1, source_target_pairs={{0,96},{32,0},{64,32},{96,64},{1,97},{33,1},{65,33},{97,65},{2,98}... | collective-permute-start | bytes 589832 | tf_op jit(solution)/shard_map/ppermute | solution.py:26
  176.0 10.5 %collective-permute-start.31 = (bf16[192,512]{1,0:T(8,128)(2,1)S(1)}, bf16[192,512]{1,0:T(8,128)(2,1)S(1)}, u32[]{:S(2)}, u32[]{:S(2)}) collective-permute-start(bf16[192,512]{1,0:T(8,128)(2,1)S(1)} %shard_map.107.refs_0_), channel_id=1, source_target_pairs={{0,64},{32,96},{64,0},{96,32},{1,65},{33,97},{65,1},{97,33},{2,66}... | collective-permute-start | bytes 589832 | tf_op jit(solution)/shard_map/ppermute | solution.py:26
  176.5 14.6 %collective-permute-start.30 = (bf16[192,512]{1,0:T(8,128)(2,1)S(1)}, bf16[192,512]{1,0:T(8,128)(2,1)S(1)}, u32[]{:S(2)}, u32[]{:S(2)}) collective-permute-start(bf16[192,512]{1,0:T(8,128)(2,1)S(1)} %shard_map.107.refs_0_), channel_id=1, source_target_pairs={{0,32},{32,64},{64,96},{96,0},{1,33},{33,65},{65,97},{97,1},{2,34}... | collective-permute-start | bytes 589832 | tf_op jit(solution)/shard_map/ppermute | solution.py:26
  (11 other events, 78.7 us)
Sparse Core Ops, SparseCore 0:
  11.2 27.8 reduce-scatter.1
Sparse Core Ops, SparseCore 1:
  11.5 73.4 all-gather.1

commit v5 on v4

--- a/solution.py
+++ b/solution.py
@@ -130,20 +130,19 @@
         out[...] = sum(piece[lines].astype(f32) for piece in pieces).astype(bf16)
 
 
-def right_kernel(place, *refs):
+def right_kernel(chosen, place, *refs):
     own, arrived, basis = refs[:CHUNKS], refs[CHUNKS : 2 * CHUNKS], refs[2 * CHUNKS]
     outs, rows = refs[2 * CHUNKS + 1 : -1], refs[-1]
     width = own[0].shape[1]
     for chunk in range(CHUNKS):
         rows[:, side(place[3] * CHUNKS + chunk, width)] = own[chunk][...]
         rows[:, side((1 - place[3]) * CHUNKS + chunk, width)] = arrived[chunk][...]
-    for chunk in range(CHUNKS):
-        for d in range(RING):
-            for core in range(2):
-                block = (lax.rem(place[0] + d, RING) * 2 + core) * CHUNKS + chunk
-                outs[chunk * RING + d][:, core * width : (core + 1) * width] = jnp.dot(
-                    rows[...], basis[:, side(block, width)], preferred_element_type=f32
-                ).astype(bf16)
+    for d in range(RING):
+        for core in range(2):
+            block = (lax.rem(place[0] + d, RING) * 2 + core) * CHUNKS + chosen
+            outs[d][:, core * width : (core + 1) * width] = jnp.dot(
+                rows[...], basis[:, side(block, width)], preferred_element_type=f32
+            ).astype(bf16)
 
 
 def moment_kernel(place, *refs):
@@ -271,17 +270,19 @@
         kept.append(own)
         arrived.append(swap(other))
 
-    parts = call(
-        right_kernel,
-        place,
-        [*kept, *arrived, basis],
-        [shape(rows, 2 * width)] * (RING * CHUNKS),
-        2 * rows * columns * RING * columns,
-        [pltpu.VMEM((rows, columns), bf16)],
-    )
-    so_far, chunks = (), []
+    so_far, chunks, follow = (), [], []
     for chunk in range(CHUNKS):
-        pieces = spread(parts[chunk * RING : (chunk + 1) * RING], "x")
+        parts = call(
+            functools.partial(right_kernel, chunk),
+            place,
+            [*kept, *arrived, basis],
+            [shape(rows, 2 * width)] * RING,
+            2 * rows * columns * RING * columns // CHUNKS,
+            [pltpu.VMEM((rows, columns), bf16)],
+            after=follow,
+        )
+        follow = parts[:1]
+        pieces = spread(parts, "x")
         *so_far, own, lent = moments(place, chunk, pieces, moment_one, moment_two, so_far)
         chunks.append(call(stack_kernel, place, [own, swap(lent)], [shape(both, width)])[0])
     new_one, new_two = so_far

time: 202 us -> 201 us (level)
  waiting for transfers between devices: 48 us -> 45.9 us
    ppermute x36, waiting for transfers between devices: 42 us -> 39.9 us  [shift(): lax.ppermute(value, axis, [(i, (i + distance) % RING) for i in range(RING)])]
    pallas_call x18 -> x19, Pallas kernels: 23.6 us -> 24.3 us  [call(): pl.pallas_call(body, out_shape=outs, in_specs=[pl.BlockSpec(memory_space=...]
  transfers between devices with their start and end apart: 46 -> 46, of which waited for: 20 -> 19; matrix products, arithmetic and copies ran while one was open for 0% -> 0% of each run, Pallas kernels for 11% -> 12%
where the time goes in v5:
time: 201 us
  starting transfers between devices  64.4 us (32%)
  waiting for transfers between devices  45.9 us (23%)
  blocking collectives  37.3 us (19%)
  Pallas kernels  28.2 us (14%)
  between operations  15.7 us (8%)
  local copies, waits for them, and re-layouts  9.26 us (5%)
    ppermute x36, starting transfers between devices, shift(): lax.ppermute(value, axis, [(i, (i + distance) % RING) for i in range(RING)])  54.9 us
    ppermute x36, waiting for transfers between devices, shift(): lax.ppermute(value, axis, [(i, (i + distance) % RING) for i in range(RING)])  39.9 us
    all_to_all x1, blocking collectives, per_device(): lax.all_to_all(parts, 'y', 0, 0, tiled=True).reshape(RING * rows, strip)  37.3 us
    pallas_call x19, Pallas kernels, call(): pl.pallas_call(body, out_shape=outs, in_specs=[pl.BlockSpec(memory_space=...  24.3 us
    ppermute x8, starting transfers between devices, swap(): return lax.ppermute(value, 'core', [(0, 1), (1, 0)])  9.45 us
    unnamed x26, local copies, waits for them, and re-layouts  9.26 us
    ppermute x8, waiting for transfers between devices, swap(): return lax.ppermute(value, 'core', [(0, 1), (1, 0)])  4.85 us
  transfers between devices with their start and end apart: 46, of which 19 were waited for; matrix products, arithmetic and copies ran while one was open for 0% of the time, Pallas kernels for 12%

profile of v5, /device:TPU:1, one launch (start us, length us, event | category | flops | bytes accessed | tf_op | source)
XLA Modules:
  0.0 200.8 jit_solution(14357416004204309708)
XLA Ops:
  9.4 1.7 copy-done.6
  11.8 37.3 %all_to_all.5 = bf16[4,192,1536]{2,1,0:T(8,128)(2,1)S(1)} all-to-all(bf16[4,192,1536]{2,1,0:T(8,128)(2,1)S(1)} %shard_map.93), channel_id=1, replica_groups=mesh['x'=4,'z'=4,'y'=4,'core'=2] {'y'}, dimensions={0} | all-to-all | bytes 4718592 | tf_op jit(solution)/shard_map/all_to_all | solution.py:245
  50.9 1.9 collective-permute-start
  58.3 2.7 %collective-permute-start.10 = (bf16[384,256]{1,0:T(8,128)(2,1)S(1)}, bf16[384,256]{1,0:T(8,128)(2,1)S(1)}, u32[]{:S(2)}, u32[]{:S(2)}) collective-permute-start(bf16[384,256]{1,0:T(8,128)(2,1)S(1)} %get-tuple-element.54.refs_0_), channel_id=1, source_target_pairs={{0,6},{2,0},{4,2},{6,4},{1,7},{3,1},{5,3},{7,5},{8,14},{10,8},{12,... | collective-permute-start | bytes 589832 | tf_op jit(solution)/shard_map/ppermute | solution.py:26
  60.9 5.7 %collective-permute-done.3.refs_3_ = bf16[384,256]{1,0:T(8,128)(2,1)S(1)} collective-permute-done((bf16[384,256]{1,0:T(8,128)(2,1)S(1)}, bf16[384,256]{1,0:T(8,128)(2,1)S(1)}, u32[]{:S(2)}, u32[]{:S(2)}) %collective-permute-start.3) | collective-permute-done | bytes 196640 | tf_op jit(solution)/shard_map/ppermute | solution.py:26
  66.7 1.3 collective-permute-start.9
  69.1 6.6 %collective-permute-start.8 = (bf16[384,256]{1,0:T(8,128)(2,1)S(1)}, bf16[384,256]{1,0:T(8,128)(2,1)S(1)}, u32[]{:S(2)}, u32[]{:S(2)}) collective-permute-start(bf16[384,256]{1,0:T(8,128)(2,1)S(1)} %get-tuple-element.54.refs_0_), channel_id=1, source_target_pairs={{0,2},{2,4},{4,6},{6,0},{1,3},{3,5},{5,7},{7,1},{8,10},{10,12},{12... | collective-permute-start | bytes 589832 | tf_op jit(solution)/shard_map/ppermute | solution.py:26
  75.7 1.7 copy-done.2
  77.4 2.6 %shard_map.97 = (bf16[384,256]{1,0:T(8,128)(2,1)S(1)}, bf16[384,256]{1,0:T(8,128)(2,1)S(1)}, bf16[384,256]{1,0:T(8,128)(2,1)S(1)}, bf16[384,256]{1,0:T(8,128)(2,1)S(1)}) custom-call(s32[4]{0:T(128)S(1)} %pad_add_fusion.place, bf16[384,256]{1,0:T(8,128)(2,1)S(1)} %copy-done.9, bf16[384,256]{1,0:T(8,128)(2,1)S(1)} %collective-permute-done.1.refs_1_, ...), custom_call_target="tpu_custom_call" | custom-call | flops 1207959552 | bytes 6291456 | tf_op jit(solution)/shard_map/pallas_call | solution.py:51
  79.9 1.5 collective-permute-start.5
  81.5 3.3 %collective-permute-start.6 = (bf16[384,256]{1,0:T(8,128)(2,1)S(1)}, bf16[384,256]{1,0:T(8,128)(2,1)S(1)}, u32[]{:S(2)}, u32[]{:S(2)}) collective-permute-start(bf16[384,256]{1,0:T(8,128)(2,1)S(1)} %get-tuple-element.51), channel_id=1, source_target_pairs={{0,16},{8,24},{16,0},{24,8},{1,17},{9,25},{17,1},{25,9},{2,18},{10... | collective-permute-start | bytes 589832 | tf_op jit(solution)/shard_map/ppermute | solution.py:26
  85.5 1.4 collective-permute-done.8.refs_1_
  86.8 2.6 %shard_map.99 = (bf16[384,256]{1,0:T(8,128)(2,1)S(1)}, bf16[384,256]{1,0:T(8,128)(2,1)S(1)}, bf16[384,256]{1,0:T(8,128)(2,1)S(1)}, bf16[384,256]{1,0:T(8,128)(2,1)S(1)}) custom-call(s32[4]{0:T(128)S(1)} %pad_add_fusion.place, bf16[384,256]{1,0:T(8,128)(2,1)S(1)} %get-tuple-element.54.refs_0_, bf16[384,256]{1,0:T(8,128)(2,1)S(1)} %collective-permute-done.8.refs_1_, ...), custom_call_target="tpu_custom_call" | custom-call | flops 1207959552 | bytes 6291456 | tf_op jit(solution)/shard_map/pallas_call | solution.py:51
  89.4 1.5 collective-permute-start.11
  90.9 2.6 %collective-permute-start.12 = (bf16[384,256]{1,0:T(8,128)(2,1)S(1)}, bf16[384,256]{1,0:T(8,128)(2,1)S(1)}, u32[]{:S(2)}, u32[]{:S(2)}) collective-permute-start(bf16[384,256]{1,0:T(8,128)(2,1)S(1)} %get-tuple-element.57), channel_id=1, source_target_pairs={{0,16},{8,24},{16,0},{24,8},{1,17},{9,25},{17,1},{25,9},{2,18},{10... | collective-permute-start | bytes 589832 | tf_op jit(solution)/shard_map/ppermute | solution.py:26
  95.2 1.4 collective-permute-start.14
  96.6 1.4 collective-permute-done.11.refs_1_
  98.0 4.2 %collective-permute-done.12.refs_2_ = bf16[384,256]{1,0:T(8,128)(2,1)S(1)} collective-permute-done((bf16[384,256]{1,0:T(8,128)(2,1)S(1)}, bf16[384,256]{1,0:T(8,128)(2,1)S(1)}, u32[]{:S(2)}, u32[]{:S(2)}) %collective-permute-start.12) | collective-permute-done | bytes 196640 | tf_op jit(solution)/shard_map/ppermute | solution.py:26
  102.9 1.4 collective-permute-start.15
  105.2 3.4 %copy-done = bf16[1024,4096]{1,0:T(8,128)(2,1)S(1)} copy-done((bf16[1024,4096]{1,0:T(8,128)(2,1)S(1)}, bf16[1024,4096]{1,0:T(8,128)(2,1)}, u32[]{:S(2)}) %copy-start) | copy-done | bytes 8388632
  108.6 1.6 shard_map.101
  111.5 2.4 %collective-permute-start.20 = (bf16[192,512]{1,0:T(8,128)(2,1)S(1)}, bf16[192,512]{1,0:T(8,128)(2,1)S(1)}, u32[]{:S(2)}, u32[]{:S(2)}) collective-permute-start(bf16[192,512]{1,0:T(8,128)(2,1)S(1)} %get-tuple-element.68), channel_id=1, source_target_pairs={{0,64},{32,96},{64,0},{96,32},{1,65},{33,97},{65,1},{97,33},{2,66}... | collective-permute-start | bytes 589832 | tf_op jit(solution)/shard_map/ppermute | solution.py:26
  115.1 1.6 shard_map.102
  117.9 1.6 collective-permute-start.18
  119.5 3.3 %collective-permute-done.20.refs_2_ = bf16[192,512]{1,0:T(8,128)(2,1)S(1)} collective-permute-done((bf16[192,512]{1,0:T(8,128)(2,1)S(1)}, bf16[192,512]{1,0:T(8,128)(2,1)S(1)}, u32[]{:S(2)}, u32[]{:S(2)}) %collective-permute-start.20) | collective-permute-done | bytes 196640 | tf_op jit(solution)/shard_map/ppermute | solution.py:26
  122.8 1.9 shard_map.103
  124.7 2.0 collective-permute-start.33
  128.2 1.9 collective-permute-start.36
  131.4 1.9 shard_map.104
  136.1 2.3 %collective-permute-start.25 = (bf16[384,256]{1,0:T(8,128)(2,1)S(1)}, bf16[384,256]{1,0:T(8,128)(2,1)S(1)}, u32[]{:S(2)}, u32[]{:S(2)}) collective-permute-start(bf16[384,256]{1,0:T(8,128)(2,1)S(1)} %shard_map.105.refs_0_), channel_id=1, source_target_pairs={{0,24},{8,0},{16,8},{24,16},{1,25},{9,1},{17,9},{25,17},{2,26},{10... | collective-permute-start | bytes 589832 | tf_op jit(solution)/shard_map/ppermute | solution.py:26
  139.3 3.4 %collective-permute-done.34.refs_1_ = bf16[384,256]{1,0:T(8,128)(2,1)S(1)} collective-permute-done((bf16[384,256]{1,0:T(8,128)(2,1)S(1)}, bf16[384,256]{1,0:T(8,128)(2,1)S(1)}, u32[]{:S(2)}, u32[]{:S(2)}) %collective-permute-start.34) | collective-permute-done | bytes 196640 | tf_op jit(solution)/shard_map/ppermute | solution.py:26
  142.7 2.0 shard_map.110
  144.7 2.1 %collective-permute-start.37 = (bf16[384,256]{1,0:T(8,128)(2,1)S(1)}, bf16[384,256]{1,0:T(8,128)(2,1)S(1)}, u32[]{:S(2)}, u32[]{:S(2)}) collective-permute-start(bf16[384,256]{1,0:T(8,128)(2,1)S(1)} %get-tuple-element.83), channel_id=1, source_target_pairs={{0,6},{2,0},{4,2},{6,4},{1,7},{3,1},{5,3},{7,5},{8,14},{10,8},{12,... | collective-permute-start | bytes 589832 | tf_op jit(solution)/shard_map/ppermute | solution.py:26
  146.8 1.3 collective-permute-start.38
  148.9 2.3 %collective-permute-done.23.refs_1_ = bf16[384,256]{1,0:T(8,128)(2,1)S(1)} collective-permute-done((bf16[384,256]{1,0:T(8,128)(2,1)S(1)}, bf16[384,256]{1,0:T(8,128)(2,1)S(1)}, u32[]{:S(2)}, u32[]{:S(2)}) %collective-permute-start.23) | collective-permute-done | bytes 196640 | tf_op jit(solution)/shard_map/ppermute | solution.py:26
  151.2 2.0 shard_map.106
  153.2 2.1 %collective-permute-start.26 = (bf16[384,256]{1,0:T(8,128)(2,1)S(1)}, bf16[384,256]{1,0:T(8,128)(2,1)S(1)}, u32[]{:S(2)}, u32[]{:S(2)}) collective-permute-start(bf16[384,256]{1,0:T(8,128)(2,1)S(1)} %get-tuple-element.75), channel_id=1, source_target_pairs={{0,6},{2,0},{4,2},{6,4},{1,7},{3,1},{5,3},{7,5},{8,14},{10,8},{12,... | collective-permute-start | bytes 589832 | tf_op jit(solution)/shard_map/ppermute | solution.py:26
  155.3 1.3 collective-permute-start.27
  157.3 2.0 %collective-permute-done.39.refs_3_ = bf16[384,256]{1,0:T(8,128)(2,1)S(1)} collective-permute-done((bf16[384,256]{1,0:T(8,128)(2,1)S(1)}, bf16[384,256]{1,0:T(8,128)(2,1)S(1)}, u32[]{:S(2)}, u32[]{:S(2)}) %collective-permute-start.39) | collective-permute-done | bytes 196640 | tf_op jit(solution)/shard_map/ppermute | solution.py:26
  162.1 2.4 %collective-permute-start.43 = (bf16[192,512]{1,0:T(8,128)(2,1)S(1)}, bf16[192,512]{1,0:T(8,128)(2,1)S(1)}, u32[]{:S(2)}, u32[]{:S(2)}) collective-permute-start(bf16[192,512]{1,0:T(8,128)(2,1)S(1)} %shard_map.112.refs_0_), channel_id=1, source_target_pairs={{0,96},{32,0},{64,32},{96,64},{1,97},{33,1},{65,33},{97,65},{2,98}... | collective-permute-start | bytes 589832 | tf_op jit(solution)/shard_map/ppermute | solution.py:26
  164.5 3.3 %collective-permute-done.28.refs_3_ = bf16[384,256]{1,0:T(8,128)(2,1)S(1)} collective-permute-done((bf16[384,256]{1,0:T(8,128)(2,1)S(1)}, bf16[384,256]{1,0:T(8,128)(2,1)S(1)}, u32[]{:S(2)}, u32[]{:S(2)}) %collective-permute-start.28) | collective-permute-done | bytes 196640 | tf_op jit(solution)/shard_map/ppermute | solution.py:26
  169.0 2.6 %collective-permute-start.42 = (bf16[192,512]{1,0:T(8,128)(2,1)S(1)}, bf16[192,512]{1,0:T(8,128)(2,1)S(1)}, u32[]{:S(2)}, u32[]{:S(2)}) collective-permute-start(bf16[192,512]{1,0:T(8,128)(2,1)S(1)} %shard_map.112.refs_0_), channel_id=1, source_target_pairs={{0,64},{32,96},{64,0},{96,32},{1,65},{33,97},{65,1},{97,33},{2,66}... | collective-permute-start | bytes 589832 | tf_op jit(solution)/shard_map/ppermute | solution.py:26
  172.6 2.4 %collective-permute-start.32 = (bf16[192,512]{1,0:T(8,128)(2,1)S(1)}, bf16[192,512]{1,0:T(8,128)(2,1)S(1)}, u32[]{:S(2)}, u32[]{:S(2)}) collective-permute-start(bf16[192,512]{1,0:T(8,128)(2,1)S(1)} %shard_map.108.refs_0_), channel_id=1, source_target_pairs={{0,96},{32,0},{64,32},{96,64},{1,97},{33,1},{65,33},{97,65},{2,98}... | collective-permute-start | bytes 589832 | tf_op jit(solution)/shard_map/ppermute | solution.py:26
  177.0 5.0 %collective-permute-done.41.refs_1_ = bf16[192,512]{1,0:T(8,128)(2,1)S(1)} collective-permute-done((bf16[192,512]{1,0:T(8,128)(2,1)S(1)}, bf16[192,512]{1,0:T(8,128)(2,1)S(1)}, u32[]{:S(2)}, u32[]{:S(2)}) %collective-permute-start.41) | collective-permute-done | bytes 196640 | tf_op jit(solution)/shard_map/ppermute | solution.py:26
  182.0 2.1 %shard_map.113.refs_5_ = f32[192,1024]{1,0:T(8,128)S(1)} custom-call(s32[4]{0:T(128)S(1)} %pad_add_fusion.place, bf16[192,512]{1,0:T(8,128)(2,1)S(1)} %shard_map.112.refs_0_, bf16[192,512]{1,0:T(8,128)(2,1)S(1)} %collective-permute-done.41.refs_1_, bf16[192,512]{1,0:T(8,128)(2,1)S(1)} %collective-permute-done.42.refs_2_, ...), custom_call_target="tpu_custom_call" | custom-call | flops 805306368 | bytes 9961472 | tf_op jit(solution)/shard_map/pallas_call | solution.py:51
  184.1 1.4 collective-permute-done.31.refs_2_
  185.5 4.6 %collective-permute-done.30.refs_1_ = bf16[192,512]{1,0:T(8,128)(2,1)S(1)} collective-permute-done((bf16[192,512]{1,0:T(8,128)(2,1)S(1)}, bf16[192,512]{1,0:T(8,128)(2,1)S(1)}, u32[]{:S(2)}, u32[]{:S(2)}) %collective-permute-start.30) | collective-permute-done | bytes 196640 | tf_op jit(solution)/shard_map/ppermute | solution.py:26
  190.0 3.3 %shard_map.114 = (f32[192,1024]{1,0:T(8,128)}, f32[192,1024]{1,0:T(8,128)}) custom-call(s32[4]{0:T(128)S(1)} %pad_add_fusion.place, bf16[192,512]{1,0:T(8,128)(2,1)S(1)} %shard_map.108.refs_0_, bf16[192,512]{1,0:T(8,128)(2,1)S(1)} %collective-permute-done.30.refs_1_, bf16[192,512]{1,0:T(8,128)(2,1)S(1)} %collective-permute-done.31.refs_2_, ...), custom_call_target="tpu_custom_call" | custom-call | flops 805306368 | bytes 12320768 | tf_op jit(solution)/shard_map/pallas_call | solution.py:51
  (97 shorter events, 33.0 us)
Async XLA Ops:
  8.0 41.1 %reduce-scatter.2.cloned.1.call-start = ((), (), s32[]{:S(2)}) async-start(), calls=%async_computation.2 | async-start | bytes 1966080 | tf_op jit(solution)/shard_map/reduce_scatter | solution.py:247
  8.7 96.5 %all-gather.2.cloned.1.call-start = ((), (), s32[]{:S(2)}) async-start(), calls=%async_computation.3 | async-start | bytes 8650752 | tf_op jit(solution)/shard_map/all_gather | solution.py:252
  50.9 3.0 %collective-permute-start = (bf16[192,512]{1,0:T(8,128)(2,1)S(1)}, bf16[192,512]{1,0:T(8,128)(2,1)S(1)}, u32[]{:S(2)}, u32[]{:S(2)}) collective-permute-start(bf16[192,512]{1,0:T(8,128)(2,1)S(1)} %shard_map.94), channel_id=1, source_target_pairs={{0,1},{1,0},{2,3},{3,2},{4,5},{5,4},{6,7},{7,6},{8,9},{9,8},{10,11... | collective-permute-start | bytes 589832 | tf_op jit(solution)/shard_map/ppermute | solution.py:30
  55.2 20.5 %collective-permute-start.4 = (bf16[768,1536]{1,0:T(8,128)(2,1)}, bf16[768,1536]{1,0:T(8,128)(2,1)S(1)}, u32[]{:S(2)}, u32[]{:S(2)}) collective-permute-start(bf16[768,1536]{1,0:T(8,128)(2,1)} %shard_map.96.refs_4_), channel_id=1, source_target_pairs={{0,1},{1,0},{2,3},{3,2},{4,5},{5,4},{6,7},{7,6},{8,9},{9,8},{10,11... | collective-permute-start | bytes 7077896 | tf_op jit(solution)/shard_map/ppermute | solution.py:30
  56.1 10.5 %collective-permute-start.3 = (bf16[384,256]{1,0:T(8,128)(2,1)S(1)}, bf16[384,256]{1,0:T(8,128)(2,1)S(1)}, u32[]{:S(2)}, u32[]{:S(2)}) collective-permute-start(bf16[384,256]{1,0:T(8,128)(2,1)S(1)} %copy-done.9), channel_id=1, source_target_pairs={{0,6},{2,0},{4,2},{6,4},{1,7},{3,1},{5,3},{7,5},{8,14},{10,8},{12,... | collective-permute-start | bytes 589832 | tf_op jit(solution)/shard_map/ppermute | solution.py:26
  57.0 12.1 %collective-permute-start.2 = (bf16[384,256]{1,0:T(8,128)(2,1)S(1)}, bf16[384,256]{1,0:T(8,128)(2,1)S(1)}, u32[]{:S(2)}, u32[]{:S(2)}) collective-permute-start(bf16[384,256]{1,0:T(8,128)(2,1)S(1)} %copy-done.9), channel_id=1, source_target_pairs={{0,4},{2,6},{4,0},{6,2},{1,5},{3,7},{5,1},{7,3},{8,12},{10,14},{12... | collective-permute-start | bytes 589832 | tf_op jit(solution)/shard_map/ppermute | solution.py:26
  58.3 17.5 %collective-permute-start.1 = (bf16[384,256]{1,0:T(8,128)(2,1)S(1)}, bf16[384,256]{1,0:T(8,128)(2,1)S(1)}, u32[]{:S(2)}, u32[]{:S(2)}) collective-permute-start(bf16[384,256]{1,0:T(8,128)(2,1)S(1)} %copy-done.9), channel_id=1, source_target_pairs={{0,2},{2,4},{4,6},{6,0},{1,3},{3,5},{5,7},{7,1},{8,10},{10,12},{12... | collective-permute-start | bytes 589832 | tf_op jit(solution)/shard_map/ppermute | solution.py:26
  58.3 26.5 %collective-permute-start.10 = (bf16[384,256]{1,0:T(8,128)(2,1)S(1)}, bf16[384,256]{1,0:T(8,128)(2,1)S(1)}, u32[]{:S(2)}, u32[]{:S(2)}) collective-permute-start(bf16[384,256]{1,0:T(8,128)(2,1)S(1)} %get-tuple-element.54.refs_0_), channel_id=1, source_target_pairs={{0,6},{2,0},{4,2},{6,4},{1,7},{3,1},{5,3},{7,5},{8,14},{10,8},{12,... | collective-permute-start | bytes 589832 | tf_op jit(solution)/shard_map/ppermute | solution.py:26
  66.7 18.8 %collective-permute-start.9 = (bf16[384,256]{1,0:T(8,128)(2,1)S(1)}, bf16[384,256]{1,0:T(8,128)(2,1)S(1)}, u32[]{:S(2)}, u32[]{:S(2)}) collective-permute-start(bf16[384,256]{1,0:T(8,128)(2,1)S(1)} %get-tuple-element.54.refs_0_), channel_id=1, source_target_pairs={{0,4},{2,6},{4,0},{6,2},{1,5},{3,7},{5,1},{7,3},{8,12},{10,14},{12... | collective-permute-start | bytes 589832 | tf_op jit(solution)/shard_map/ppermute | solution.py:26
  69.1 17.7 %collective-permute-start.8 = (bf16[384,256]{1,0:T(8,128)(2,1)S(1)}, bf16[384,256]{1,0:T(8,128)(2,1)S(1)}, u32[]{:S(2)}, u32[]{:S(2)}) collective-permute-start(bf16[384,256]{1,0:T(8,128)(2,1)S(1)} %get-tuple-element.54.refs_0_), channel_id=1, source_target_pairs={{0,2},{2,4},{4,6},{6,0},{1,3},{3,5},{5,7},{7,1},{8,10},{10,12},{12... | collective-permute-start | bytes 589832 | tf_op jit(solution)/shard_map/ppermute | solution.py:26
  79.9 13.6 %collective-permute-start.5 = (bf16[384,256]{1,0:T(8,128)(2,1)S(1)}, bf16[384,256]{1,0:T(8,128)(2,1)S(1)}, u32[]{:S(2)}, u32[]{:S(2)}) collective-permute-start(bf16[384,256]{1,0:T(8,128)(2,1)S(1)} %get-tuple-element.50), channel_id=1, source_target_pairs={{0,8},{8,16},{16,24},{24,0},{1,9},{9,17},{17,25},{25,1},{2,10},{10... | collective-permute-start | bytes 589832 | tf_op jit(solution)/shard_map/ppermute | solution.py:26
  81.5 13.1 %collective-permute-start.6 = (bf16[384,256]{1,0:T(8,128)(2,1)S(1)}, bf16[384,256]{1,0:T(8,128)(2,1)S(1)}, u32[]{:S(2)}, u32[]{:S(2)}) collective-permute-start(bf16[384,256]{1,0:T(8,128)(2,1)S(1)} %get-tuple-element.51), channel_id=1, source_target_pairs={{0,16},{8,24},{16,0},{24,8},{1,17},{9,25},{17,1},{25,9},{2,18},{10... | collective-permute-start | bytes 589832 | tf_op jit(solution)/shard_map/ppermute | solution.py:26
  84.8 9.8 %collective-permute-start.7 = (bf16[384,256]{1,0:T(8,128)(2,1)S(1)}, bf16[384,256]{1,0:T(8,128)(2,1)S(1)}, u32[]{:S(2)}, u32[]{:S(2)}) collective-permute-start(bf16[384,256]{1,0:T(8,128)(2,1)S(1)} %get-tuple-element.52), channel_id=1, source_target_pairs={{0,24},{8,0},{16,8},{24,16},{1,25},{9,1},{17,9},{25,17},{2,26},{10... | collective-permute-start | bytes 589832 | tf_op jit(solution)/shard_map/ppermute | solution.py:26
  89.4 8.7 %collective-permute-start.11 = (bf16[384,256]{1,0:T(8,128)(2,1)S(1)}, bf16[384,256]{1,0:T(8,128)(2,1)S(1)}, u32[]{:S(2)}, u32[]{:S(2)}) collective-permute-start(bf16[384,256]{1,0:T(8,128)(2,1)S(1)} %get-tuple-element.56), channel_id=1, source_target_pairs={{0,8},{8,16},{16,24},{24,0},{1,9},{9,17},{17,25},{25,1},{2,10},{10... | collective-permute-start | bytes 589832 | tf_op jit(solution)/shard_map/ppermute | solution.py:26
  90.9 11.3 %collective-permute-start.12 = (bf16[384,256]{1,0:T(8,128)(2,1)S(1)}, bf16[384,256]{1,0:T(8,128)(2,1)S(1)}, u32[]{:S(2)}, u32[]{:S(2)}) collective-permute-start(bf16[384,256]{1,0:T(8,128)(2,1)S(1)} %get-tuple-element.57), channel_id=1, source_target_pairs={{0,16},{8,24},{16,0},{24,8},{1,17},{9,25},{17,1},{25,9},{2,18},{10... | collective-permute-start | bytes 589832 | tf_op jit(solution)/shard_map/ppermute | solution.py:26
  93.5 8.7 %collective-permute-start.13 = (bf16[384,256]{1,0:T(8,128)(2,1)S(1)}, bf16[384,256]{1,0:T(8,128)(2,1)S(1)}, u32[]{:S(2)}, u32[]{:S(2)}) collective-permute-start(bf16[384,256]{1,0:T(8,128)(2,1)S(1)} %get-tuple-element.58), channel_id=1, source_target_pairs={{0,24},{8,0},{16,8},{24,16},{1,25},{9,1},{17,9},{25,17},{2,26},{10... | collective-permute-start | bytes 589832 | tf_op jit(solution)/shard_map/ppermute | solution.py:26
  95.2 9.1 %collective-permute-start.14 = (bf16[192,256]{1,0:T(8,128)(2,1)S(1)}, bf16[192,256]{1,0:T(8,128)(2,1)S(1)}, u32[]{:S(2)}, u32[]{:S(2)}) collective-permute-start(bf16[192,256]{1,0:T(8,128)(2,1)S(1)} %get-tuple-element.60), channel_id=1, source_target_pairs={{0,1},{1,0},{2,3},{3,2},{4,5},{5,4},{6,7},{7,6},{8,9},{9,8},{10,11... | collective-permute-start | bytes 294920 | tf_op jit(solution)/shard_map/ppermute | solution.py:30
  102.9 2.4 %collective-permute-start.15 = (bf16[192,256]{1,0:T(8,128)(2,1)S(1)}, bf16[192,256]{1,0:T(8,128)(2,1)S(1)}, u32[]{:S(2)}, u32[]{:S(2)}) collective-permute-start(bf16[192,256]{1,0:T(8,128)(2,1)S(1)} %get-tuple-element.61), channel_id=1, source_target_pairs={{0,1},{1,0},{2,3},{3,2},{4,5},{5,4},{6,7},{7,6},{8,9},{9,8},{10,11... | collective-permute-start | bytes 294920 | tf_op jit(solution)/shard_map/ppermute | solution.py:30
  110.2 7.7 %collective-permute-start.19 = (bf16[192,512]{1,0:T(8,128)(2,1)S(1)}, bf16[192,512]{1,0:T(8,128)(2,1)S(1)}, u32[]{:S(2)}, u32[]{:S(2)}) collective-permute-start(bf16[192,512]{1,0:T(8,128)(2,1)S(1)} %get-tuple-element.67), channel_id=1, source_target_pairs={{0,32},{32,64},{64,96},{96,0},{1,33},{33,65},{65,97},{97,1},{2,34}... | collective-permute-start | bytes 589832 | tf_op jit(solution)/shard_map/ppermute | solution.py:26
  111.5 11.3 %collective-permute-start.20 = (bf16[192,512]{1,0:T(8,128)(2,1)S(1)}, bf16[192,512]{1,0:T(8,128)(2,1)S(1)}, u32[]{:S(2)}, u32[]{:S(2)}) collective-permute-start(bf16[192,512]{1,0:T(8,128)(2,1)S(1)} %get-tuple-element.68), channel_id=1, source_target_pairs={{0,64},{32,96},{64,0},{96,32},{1,65},{33,97},{65,1},{97,33},{2,66}... | collective-permute-start | bytes 589832 | tf_op jit(solution)/shard_map/ppermute | solution.py:26
  113.9 8.9 %collective-permute-start.21 = (bf16[192,512]{1,0:T(8,128)(2,1)S(1)}, bf16[192,512]{1,0:T(8,128)(2,1)S(1)}, u32[]{:S(2)}, u32[]{:S(2)}) collective-permute-start(bf16[192,512]{1,0:T(8,128)(2,1)S(1)} %get-tuple-element.69), channel_id=1, source_target_pairs={{0,96},{32,0},{64,32},{96,64},{1,97},{33,1},{65,33},{97,65},{2,98}... | collective-permute-start | bytes 589832 | tf_op jit(solution)/shard_map/ppermute | solution.py:26
  116.7 14.4 %collective-permute-start.16 = (bf16[192,512]{1,0:T(8,128)(2,1)S(1)}, bf16[192,512]{1,0:T(8,128)(2,1)S(1)}, u32[]{:S(2)}, u32[]{:S(2)}) collective-permute-start(bf16[192,512]{1,0:T(8,128)(2,1)S(1)} %get-tuple-element.64), channel_id=1, source_target_pairs={{0,32},{32,64},{64,96},{96,0},{1,33},{33,65},{65,97},{97,1},{2,34}... | collective-permute-start | bytes 589832 | tf_op jit(solution)/shard_map/ppermute | solution.py:26
  117.0 14.4 %collective-permute-start.17 = (bf16[192,512]{1,0:T(8,128)(2,1)S(1)}, bf16[192,512]{1,0:T(8,128)(2,1)S(1)}, u32[]{:S(2)}, u32[]{:S(2)}) collective-permute-start(bf16[192,512]{1,0:T(8,128)(2,1)S(1)} %get-tuple-element.65), channel_id=1, source_target_pairs={{0,64},{32,96},{64,0},{96,32},{1,65},{33,97},{65,1},{97,33},{2,66}... | collective-permute-start | bytes 589832 | tf_op jit(solution)/shard_map/ppermute | solution.py:26
  117.9 13.5 %collective-permute-start.18 = (bf16[192,512]{1,0:T(8,128)(2,1)S(1)}, bf16[192,512]{1,0:T(8,128)(2,1)S(1)}, u32[]{:S(2)}, u32[]{:S(2)}) collective-permute-start(bf16[192,512]{1,0:T(8,128)(2,1)S(1)} %get-tuple-element.66), channel_id=1, source_target_pairs={{0,96},{32,0},{64,32},{96,64},{1,97},{33,1},{65,33},{97,65},{2,98}... | collective-permute-start | bytes 589832 | tf_op jit(solution)/shard_map/ppermute | solution.py:26
  124.7 2.9 %collective-permute-start.33 = (bf16[192,256]{1,0:T(8,128)(2,1)S(1)}, bf16[192,256]{1,0:T(8,128)(2,1)S(1)}, u32[]{:S(2)}, u32[]{:S(2)}) collective-permute-start(bf16[192,256]{1,0:T(8,128)(2,1)S(1)} %get-tuple-element.81), channel_id=1, source_target_pairs={{0,1},{1,0},{2,3},{3,2},{4,5},{5,4},{6,7},{7,6},{8,9},{9,8},{10,11... | collective-permute-start | bytes 294920 | tf_op jit(solution)/shard_map/ppermute | solution.py:30
  128.2 11.1 %collective-permute-start.36 = (bf16[384,256]{1,0:T(8,128)(2,1)S(1)}, bf16[384,256]{1,0:T(8,128)(2,1)S(1)}, u32[]{:S(2)}, u32[]{:S(2)}) collective-permute-start(bf16[384,256]{1,0:T(8,128)(2,1)S(1)} %shard_map.109.refs_0_), channel_id=1, source_target_pairs={{0,24},{8,0},{16,8},{24,16},{1,25},{9,1},{17,9},{25,17},{2,26},{10... | collective-permute-start | bytes 589832 | tf_op jit(solution)/shard_map/ppermute | solution.py:26
  130.2 9.2 %collective-permute-start.35 = (bf16[384,256]{1,0:T(8,128)(2,1)S(1)}, bf16[384,256]{1,0:T(8,128)(2,1)S(1)}, u32[]{:S(2)}, u32[]{:S(2)}) collective-permute-start(bf16[384,256]{1,0:T(8,128)(2,1)S(1)} %shard_map.109.refs_0_), channel_id=1, source_target_pairs={{0,16},{8,24},{16,0},{24,8},{1,17},{9,25},{17,1},{25,9},{2,18},{10... | collective-permute-start | bytes 589832 | tf_op jit(solution)/shard_map/ppermute | solution.py:26
  131.0 11.7 %collective-permute-start.34 = (bf16[384,256]{1,0:T(8,128)(2,1)S(1)}, bf16[384,256]{1,0:T(8,128)(2,1)S(1)}, u32[]{:S(2)}, u32[]{:S(2)}) collective-permute-start(bf16[384,256]{1,0:T(8,128)(2,1)S(1)} %shard_map.109.refs_0_), channel_id=1, source_target_pairs={{0,8},{8,16},{16,24},{24,0},{1,9},{9,17},{17,25},{25,1},{2,10},{10... | collective-permute-start | bytes 589832 | tf_op jit(solution)/shard_map/ppermute | solution.py:26
  131.4 50.6 %slice-start = ((s8[8388608]{0:T(1024)(128)(4,1)}), s8[4194304]{0:T(1024)(128)(4,1)S(1)}, s32[]{:S(2)}) async-start(s8[8388608]{0:T(1024)(128)(4,1)} %bitcast.6), calls=%async_computation.4 | async-start | bytes 8388608
  133.4 2.1 %collective-permute-start.22 = (bf16[192,256]{1,0:T(8,128)(2,1)S(1)}, bf16[192,256]{1,0:T(8,128)(2,1)S(1)}, u32[]{:S(2)}, u32[]{:S(2)}) collective-permute-start(bf16[192,256]{1,0:T(8,128)(2,1)S(1)} %get-tuple-element.73), channel_id=1, source_target_pairs={{0,1},{1,0},{2,3},{3,2},{4,5},{5,4},{6,7},{7,6},{8,9},{9,8},{10,11... | collective-permute-start | bytes 294920 | tf_op jit(solution)/shard_map/ppermute | solution.py:30
  136.1 45.9 %slice-start.1 = ((s8[8388608]{0:T(1024)(128)(4,1)}), s8[4194304]{0:T(1024)(128)(4,1)S(1)}, s32[]{:S(2)}) async-start(s8[8388608]{0:T(1024)(128)(4,1)} %bitcast.6), calls=%async_computation.5 | async-start | bytes 8388608
  136.1 12.0 %collective-permute-start.25 = (bf16[384,256]{1,0:T(8,128)(2,1)S(1)}, bf16[384,256]{1,0:T(8,128)(2,1)S(1)}, u32[]{:S(2)}, u32[]{:S(2)}) collective-permute-start(bf16[384,256]{1,0:T(8,128)(2,1)S(1)} %shard_map.105.refs_0_), channel_id=1, source_target_pairs={{0,24},{8,0},{16,8},{24,16},{1,25},{9,1},{17,9},{25,17},{2,26},{10... | collective-permute-start | bytes 589832 | tf_op jit(solution)/shard_map/ppermute | solution.py:26
  138.4 10.4 %collective-permute-start.24 = (bf16[384,256]{1,0:T(8,128)(2,1)S(1)}, bf16[384,256]{1,0:T(8,128)(2,1)S(1)}, u32[]{:S(2)}, u32[]{:S(2)}) collective-permute-start(bf16[384,256]{1,0:T(8,128)(2,1)S(1)} %shard_map.105.refs_0_), channel_id=1, source_target_pairs={{0,16},{8,24},{16,0},{24,8},{1,17},{9,25},{17,1},{25,9},{2,18},{10... | collective-permute-start | bytes 589832 | tf_op jit(solution)/shard_map/ppermute | solution.py:26
  139.3 11.8 %collective-permute-start.23 = (bf16[384,256]{1,0:T(8,128)(2,1)S(1)}, bf16[384,256]{1,0:T(8,128)(2,1)S(1)}, u32[]{:S(2)}, u32[]{:S(2)}) collective-permute-start(bf16[384,256]{1,0:T(8,128)(2,1)S(1)} %shard_map.105.refs_0_), channel_id=1, source_target_pairs={{0,8},{8,16},{16,24},{24,0},{1,9},{9,17},{17,25},{25,1},{2,10},{10... | collective-permute-start | bytes 589832 | tf_op jit(solution)/shard_map/ppermute | solution.py:26
  144.7 11.8 %collective-permute-start.37 = (bf16[384,256]{1,0:T(8,128)(2,1)S(1)}, bf16[384,256]{1,0:T(8,128)(2,1)S(1)}, u32[]{:S(2)}, u32[]{:S(2)}) collective-permute-start(bf16[384,256]{1,0:T(8,128)(2,1)S(1)} %get-tuple-element.83), channel_id=1, source_target_pairs={{0,6},{2,0},{4,2},{6,4},{1,7},{3,1},{5,3},{7,5},{8,14},{10,8},{12,... | collective-permute-start | bytes 589832 | tf_op jit(solution)/shard_map/ppermute | solution.py:26
  146.8 10.5 %collective-permute-start.38 = (bf16[384,256]{1,0:T(8,128)(2,1)S(1)}, bf16[384,256]{1,0:T(8,128)(2,1)S(1)}, u32[]{:S(2)}, u32[]{:S(2)}) collective-permute-start(bf16[384,256]{1,0:T(8,128)(2,1)S(1)} %get-tuple-element.84), channel_id=1, source_target_pairs={{0,4},{2,6},{4,0},{6,2},{1,5},{3,7},{5,1},{7,3},{8,12},{10,14},{12... | collective-permute-start | bytes 589832 | tf_op jit(solution)/shard_map/ppermute | solution.py:26
  148.1 11.3 %collective-permute-start.39 = (bf16[384,256]{1,0:T(8,128)(2,1)S(1)}, bf16[384,256]{1,0:T(8,128)(2,1)S(1)}, u32[]{:S(2)}, u32[]{:S(2)}) collective-permute-start(bf16[384,256]{1,0:T(8,128)(2,1)S(1)} %get-tuple-element.85), channel_id=1, source_target_pairs={{0,2},{2,4},{4,6},{6,0},{1,3},{3,5},{5,7},{7,1},{8,10},{10,12},{12... | collective-permute-start | bytes 589832 | tf_op jit(solution)/shard_map/ppermute | solution.py:26
  153.2 11.4 %collective-permute-start.26 = (bf16[384,256]{1,0:T(8,128)(2,1)S(1)}, bf16[384,256]{1,0:T(8,128)(2,1)S(1)}, u32[]{:S(2)}, u32[]{:S(2)}) collective-permute-start(bf16[384,256]{1,0:T(8,128)(2,1)S(1)} %get-tuple-element.75), channel_id=1, source_target_pairs={{0,6},{2,0},{4,2},{6,4},{1,7},{3,1},{5,3},{7,5},{8,14},{10,8},{12,... | collective-permute-start | bytes 589832 | tf_op jit(solution)/shard_map/ppermute | solution.py:26
  155.3 9.2 %collective-permute-start.27 = (bf16[384,256]{1,0:T(8,128)(2,1)S(1)}, bf16[384,256]{1,0:T(8,128)(2,1)S(1)}, u32[]{:S(2)}, u32[]{:S(2)}) collective-permute-start(bf16[384,256]{1,0:T(8,128)(2,1)S(1)} %get-tuple-element.76), channel_id=1, source_target_pairs={{0,4},{2,6},{4,0},{6,2},{1,5},{3,7},{5,1},{7,3},{8,12},{10,14},{12... | collective-permute-start | bytes 589832 | tf_op jit(solution)/shard_map/ppermute | solution.py:26
  156.5 11.3 %collective-permute-start.28 = (bf16[384,256]{1,0:T(8,128)(2,1)S(1)}, bf16[384,256]{1,0:T(8,128)(2,1)S(1)}, u32[]{:S(2)}, u32[]{:S(2)}) collective-permute-start(bf16[384,256]{1,0:T(8,128)(2,1)S(1)} %get-tuple-element.77), channel_id=1, source_target_pairs={{0,2},{2,4},{4,6},{6,0},{1,3},{3,5},{5,7},{7,1},{8,10},{10,12},{12... | collective-permute-start | bytes 589832 | tf_op jit(solution)/shard_map/ppermute | solution.py:26
  160.0 1.5 collective-permute-start.40
  162.1 13.4 %collective-permute-start.43 = (bf16[192,512]{1,0:T(8,128)(2,1)S(1)}, bf16[192,512]{1,0:T(8,128)(2,1)S(1)}, u32[]{:S(2)}, u32[]{:S(2)}) collective-permute-start(bf16[192,512]{1,0:T(8,128)(2,1)S(1)} %shard_map.112.refs_0_), channel_id=1, source_target_pairs={{0,96},{32,0},{64,32},{96,64},{1,97},{33,1},{65,33},{97,65},{2,98}... | collective-permute-start | bytes 589832 | tf_op jit(solution)/shard_map/ppermute | solution.py:26
  168.5 3.5 %collective-permute-start.29 = (bf16[192,256]{1,0:T(8,128)(2,1)S(1)}, bf16[192,256]{1,0:T(8,128)(2,1)S(1)}, u32[]{:S(2)}, u32[]{:S(2)}) collective-permute-start(bf16[192,256]{1,0:T(8,128)(2,1)S(1)} %get-tuple-element.79), channel_id=1, source_target_pairs={{0,1},{1,0},{2,3},{3,2},{4,5},{5,4},{6,7},{7,6},{8,9},{9,8},{10,11... | collective-permute-start | bytes 294920 | tf_op jit(solution)/shard_map/ppermute | solution.py:30
  169.0 8.0 %collective-permute-start.42 = (bf16[192,512]{1,0:T(8,128)(2,1)S(1)}, bf16[192,512]{1,0:T(8,128)(2,1)S(1)}, u32[]{:S(2)}, u32[]{:S(2)}) collective-permute-start(bf16[192,512]{1,0:T(8,128)(2,1)S(1)} %shard_map.112.refs_0_), channel_id=1, source_target_pairs={{0,64},{32,96},{64,0},{96,32},{1,65},{33,97},{65,1},{97,33},{2,66}... | collective-permute-start | bytes 589832 | tf_op jit(solution)/shard_map/ppermute | solution.py:26
  171.7 10.4 %collective-permute-start.41 = (bf16[192,512]{1,0:T(8,128)(2,1)S(1)}, bf16[192,512]{1,0:T(8,128)(2,1)S(1)}, u32[]{:S(2)}, u32[]{:S(2)}) collective-permute-start(bf16[192,512]{1,0:T(8,128)(2,1)S(1)} %shard_map.112.refs_0_), channel_id=1, source_target_pairs={{0,32},{32,64},{64,96},{96,0},{1,33},{33,65},{65,97},{97,1},{2,34}... | collective-permute-start | bytes 589832 | tf_op jit(solution)/shard_map/ppermute | solution.py:26
  172.6 11.5 %collective-permute-start.32 = (bf16[192,512]{1,0:T(8,128)(2,1)S(1)}, bf16[192,512]{1,0:T(8,128)(2,1)S(1)}, u32[]{:S(2)}, u32[]{:S(2)}) collective-permute-start(bf16[192,512]{1,0:T(8,128)(2,1)S(1)} %shard_map.108.refs_0_), channel_id=1, source_target_pairs={{0,96},{32,0},{64,32},{96,64},{1,97},{33,1},{65,33},{97,65},{2,98}... | collective-permute-start | bytes 589832 | tf_op jit(solution)/shard_map/ppermute | solution.py:26
  175.0 10.5 %collective-permute-start.31 = (bf16[192,512]{1,0:T(8,128)(2,1)S(1)}, bf16[192,512]{1,0:T(8,128)(2,1)S(1)}, u32[]{:S(2)}, u32[]{:S(2)}) collective-permute-start(bf16[192,512]{1,0:T(8,128)(2,1)S(1)} %shard_map.108.refs_0_), channel_id=1, source_target_pairs={{0,64},{32,96},{64,0},{96,32},{1,65},{33,97},{65,1},{97,33},{2,66}... | collective-permute-start | bytes 589832 | tf_op jit(solution)/shard_map/ppermute | solution.py:26
  175.5 14.6 %collective-permute-start.30 = (bf16[192,512]{1,0:T(8,128)(2,1)S(1)}, bf16[192,512]{1,0:T(8,128)(2,1)S(1)}, u32[]{:S(2)}, u32[]{:S(2)}) collective-permute-start(bf16[192,512]{1,0:T(8,128)(2,1)S(1)} %shard_map.108.refs_0_), channel_id=1, source_target_pairs={{0,32},{32,64},{64,96},{96,0},{1,33},{33,65},{65,97},{97,1},{2,34}... | collective-permute-start | bytes 589832 | tf_op jit(solution)/shard_map/ppermute | solution.py:26
  (11 other events, 63.7 us)
Sparse Core Ops, SparseCore 0:
  11.2 27.8 reduce-scatter.1
Sparse Core Ops, SparseCore 1:
  11.5 73.4 all-gather.1
